TPU v7x, 256 devices: a whole 4x4x8 slice. The times are simulated.
256 devices in a mesh: tm: 32 (over y_hi, z, core), slab: 8 (over x, y_lo).
Axes of the slice: x: 4, y: 4 (y_hi: 2, y_lo: 2; y = y_hi * 2 + y_lo), z: 8, core: 2. Of those that a mesh axis runs over, the one named last changes fastest.
Arguments:
- sources: float32 [4, 256, 128, 512], P(None, 'tm', 'slab'), may hold values from -6 to 6
- phonons: float32 [256, 128, 512], P('tm', 'slab'), may hold values from -3 to 3
- momenta: float32 [256, 128, 512], P('tm', 'slab'), may hold values from -6 to 6
- kernel: float32 [256], replicated, may hold values from -0.375 to 0.375
- bonds: int32 [2, 128, 512], P(None, 'slab'), may hold values 0 or 1
Outputs:
- half_momenta: float32 [256, 128, 512], P('tm', 'slab')
- new_phonons: float32 [256, 128, 512], P('tm', 'slab')
All inputs are finite; a program needn't handle non-finite values. No bound on the sum of `bonds` on one device may be relied on, other than what follows from the above.
Results may differ from a plain program's by a relative error of at most 0.0001.
Values sent between devices are 32-bit elements; how exact they have to be, the bound alone decides.
No kernel may reach another device: no remote copies, remote signals or barrier semaphores. Data moves between devices by JAX's collectives and lax.ppermute only.
A program may use at most 64 MiB of HBM per device.

v0:
```python
import jax
import jax.numpy as jnp
from jax import lax
from jax.sharding import PartitionSpec as P

ITERS = 2


hopping = 0.1
coupling = 0.2
restore = 0.25
spring = 0.25
stepsize = 0.5


def passed_along(block, axis, distance):
    devices = range(lax.axis_size(axis))
    route = [((i - distance) % len(devices), i) for i in devices]
    return lax.ppermute(block, axis, route)


def extended(block, sides, width):
    for axis, dim in sides:
        count = lax.axis_size(axis)
        forward = [(i, i + 1) for i in range(count - 1)]
        forward.append((count - 1, 0))
        backward = [(target, source) for source, target in forward]
        low = lax.ppermute(
            lax.slice_in_dim(block, block.shape[dim] - width, None, axis=dim), axis, forward
        )
        high = lax.ppermute(lax.slice_in_dim(block, 0, width, axis=dim), axis, backward)
        block = jnp.concatenate([low, block, high], axis=dim)
    return block


def inner_local(first, second):
    return jnp.sum(first * second, axis=(1, 2, 3))


def circulant_table(kernel):
    total_time = kernel.shape[0]
    rolled = jnp.roll(kernel, total_time - 1)
    tiled = jnp.tile(rolled, total_time + 1)
    shifted = tiled.reshape(total_time, total_time + 1)[:, :total_time]
    return shifted[:, ::-1]


def body(sources, phonons, momenta, kernel, bonds):
    slices = sources.shape[1]
    rows = sources.shape[2]
    horiz = bonds[0].astype(jnp.float32)
    vert = bonds[1].astype(jnp.float32)
    bond_edge = passed_along(bonds[1][rows - 1 :], "slab", 1).astype(jnp.float32)
    vert_padded = jnp.concatenate([bond_edge, vert], axis=0)
    start_time = lax.axis_index("tm") * slices
    times = start_time + jnp.arange(slices, dtype=jnp.int32)
    sign = jnp.where(times == 0, -1.0, 1.0).astype(jnp.float32)[:, None, None]
    weight = sign * jnp.exp(coupling * phonons)

    def kinetic(field):
        padded = extended(field, (("slab", 2),), 1)
        below = (padded[:, :, : rows + 1] * vert_padded)[:, :, :rows]
        above = vert * padded[:, :, 2:]
        beside = horiz * jnp.roll(field, -1, 3) + jnp.roll(horiz * field, 1, 3) + above + below
        return field + hopping * beside

    def forward_op(field):
        moved = kinetic(field)
        earlier = passed_along(moved[:, slices - 1 :], "tm", 1)
        shifted = jnp.concatenate([earlier, moved[:, : slices - 1]], axis=1)
        return field - weight * shifted

    def expand(values):
        return values[:, None, None, None]

    def squares(field):
        return expand(lax.psum(inner_local(field, field), ("tm", "slab")))

    solution = jnp.zeros_like(sources)
    forward_sum = jnp.zeros_like(sources)
    residual = sources
    direction = sources
    norm_now = squares(residual)
    for step in range(ITERS):
        normal_moved = forward_op(direction)
        scaled = weight * normal_moved
        later = passed_along(scaled[:, :1], "tm", -1)
        adjoint_shifted = jnp.concatenate([scaled[:, 1:], later], axis=1)
        image = normal_moved - kinetic(adjoint_shifted)
        curve = expand(lax.psum(inner_local(direction, image), ("tm", "slab")))
        alpha = norm_now / curve
        solution = solution + alpha * direction
        forward_sum = forward_sum + alpha * normal_moved
        residual = residual - alpha * image
        norm_next = squares(residual)
        direction = residual + norm_next / norm_now * direction
        norm_now = norm_next
    image_y = forward_op(solution)
    fermion_force = 2.0 * coupling * jnp.sum(image_y * (solution - image_y), axis=0)
    phonon_pad = extended(phonons, (("tm", 0),), 1)
    boson_force = restore * phonons + spring * (2.0 * phonons - phonon_pad[2:] - phonon_pad[:-2])
    half_momenta = momenta - 0.5 * stepsize * (boson_force + fermion_force)
    circulant = circulant_table(kernel)
    flat = half_momenta.reshape(slices, -1)
    columns = lax.all_to_all(flat, "tm", split_axis=1, concat_axis=0, tiled=True)
    mixed = jnp.dot(
        circulant, columns, precision=lax.Precision.HIGHEST, preferred_element_type=jnp.float32
    )
    drift = lax.all_to_all(mixed, "tm", split_axis=0, concat_axis=1, tiled=True)
    new_phonons = phonons + stepsize * drift.reshape(phonons.shape)
    return (half_momenta, new_phonons)


def solution(mesh):
    return jax.shard_map(
        body,
        mesh=mesh,
        in_specs=(
            P(None, "tm", "slab", None),
            P("tm", "slab", None),
            P("tm", "slab", None),
            P(),
            P(None, "slab", None),
        ),
        out_specs=(P("tm", "slab", None), P("tm", "slab", None)),
        check_vma=False,
    )
```

profile of v0, /device:TPU:1, one launch (start us, length us, event | category | flops | bytes accessed | tf_op | source)
XLA Modules:
  0.0 347.6 jit_solution(3339508882631839150)
XLA Ops:
  1.4 2.1 collective-permute-start.4
  3.5 2.0 fusion.66
  6.5 2.5 collective-permute-start.2
  9.0 1.4 broadcast_multiply_fusion.2
  11.9 1.6 fusion.34
  13.6 3.1 collective-permute-start.5
  16.9 1.8 collective-permute-done.5
  19.0 6.1 %collective-permute-start.6 = (f32[4,1,16,512]{3,2,1,0:T(8,128)S(1)}, f32[4,1,16,512]{3,2,1,0:T(8,128)S(1)}, u32[]{:S(2)}, u32[]{:S(2)}) collective-permute-start(f32[4,1,16,512]{3,2,1,0:T(8,128)S(1)} %slice.275), channel_id=1, source_target_pairs={{8,0},{16,8},{24,16},{32,24},{40,32},{48,40},{56,48},{64,56},{72,6... | collective-permute-start | bytes 393224 | tf_op jit(solution)/shard_map/ppermute | solution.py:19
  26.2 3.6 %collective-permute-start.7 = (f32[4,8,1,512]{3,2,1,0:T(1,128)S(1)}, f32[4,8,1,512]{3,2,1,0:T(1,128)S(1)}, u32[]{:S(2)}, u32[]{:S(2)}) collective-permute-start(f32[4,8,1,512]{3,2,1,0:T(1,128)S(1)} %get-tuple-element.17), channel_id=1, source_target_pairs={{1,0},{2,1},{3,2},{4,3},{5,4},{6,5},{7,6},{0,7},{9,8},{10,9},{11,1... | collective-permute-start | bytes 196616 | tf_op jit(solution)/shard_map/ppermute | solution.py:31
  32.7 79.3 %all-reduce = (f32[4]{0:T(128)S(1)}, f32[4]{0:T(128)S(1)}) all-reduce(f32[4]{0:T(128)S(1)} %get-tuple-element.3, f32[4]{0:T(128)S(1)} %get-tuple-element.2), channel_id=1, replica_groups=mesh['tm'=32,'slab'=8] {'tm','slab'}, use_global_device_ids=true, to_apply=%region_1.2 | all-reduce | flops 8 | bytes 64 | tf_op jit(solution)/shard_map/psum | solution.py:77
  112.3 72.4 %psum.30 = f32[4]{0:T(128)S(1)} all-reduce(f32[4]{0:T(128)S(1)} %multiply_reduce_fusion), channel_id=1, replica_groups=mesh['tm'=32,'slab'=8] {'tm','slab'}, use_global_device_ids=true, to_apply=%region_5.6 | all-reduce | flops 4 | bytes 32 | tf_op jit(solution)/shard_map/psum | solution.py:77
  185.8 3.3 collective-permute-start.9
  189.6 1.2 collective-permute-done.10
  191.7 3.5 collective-permute-start.11
  195.2 1.9 collective-permute-done.11
  197.4 4.5 %collective-permute-start.12 = (f32[4,1,16,512]{3,2,1,0:T(8,128)S(1)}, f32[4,1,16,512]{3,2,1,0:T(8,128)S(1)}, u32[]{:S(2)}, u32[]{:S(2)}) collective-permute-start(f32[4,1,16,512]{3,2,1,0:T(8,128)S(1)} %slice.297), channel_id=1, source_target_pairs={{8,0},{16,8},{24,16},{32,24},{40,32},{48,40},{56,48},{64,56},{72,6... | collective-permute-start | bytes 393224 | tf_op jit(solution)/shard_map/ppermute | solution.py:19
  203.7 3.3 collective-permute-start.13
  209.8 80.1 %psum.31 = f32[4]{0:T(128)S(1)} all-reduce(f32[4]{0:T(128)S(1)} %fusion.15), channel_id=1, replica_groups=mesh['tm'=32,'slab'=8] {'tm','slab'}, use_global_device_ids=true, to_apply=%region_7.8 | all-reduce | flops 4 | bytes 32 | tf_op jit(solution)/shard_map/psum | solution.py:90
  290.5 3.6 %collective-permute-start.15 = (f32[4,8,1,512]{3,2,1,0:T(1,128)S(1)}, f32[4,8,1,512]{3,2,1,0:T(1,128)S(1)}, u32[]{:S(2)}, u32[]{:S(2)}) collective-permute-start(f32[4,8,1,512]{3,2,1,0:T(1,128)S(1)} %get-tuple-element.11), channel_id=1, source_target_pairs={{1,0},{2,1},{3,2},{4,3},{5,4},{6,5},{7,6},{0,7},{9,8},{10,9},{11,1... | collective-permute-start | bytes 196616 | tf_op jit(solution)/shard_map/ppermute | solution.py:31
  296.6 1.7 collective-permute-start.17
  300.6 1.9 collective-permute-done
  304.2 11.0 %all-to-all-start = ((f32[8,32,256]{2,0,1:T(8,128)}), f32[8,32,256]{2,0,1:T(8,128)S(1)}, u32[]{:S(2)}, u32[]{:S(2)}) async-start(f32[8,32,256]{2,0,1:T(8,128)} %copy.8), calls=%async_computation | async-start | bytes 524288 | tf_op jit(solution)/shard_map/all_to_all | solution.py:105
  317.2 11.4 %all-to-all-done = f32[8,32,256]{2,0,1:T(8,128)S(1)} async-done(((f32[8,32,256]{2,0,1:T(8,128)}), f32[8,32,256]{2,0,1:T(8,128)S(1)}, u32[]{:S(2)}, u32[]{:S(2)}) %all-to-all-start) | async-done | bytes 262176 | tf_op jit(solution)/shard_map/all_to_all | solution.py:105
  329.0 17.7 %all_to_all.29 = f32[32,8,256]{2,1,0:T(8,128)S(1)} all-to-all(f32[32,8,256]{2,1,0:T(8,128)S(1)} %fusion.56), channel_id=1, replica_groups=mesh['tm'=32,'slab'=8] {'tm'}, dimensions={0} | all-to-all | bytes 524288 | tf_op jit(solution)/shard_map/all_to_all | solution.py:109
  (105 shorter events, 25.7 us)
Async XLA Ops:
  1.4 7.7 %copy-start.6 = (s32[2,16,512]{2,1,0:T(8,128)S(1)}, s32[2,16,512]{2,1,0:T(8,128)}, u32[]{:S(2)}) copy-start(s32[2,16,512]{2,1,0:T(8,128)} %param.9) | copy-start | bytes 196612
  1.4 9.7 %collective-permute-start.4 = (s32[1,512]{1,0:T(1,128)S(1)}, s32[1,512]{1,0:T(1,128)S(1)}, u32[]{:S(2)}, u32[]{:S(2)}) collective-permute-start(s32[1,512]{1,0:T(1,128)S(1)} %slice_bitcast_fusion), channel_id=1, source_target_pairs={{7,0},{0,1},{1,2},{2,3},{3,4},{4,5},{5,6},{6,7},{15,8},{8,9},{9,10... | collective-permute-start | bytes 6152 | tf_op jit(solution)/shard_map/ppermute | solution.py:19
  5.4 5.7 %collective-permute-start.3 = (f32[4,8,1,512]{3,2,1,0:T(1,128)}, f32[4,8,1,512]{3,2,1,0:T(1,128)}, u32[]{:S(2)}, u32[]{:S(2)}) collective-permute-start(f32[4,8,1,512]{3,2,1,0:T(1,128)} %get-tuple-element.20), channel_id=1, source_target_pairs={{0,1},{1,2},{2,3},{3,4},{4,5},{5,6},{6,7},{7,0},{8,9},{9,10},{10,1... | collective-permute-start | bytes 196616 | tf_op jit(solution)/shard_map/ppermute | solution.py:28
  6.5 4.6 %collective-permute-start.2 = (f32[4,8,1,512]{3,2,1,0:T(1,128)}, f32[4,8,1,512]{3,2,1,0:T(1,128)}, u32[]{:S(2)}, u32[]{:S(2)}) collective-permute-start(f32[4,8,1,512]{3,2,1,0:T(1,128)} %get-tuple-element.19), channel_id=1, source_target_pairs={{1,0},{2,1},{3,2},{4,3},{5,4},{6,5},{7,6},{0,7},{9,8},{10,9},{11,1... | collective-permute-start | bytes 196616 | tf_op jit(solution)/shard_map/ppermute | solution.py:31
  13.6 3.1 copy-start.2
  13.6 5.1 %collective-permute-start.5 = (f32[4,1,16,512]{3,2,1,0:T(8,128)S(1)}, f32[4,1,16,512]{3,2,1,0:T(8,128)S(1)}, u32[]{:S(2)}, u32[]{:S(2)}) collective-permute-start(f32[4,1,16,512]{3,2,1,0:T(8,128)S(1)} %slice.272), channel_id=1, source_target_pairs={{248,0},{0,8},{8,16},{16,24},{24,32},{32,40},{40,48},{48,56},{56,6... | collective-permute-start | bytes 393224 | tf_op jit(solution)/shard_map/ppermute | solution.py:19
  19.0 7.0 %collective-permute-start.6 = (f32[4,1,16,512]{3,2,1,0:T(8,128)S(1)}, f32[4,1,16,512]{3,2,1,0:T(8,128)S(1)}, u32[]{:S(2)}, u32[]{:S(2)}) collective-permute-start(f32[4,1,16,512]{3,2,1,0:T(8,128)S(1)} %slice.275), channel_id=1, source_target_pairs={{8,0},{16,8},{24,16},{32,24},{40,32},{48,40},{56,48},{64,56},{72,6... | collective-permute-start | bytes 393224 | tf_op jit(solution)/shard_map/ppermute | solution.py:19
  26.1 5.3 %collective-permute-start.8 = (f32[4,8,1,512]{3,2,1,0:T(1,128)S(1)}, f32[4,8,1,512]{3,2,1,0:T(1,128)S(1)}, u32[]{:S(2)}, u32[]{:S(2)}) collective-permute-start(f32[4,8,1,512]{3,2,1,0:T(1,128)S(1)} %get-tuple-element.18), channel_id=1, source_target_pairs={{0,1},{1,2},{2,3},{3,4},{4,5},{5,6},{6,7},{7,0},{8,9},{9,10},{10,1... | collective-permute-start | bytes 196616 | tf_op jit(solution)/shard_map/ppermute | solution.py:28
  26.2 5.2 %collective-permute-start.7 = (f32[4,8,1,512]{3,2,1,0:T(1,128)S(1)}, f32[4,8,1,512]{3,2,1,0:T(1,128)S(1)}, u32[]{:S(2)}, u32[]{:S(2)}) collective-permute-start(f32[4,8,1,512]{3,2,1,0:T(1,128)S(1)} %get-tuple-element.17), channel_id=1, source_target_pairs={{1,0},{2,1},{3,2},{4,3},{5,4},{6,5},{7,6},{0,7},{9,8},{10,9},{11,1... | collective-permute-start | bytes 196616 | tf_op jit(solution)/shard_map/ppermute | solution.py:31
  185.3 5.6 %collective-permute-start.10 = (f32[4,8,1,512]{3,2,1,0:T(1,128)S(1)}, f32[4,8,1,512]{3,2,1,0:T(1,128)S(1)}, u32[]{:S(2)}, u32[]{:S(2)}) collective-permute-start(f32[4,8,1,512]{3,2,1,0:T(1,128)S(1)} %get-tuple-element.16), channel_id=1, source_target_pairs={{0,1},{1,2},{2,3},{3,4},{4,5},{5,6},{6,7},{7,0},{8,9},{9,10},{10,1... | collective-permute-start | bytes 196616 | tf_op jit(solution)/shard_map/ppermute | solution.py:28
  185.8 5.0 %collective-permute-start.9 = (f32[4,8,1,512]{3,2,1,0:T(1,128)S(1)}, f32[4,8,1,512]{3,2,1,0:T(1,128)S(1)}, u32[]{:S(2)}, u32[]{:S(2)}) collective-permute-start(f32[4,8,1,512]{3,2,1,0:T(1,128)S(1)} %get-tuple-element.15), channel_id=1, source_target_pairs={{1,0},{2,1},{3,2},{4,3},{5,4},{6,5},{7,6},{0,7},{9,8},{10,9},{11,1... | collective-permute-start | bytes 196616 | tf_op jit(solution)/shard_map/ppermute | solution.py:31
  191.7 5.4 %collective-permute-start.11 = (f32[4,1,16,512]{3,2,1,0:T(8,128)S(1)}, f32[4,1,16,512]{3,2,1,0:T(8,128)S(1)}, u32[]{:S(2)}, u32[]{:S(2)}) collective-permute-start(f32[4,1,16,512]{3,2,1,0:T(8,128)S(1)} %slice.294), channel_id=1, source_target_pairs={{248,0},{0,8},{8,16},{16,24},{24,32},{32,40},{40,48},{48,56},{56,6... | collective-permute-start | bytes 393224 | tf_op jit(solution)/shard_map/ppermute | solution.py:19
  197.4 5.5 %collective-permute-start.12 = (f32[4,1,16,512]{3,2,1,0:T(8,128)S(1)}, f32[4,1,16,512]{3,2,1,0:T(8,128)S(1)}, u32[]{:S(2)}, u32[]{:S(2)}) collective-permute-start(f32[4,1,16,512]{3,2,1,0:T(8,128)S(1)} %slice.297), channel_id=1, source_target_pairs={{8,0},{16,8},{24,16},{32,24},{40,32},{48,40},{56,48},{64,56},{72,6... | collective-permute-start | bytes 393224 | tf_op jit(solution)/shard_map/ppermute | solution.py:19
  203.0 5.6 %collective-permute-start.14 = (f32[4,8,1,512]{3,2,1,0:T(1,128)S(1)}, f32[4,8,1,512]{3,2,1,0:T(1,128)S(1)}, u32[]{:S(2)}, u32[]{:S(2)}) collective-permute-start(f32[4,8,1,512]{3,2,1,0:T(1,128)S(1)} %get-tuple-element.14), channel_id=1, source_target_pairs={{0,1},{1,2},{2,3},{3,4},{4,5},{5,6},{6,7},{7,0},{8,9},{9,10},{10,1... | collective-permute-start | bytes 196616 | tf_op jit(solution)/shard_map/ppermute | solution.py:28
  203.7 4.9 %collective-permute-start.13 = (f32[4,8,1,512]{3,2,1,0:T(1,128)S(1)}, f32[4,8,1,512]{3,2,1,0:T(1,128)S(1)}, u32[]{:S(2)}, u32[]{:S(2)}) collective-permute-start(f32[4,8,1,512]{3,2,1,0:T(1,128)S(1)} %get-tuple-element.13), channel_id=1, source_target_pairs={{1,0},{2,1},{3,2},{4,3},{5,4},{6,5},{7,6},{0,7},{9,8},{10,9},{11,1... | collective-permute-start | bytes 196616 | tf_op jit(solution)/shard_map/ppermute | solution.py:31
  290.4 5.4 %collective-permute-start.16 = (f32[4,8,1,512]{3,2,1,0:T(1,128)S(1)}, f32[4,8,1,512]{3,2,1,0:T(1,128)S(1)}, u32[]{:S(2)}, u32[]{:S(2)}) collective-permute-start(f32[4,8,1,512]{3,2,1,0:T(1,128)S(1)} %get-tuple-element.12), channel_id=1, source_target_pairs={{0,1},{1,2},{2,3},{3,4},{4,5},{5,6},{6,7},{7,0},{8,9},{9,10},{10,1... | collective-permute-start | bytes 196616 | tf_op jit(solution)/shard_map/ppermute | solution.py:28
  290.5 5.3 %collective-permute-start.15 = (f32[4,8,1,512]{3,2,1,0:T(1,128)S(1)}, f32[4,8,1,512]{3,2,1,0:T(1,128)S(1)}, u32[]{:S(2)}, u32[]{:S(2)}) collective-permute-start(f32[4,8,1,512]{3,2,1,0:T(1,128)S(1)} %get-tuple-element.11), channel_id=1, source_target_pairs={{1,0},{2,1},{3,2},{4,3},{5,4},{6,5},{7,6},{0,7},{9,8},{10,9},{11,1... | collective-permute-start | bytes 196616 | tf_op jit(solution)/shard_map/ppermute | solution.py:31
  296.6 1.8 copy-start.3
  296.6 3.7 %collective-permute-start.17 = (f32[4,1,16,512]{3,2,1,0:T(8,128)S(1)}, f32[4,1,16,512]{3,2,1,0:T(8,128)S(1)}, u32[]{:S(2)}, u32[]{:S(2)}) collective-permute-start(f32[4,1,16,512]{3,2,1,0:T(8,128)S(1)} %slice.316), channel_id=1, source_target_pairs={{248,0},{0,8},{8,16},{16,24},{24,32},{32,40},{40,48},{48,56},{56,6... | collective-permute-start | bytes 393224 | tf_op jit(solution)/shard_map/ppermute | solution.py:19
  298.4 2.3 collective-permute-start.1
  299.2 3.3 collective-permute-start
  299.8 2.8 copy-start.5
  304.2 11.0 %copy-start.7 = (f32[256]{0:T(256)S(1)}, f32[256]{0:T(256)}, u32[]{:S(2)}) copy-start(f32[256]{0:T(256)} %param.8) | copy-start | bytes 3076
  304.2 24.4 %all-to-all-start = ((f32[8,32,256]{2,0,1:T(8,128)}), f32[8,32,256]{2,0,1:T(8,128)S(1)}, u32[]{:S(2)}, u32[]{:S(2)}) async-start(f32[8,32,256]{2,0,1:T(8,128)} %copy.8), calls=%async_computation | async-start | bytes 524288 | tf_op jit(solution)/shard_map/all_to_all | solution.py:105
  (4 other events, 4.5 us)
where the time goes:
time: 349 us; the launch traced here: 348 us
  blocking collectives  249 us (71%)
  starting transfers between devices  52 us (15%)
  waiting for transfers between devices  23.7 us (7%)
  other arithmetic  11.9 us (3%)
  local copies, waits for them, and re-layouts  9.07 us (3%)
    psum x2, blocking collectives, squares(): return expand(lax.psum(inner_local(field, field), ('tm', 'slab')))  152 us
    psum x1, blocking collectives, body(): curve = expand(lax.psum(inner_local(direction, image), ('tm', 'slab')))  80.1 us
    ppermute x6, starting transfers between devices, passed_along(): return lax.ppermute(block, axis, route)  20.9 us
    all_to_all x1, blocking collectives, body(): drift = lax.all_to_all(mixed, 'tm', split_axis=0, concat_axis=1, tiled=True)  17.7 us
    ppermute x6, starting transfers between devices, extended(): lax.ppermute(lax.slice_in_dim(block, 0, width, axis=dim), axis, backward)  16.7 us
    all_to_all x1, waiting for transfers between devices, body(): lax.all_to_all(flat, 'tm', split_axis=1, concat_axis=0, tiled=True)  11.4 us
    all_to_all x1, starting transfers between devices, body(): lax.all_to_all(flat, 'tm', split_axis=1, concat_axis=0, tiled=True)  11 us
  transfers between devices with their start and end apart: 19, of which 11 were waited for; matrix products, arithmetic and copies ran while one was open for 3% of the time, Pallas kernels for 0%

commit v1 on v0

--- a/solution.py
+++ b/solution.py
@@ -2,9 +2,6 @@
 import jax.numpy as jnp
 from jax import lax
 from jax.sharding import PartitionSpec as P
-
-ITERS = 2
-
 
 hopping = 0.1
 coupling = 0.2
@@ -35,6 +32,21 @@
 
 def inner_local(first, second):
     return jnp.sum(first * second, axis=(1, 2, 3))
+
+
+def from_all(row):
+    axes = ("tm", "slab")
+    everyone = lax.axis_size("tm") * lax.axis_size("slab")
+    copies = jnp.broadcast_to(row[None], (everyone,) + row.shape)
+    return lax.all_to_all(copies, axes, split_axis=0, concat_axis=0, tiled=True)
+
+
+def krylov_coefficients(moments):
+    alpha = moments[0] / moments[1]
+    square = moments[2] / moments[1]
+    cube = moments[3] / moments[1]
+    spread = cube - square * square
+    return (alpha * cube - square) / spread, (1.0 - alpha * square) / spread
 
 
 def circulant_table(kernel):
@@ -70,32 +82,27 @@
         shifted = jnp.concatenate([earlier, moved[:, : slices - 1]], axis=1)
         return field - weight * shifted
 
-    def expand(values):
-        return values[:, None, None, None]
+    def transposed_op(field):
+        scaled = weight * field
+        later = passed_along(scaled[:, :1], "tm", -1)
+        return field - kinetic(jnp.concatenate([scaled[:, 1:], later], axis=1))
 
-    def squares(field):
-        return expand(lax.psum(inner_local(field, field), ("tm", "slab")))
-
-    solution = jnp.zeros_like(sources)
-    forward_sum = jnp.zeros_like(sources)
-    residual = sources
-    direction = sources
-    norm_now = squares(residual)
-    for step in range(ITERS):
-        normal_moved = forward_op(direction)
-        scaled = weight * normal_moved
-        later = passed_along(scaled[:, :1], "tm", -1)
-        adjoint_shifted = jnp.concatenate([scaled[:, 1:], later], axis=1)
-        image = normal_moved - kinetic(adjoint_shifted)
-        curve = expand(lax.psum(inner_local(direction, image), ("tm", "slab")))
-        alpha = norm_now / curve
-        solution = solution + alpha * direction
-        forward_sum = forward_sum + alpha * normal_moved
-        residual = residual - alpha * image
-        norm_next = squares(residual)
-        direction = residual + norm_next / norm_now * direction
-        norm_now = norm_next
-    image_y = forward_op(solution)
+    first = forward_op(sources)
+    normal = transposed_op(first)
+    second = forward_op(normal)
+    partial = jnp.concatenate(
+        [
+            inner_local(sources, sources),
+            inner_local(first, first),
+            inner_local(normal, normal),
+            inner_local(second, second),
+        ]
+    )
+    moments = jnp.sum(from_all(jnp.pad(partial, (0, 128 - partial.shape[0]))), axis=0)
+    low, high = krylov_coefficients(moments[: 4 * sources.shape[0]].reshape(4, -1))
+    expand = lambda values: values[:, None, None, None]
+    solution = expand(low) * sources + expand(high) * normal
+    image_y = expand(low) * first + expand(high) * second
     fermion_force = 2.0 * coupling * jnp.sum(image_y * (solution - image_y), axis=0)
     phonon_pad = extended(phonons, (("tm", 0),), 1)
     boson_force = restore * phonons + spring * (2.0 * phonons - phonon_pad[2:] - phonon_pad[:-2])

time: 349 us -> 120 us (0.34)
  blocking collectives: 249 us -> 17.7 us
  waiting for transfers between devices: 23.7 us -> 34.4 us
  starting transfers between devices: 52 us -> 44.1 us
    psum x3 -> x0, blocking collectives: 232 us -> none  [the longest x2 152 us: squares(): return expand(lax.psum(inner_local(field, field), ('tm', 'slab')))]
    all_to_all x0 -> x1, starting transfers between devices: none -> 16 us  [from_all(): return lax.all_to_all(copies, axes, split_axis=0, concat_axis=0, tiled=True)]
    ppermute x6 -> x4, starting transfers between devices: 16.7 us -> 8.17 us  [extended(): lax.ppermute(lax.slice_in_dim(block, 0, width, axis=dim), axis, backward)]
    all_to_all x0 -> x1, waiting for transfers between devices: none -> 7.96 us  [from_all(): return lax.all_to_all(copies, axes, split_axis=0, concat_axis=0, tiled=True)]
    ppermute x6 -> x4, starting transfers between devices: 20.9 us -> 13.4 us  [passed_along(): return lax.ppermute(block, axis, route)]
    all_to_all x1, starting transfers between devices: 11 us -> 5.05 us  [body(): lax.all_to_all(flat, 'tm', split_axis=1, concat_axis=0, tiled=True)]
  transfers between devices with their start and end apart: 19 -> 14, of which waited for: 11 -> 9; matrix products, arithmetic and copies ran while one was open for 3% -> 10% of each run, Pallas kernels for 0% -> 0%
where the time goes in v1:
time: 120 us
  starting transfers between devices  44.1 us (37%)
  waiting for transfers between devices  34.4 us (29%)
  blocking collectives  17.7 us (15%)
  other arithmetic  11.7 us (10%)
  local copies, waits for them, and re-layouts  10.4 us (9%)
    all_to_all x1, blocking collectives, body(): drift = lax.all_to_all(mixed, 'tm', split_axis=0, concat_axis=1, tiled=True)  17.7 us
    all_to_all x1, starting transfers between devices, from_all(): return lax.all_to_all(copies, axes, split_axis=0, concat_axis=0, tiled=True)  16 us
    ppermute x4, starting transfers between devices, passed_along(): return lax.ppermute(block, axis, route)  13.4 us
    all_to_all x1, waiting for transfers between devices, body(): lax.all_to_all(flat, 'tm', split_axis=1, concat_axis=0, tiled=True)  11.5 us
    ppermute x4, starting transfers between devices, extended(): lax.ppermute(lax.slice_in_dim(block, 0, width, axis=dim), axis, backward)  8.17 us
    all_to_all x1, waiting for transfers between devices, from_all(): return lax.all_to_all(copies, axes, split_axis=0, concat_axis=0, tiled=True)  7.96 us
    ppermute x4, waiting for transfers between devices, extended(): lax.ppermute(lax.slice_in_dim(block, block.shape[dim] - width, None, axis...  6.86 us
    ppermute x4, waiting for transfers between devices, passed_along(): return lax.ppermute(block, axis, route)  6.81 us
  transfers between devices with their start and end apart: 14, of which 9 were waited for; matrix products, arithmetic and copies ran while one was open for 10% of the time, Pallas kernels for 0%

profile of v1, /device:TPU:1, one launch (start us, length us, event | category | flops | bytes accessed | tf_op | source)
XLA Modules:
  0.0 119.7 jit_solution(2333081198636941457)
XLA Ops:
  1.4 2.1 %collective-permute-start.4 = (s32[1,512]{1,0:T(1,128)S(1)}, s32[1,512]{1,0:T(1,128)S(1)}, u32[]{:S(2)}, u32[]{:S(2)}) collective-permute-start(s32[1,512]{1,0:T(1,128)S(1)} %slice_bitcast_fusion), channel_id=1, source_target_pairs={{7,0},{0,1},{1,2},{2,3},{3,4},{4,5},{5,6},{6,7},{15,8},{8,9},{9,10... | collective-permute-start | bytes 6152 | tf_op jit(solution)/shard_map/ppermute | solution.py:16
  3.5 2.0 %fusion.43 = (f32[4,8,1,512]{3,2,1,0:T(1,128)}, f32[4,8,1,512]{3,2,1,0:T(1,128)}) fusion(f32[4,8,16,512]{3,2,1,0:T(8,128)} %param.5), kind=kLoop, calls=%fused_computation.91 | loop fusion | bytes 262144 | tf_op jit(solution)/shard_map/slice | solution.py:28
  5.4 2.2 %collective-permute-start.2 = (f32[4,8,1,512]{3,2,1,0:T(1,128)}, f32[4,8,1,512]{3,2,1,0:T(1,128)S(1)}, u32[]{:S(2)}, u32[]{:S(2)}) collective-permute-start(f32[4,8,1,512]{3,2,1,0:T(1,128)} %get-tuple-element.18), channel_id=1, source_target_pairs={{1,0},{2,1},{3,2},{4,3},{5,4},{6,5},{7,6},{0,7},{9,8},{10,9},{11,1... | collective-permute-start | bytes 196616 | tf_op jit(solution)/shard_map/ppermute | solution.py:28
  7.7 1.4 %broadcast_multiply_fusion.1 = f32[4,8,16,512]{3,2,1,0:T(8,128)S(1)} fusion(f32[4,8,16,512]{3,2,1,0:T(8,128)} %param.5, f32[16,512]{1,0:T(8,128)S(1)} %get-tuple-element.23), kind=kLoop, calls=%fused_computation.55 | loop fusion | flops 262144 | bytes 2129920 | tf_op jit(solution)/shard_map/mul | solution.py:76
  9.8 3.4 %collective-permute-done.3 = f32[4,8,1,512]{3,2,1,0:T(1,128)} collective-permute-done((f32[4,8,1,512]{3,2,1,0:T(1,128)}, f32[4,8,1,512]{3,2,1,0:T(1,128)}, u32[]{:S(2)}, u32[]{:S(2)}) %collective-permute-start.3) | collective-permute-done | bytes 65568 | tf_op jit(solution)/shard_map/ppermute | solution.py:25
  13.2 1.7 %multiply_reduce_fusion.3 = (f32[4]{0:T(128)S(1)}, f32[4,8,16,512]{3,2,1,0:T(8,128)S(1)}) fusion(f32[4,8,16,512]{3,2,1,0:T(8,128)S(1)} %copy-done.1, f32[16,512]{1,0:T(8,128)S(1)} %slice.212, f32[4,8,1,512]{3,2,1,0:T(1,128)} %collective-permute-done.3, f32[4,8,1,512]{3,2,1,0:T(1,128)S(1)} %collective-permute-done.2, f32[16,512]{1,0:T(8,128)S(1)} %get-tuple-element.22, ...), kind=kLoop, calls=%fused_computation.52 | loop fusion | flops 3670012 | bytes 4423696 | tf_op jit(solution)/shard_map/reduce_sum | solution.py:34
  14.9 4.0 %collective-permute-start.5 = (f32[4,1,16,512]{3,2,1,0:T(8,128)S(1)}, f32[4,1,16,512]{3,2,1,0:T(8,128)S(1)}, u32[]{:S(2)}, u32[]{:S(2)}) collective-permute-start(f32[4,1,16,512]{3,2,1,0:T(8,128)S(1)} %slice.213), channel_id=1, source_target_pairs={{248,0},{0,8},{8,16},{16,24},{24,32},{32,40},{40,48},{48,56},{56,6... | collective-permute-start | bytes 393224 | tf_op jit(solution)/shard_map/ppermute | solution.py:16
  19.1 1.8 %collective-permute-done.5 = f32[4,1,16,512]{3,2,1,0:T(8,128)S(1)} collective-permute-done((f32[4,1,16,512]{3,2,1,0:T(8,128)S(1)}, f32[4,1,16,512]{3,2,1,0:T(8,128)S(1)}, u32[]{:S(2)}, u32[]{:S(2)}) %collective-permute-start.5) | collective-permute-done | bytes 131104 | tf_op jit(solution)/shard_map/ppermute | solution.py:16
  21.5 6.3 %collective-permute-start.6 = (f32[4,1,16,512]{3,2,1,0:T(8,128)S(1)}, f32[4,1,16,512]{3,2,1,0:T(8,128)S(1)}, u32[]{:S(2)}, u32[]{:S(2)}) collective-permute-start(f32[4,1,16,512]{3,2,1,0:T(8,128)S(1)} %slice.216), channel_id=1, source_target_pairs={{8,0},{16,8},{24,16},{32,24},{40,32},{48,40},{56,48},{64,56},{72,6... | collective-permute-start | bytes 393224 | tf_op jit(solution)/shard_map/ppermute | solution.py:16
  29.4 1.4 %collective-permute-start.8 = (f32[4,8,1,512]{3,2,1,0:T(1,128)S(1)}, f32[4,8,1,512]{3,2,1,0:T(1,128)S(1)}, u32[]{:S(2)}, u32[]{:S(2)}) collective-permute-start(f32[4,8,1,512]{3,2,1,0:T(1,128)S(1)} %get-tuple-element.17), channel_id=1, source_target_pairs={{0,1},{1,2},{2,3},{3,4},{4,5},{5,6},{6,7},{7,0},{8,9},{9,10},{10,1... | collective-permute-start | bytes 196616 | tf_op jit(solution)/shard_map/ppermute | solution.py:25
  31.2 1.3 %collective-permute-done.7 = f32[4,8,1,512]{3,2,1,0:T(1,128)S(1)} collective-permute-done((f32[4,8,1,512]{3,2,1,0:T(1,128)S(1)}, f32[4,8,1,512]{3,2,1,0:T(1,128)S(1)}, u32[]{:S(2)}, u32[]{:S(2)}) %collective-permute-start.7) | collective-permute-done | bytes 65568 | tf_op jit(solution)/shard_map/ppermute | solution.py:28
  32.5 2.3 %collective-permute-done.8 = f32[4,8,1,512]{3,2,1,0:T(1,128)S(1)} collective-permute-done((f32[4,8,1,512]{3,2,1,0:T(1,128)S(1)}, f32[4,8,1,512]{3,2,1,0:T(1,128)S(1)}, u32[]{:S(2)}, u32[]{:S(2)}) %collective-permute-start.8) | collective-permute-done | bytes 65568 | tf_op jit(solution)/shard_map/ppermute | solution.py:25
  35.9 3.6 %collective-permute-start.9 = (f32[4,8,1,512]{3,2,1,0:T(1,128)S(1)}, f32[4,8,1,512]{3,2,1,0:T(1,128)S(1)}, u32[]{:S(2)}, u32[]{:S(2)}) collective-permute-start(f32[4,8,1,512]{3,2,1,0:T(1,128)S(1)} %get-tuple-element.14), channel_id=1, source_target_pairs={{1,0},{2,1},{3,2},{4,3},{5,4},{6,5},{7,6},{0,7},{9,8},{10,9},{11,1... | collective-permute-start | bytes 196616 | tf_op jit(solution)/shard_map/ppermute | solution.py:28
  40.0 1.1 collective-permute-done.10
  42.9 4.1 %collective-permute-done.11 = f32[4,1,16,512]{3,2,1,0:T(8,128)S(1)} collective-permute-done((f32[4,1,16,512]{3,2,1,0:T(8,128)S(1)}, f32[4,1,16,512]{3,2,1,0:T(8,128)S(1)}, u32[]{:S(2)}, u32[]{:S(2)}) %collective-permute-start.11) | collective-permute-done | bytes 131104 | tf_op jit(solution)/shard_map/ppermute | solution.py:16
  48.2 16.0 %all-to-all-start = ((f32[256,1,128]{2,1,0:T(1,128)}), f32[256,1,128]{2,1,0:T(1,128)}, u32[]{:S(2)}, u32[]{:S(2)}) async-start(f32[256,1,128]{2,1,0:T(1,128)} %broadcast_in_dim.12), calls=%async_computation | async-start | bytes 262144 | tf_op jit(solution)/shard_map/all_to_all | solution.py:41
  64.2 1.4 %fusion.44 = (f32[1,16,512]{2,1,0:T(8,128)}, f32[1,16,512]{2,1,0:T(8,128)}) fusion(f32[8,16,512]{2,1,0:T(8,128)} %param.6), kind=kLoop, calls=%fused_computation.92 | loop fusion | bytes 131072 | tf_op jit(solution)/shard_map/slice | solution.py:28
  65.6 2.2 %collective-permute-start = (f32[1,16,512]{2,1,0:T(8,128)}, f32[1,16,512]{2,1,0:T(8,128)}, u32[]{:S(2)}, u32[]{:S(2)}) collective-permute-start(f32[1,16,512]{2,1,0:T(8,128)} %get-tuple-element.20), channel_id=1, source_target_pairs={{8,0},{16,8},{24,16},{32,24},{40,32},{48,40},{56,48},{64,56},{72,6... | collective-permute-start | bytes 98312 | tf_op jit(solution)/shard_map/ppermute | solution.py:28
  67.8 8.0 %all-to-all-done = f32[256,1,128]{2,1,0:T(1,128)} async-done(((f32[256,1,128]{2,1,0:T(1,128)}), f32[256,1,128]{2,1,0:T(1,128)}, u32[]{:S(2)}, u32[]{:S(2)}) %all-to-all-start) | async-done | bytes 131104 | tf_op jit(solution)/shard_map/all_to_all | solution.py:41
  75.8 1.0 reduce_sum.58
  76.9 1.9 %fusion.1 = f32[8,16,512]{2,1,0:T(8,128)S(1)} fusion(f32[4,8,16,512]{3,2,1,0:T(8,128)S(1)} %get-tuple-element.11, f32[4,8,16,512]{3,2,1,0:T(8,128)S(1)} %copy-done.1, f32[4,8,16,512]{3,2,1,0:T(8,128)S(1)} %get-tuple-element.9, f32[4]{0:T(128)S(1)} %subtract_divide_fusion, f32[4]{0:T(128)S(1)} %get-tuple-element.4, f32[4,7,16,512]{3,2,1,0:T(8,128)} %copy-done.2, ...), kind=kLoop, calls=%fused_computation.11 | loop fusion | flops 3080192 | bytes 4718624 | tf_op jit(solution)/shard_map/reduce_sum | solution.py:106
  81.2 5.0 %all-to-all-start.1 = ((f32[8,32,256]{2,0,1:T(8,128)}), f32[8,32,256]{2,0,1:T(8,128)S(1)}, u32[]{:S(2)}, u32[]{:S(2)}) async-start(f32[8,32,256]{2,0,1:T(8,128)} %copy.13), calls=%async_computation.1 | async-start | bytes 524288 | tf_op jit(solution)/shard_map/all_to_all | solution.py:112
  88.3 11.5 %all-to-all-done.1 = f32[8,32,256]{2,0,1:T(8,128)S(1)} async-done(((f32[8,32,256]{2,0,1:T(8,128)}), f32[8,32,256]{2,0,1:T(8,128)S(1)}, u32[]{:S(2)}, u32[]{:S(2)}) %all-to-all-start.1) | async-done | bytes 262176 | tf_op jit(solution)/shard_map/all_to_all | solution.py:112
  100.2 17.7 %all_to_all.35 = f32[32,8,256]{2,1,0:T(8,128)S(1)} all-to-all(f32[32,8,256]{2,1,0:T(8,128)S(1)} %fusion.35), channel_id=1, replica_groups=mesh['tm'=32,'slab'=8] {'tm'}, dimensions={0} | all-to-all | bytes 524288 | tf_op jit(solution)/shard_map/all_to_all | solution.py:116
  (81 shorter events, 15.3 us)
Async XLA Ops:
  1.4 6.3 %copy-start.8 = (s32[2,16,512]{2,1,0:T(8,128)S(1)}, s32[2,16,512]{2,1,0:T(8,128)}, u32[]{:S(2)}) copy-start(s32[2,16,512]{2,1,0:T(8,128)} %param.9) | copy-start | bytes 196612
  1.4 8.4 %collective-permute-start.4 = (s32[1,512]{1,0:T(1,128)S(1)}, s32[1,512]{1,0:T(1,128)S(1)}, u32[]{:S(2)}, u32[]{:S(2)}) collective-permute-start(s32[1,512]{1,0:T(1,128)S(1)} %slice_bitcast_fusion), channel_id=1, source_target_pairs={{7,0},{0,1},{1,2},{2,3},{3,4},{4,5},{5,6},{6,7},{15,8},{8,9},{9,10... | collective-permute-start | bytes 6152 | tf_op jit(solution)/shard_map/ppermute | solution.py:16
  5.4 4.3 %collective-permute-start.2 = (f32[4,8,1,512]{3,2,1,0:T(1,128)}, f32[4,8,1,512]{3,2,1,0:T(1,128)S(1)}, u32[]{:S(2)}, u32[]{:S(2)}) collective-permute-start(f32[4,8,1,512]{3,2,1,0:T(1,128)} %get-tuple-element.18), channel_id=1, source_target_pairs={{1,0},{2,1},{3,2},{4,3},{5,4},{6,5},{7,6},{0,7},{9,8},{10,9},{11,1... | collective-permute-start | bytes 196616 | tf_op jit(solution)/shard_map/ppermute | solution.py:28
  7.7 5.5 %collective-permute-start.3 = (f32[4,8,1,512]{3,2,1,0:T(1,128)}, f32[4,8,1,512]{3,2,1,0:T(1,128)}, u32[]{:S(2)}, u32[]{:S(2)}) collective-permute-start(f32[4,8,1,512]{3,2,1,0:T(1,128)} %get-tuple-element.19), channel_id=1, source_target_pairs={{0,1},{1,2},{2,3},{3,4},{4,5},{5,6},{6,7},{7,0},{8,9},{9,10},{10,1... | collective-permute-start | bytes 196616 | tf_op jit(solution)/shard_map/ppermute | solution.py:25
  7.7 1.5 %copy-start = (f32[4,8,16,512]{3,2,1,0:T(8,128)S(1)}, f32[4,8,16,512]{3,2,1,0:T(8,128)}, u32[]{:S(2)}) copy-start(f32[4,8,16,512]{3,2,1,0:T(8,128)} %param.5) | copy-start | bytes 3145732
  9.2 4.0 %copy-start.1 = (f32[4,8,16,512]{3,2,1,0:T(8,128)S(1)}, f32[4,8,16,512]{3,2,1,0:T(8,128)}, u32[]{:S(2)}) copy-start(f32[4,8,16,512]{3,2,1,0:T(8,128)} %param.5) | copy-start | bytes 3145732
  9.6 3.6 %slice-start = ((f32[4,8,16,512]{3,2,1,0:T(8,128)}), f32[4,8,16,1]{3,2,1,0:T(8,128)S(1)}, s32[]{:S(2)}) async-start(f32[4,8,16,512]{3,2,1,0:T(8,128)} %param.5), calls=%async_computation.3 | async-start | bytes 524288 | tf_op jit(solution)/shard_map/jit(_roll_static)/slice | solution.py:76
  14.9 4.1 %copy-start.3 = (f32[8,16,512]{2,1,0:T(8,128)S(1)}, f32[8,16,512]{2,1,0:T(8,128)}, u32[]{:S(2)}) copy-start(f32[8,16,512]{2,1,0:T(8,128)} %param.6) | copy-start | bytes 786436
  14.9 6.0 %collective-permute-start.5 = (f32[4,1,16,512]{3,2,1,0:T(8,128)S(1)}, f32[4,1,16,512]{3,2,1,0:T(8,128)S(1)}, u32[]{:S(2)}, u32[]{:S(2)}) collective-permute-start(f32[4,1,16,512]{3,2,1,0:T(8,128)S(1)} %slice.213), channel_id=1, source_target_pairs={{248,0},{0,8},{8,16},{16,24},{24,32},{32,40},{40,48},{48,56},{56,6... | collective-permute-start | bytes 393224 | tf_op jit(solution)/shard_map/ppermute | solution.py:16
  21.5 7.3 %collective-permute-start.6 = (f32[4,1,16,512]{3,2,1,0:T(8,128)S(1)}, f32[4,1,16,512]{3,2,1,0:T(8,128)S(1)}, u32[]{:S(2)}, u32[]{:S(2)}) collective-permute-start(f32[4,1,16,512]{3,2,1,0:T(8,128)S(1)} %slice.216), channel_id=1, source_target_pairs={{8,0},{16,8},{24,16},{32,24},{40,32},{48,40},{56,48},{64,56},{72,6... | collective-permute-start | bytes 393224 | tf_op jit(solution)/shard_map/ppermute | solution.py:16
  29.3 3.2 %collective-permute-start.7 = (f32[4,8,1,512]{3,2,1,0:T(1,128)S(1)}, f32[4,8,1,512]{3,2,1,0:T(1,128)S(1)}, u32[]{:S(2)}, u32[]{:S(2)}) collective-permute-start(f32[4,8,1,512]{3,2,1,0:T(1,128)S(1)} %get-tuple-element.16), channel_id=1, source_target_pairs={{1,0},{2,1},{3,2},{4,3},{5,4},{6,5},{7,6},{0,7},{9,8},{10,9},{11,1... | collective-permute-start | bytes 196616 | tf_op jit(solution)/shard_map/ppermute | solution.py:28
  29.4 5.3 %collective-permute-start.8 = (f32[4,8,1,512]{3,2,1,0:T(1,128)S(1)}, f32[4,8,1,512]{3,2,1,0:T(1,128)S(1)}, u32[]{:S(2)}, u32[]{:S(2)}) collective-permute-start(f32[4,8,1,512]{3,2,1,0:T(1,128)S(1)} %get-tuple-element.17), channel_id=1, source_target_pairs={{0,1},{1,2},{2,3},{3,4},{4,5},{5,6},{6,7},{7,0},{8,9},{9,10},{10,1... | collective-permute-start | bytes 196616 | tf_op jit(solution)/shard_map/ppermute | solution.py:25
  35.8 5.3 %collective-permute-start.10 = (f32[4,8,1,512]{3,2,1,0:T(1,128)S(1)}, f32[4,8,1,512]{3,2,1,0:T(1,128)S(1)}, u32[]{:S(2)}, u32[]{:S(2)}) collective-permute-start(f32[4,8,1,512]{3,2,1,0:T(1,128)S(1)} %get-tuple-element.15), channel_id=1, source_target_pairs={{0,1},{1,2},{2,3},{3,4},{4,5},{5,6},{6,7},{7,0},{8,9},{9,10},{10,1... | collective-permute-start | bytes 196616 | tf_op jit(solution)/shard_map/ppermute | solution.py:25
  35.9 5.2 %collective-permute-start.9 = (f32[4,8,1,512]{3,2,1,0:T(1,128)S(1)}, f32[4,8,1,512]{3,2,1,0:T(1,128)S(1)}, u32[]{:S(2)}, u32[]{:S(2)}) collective-permute-start(f32[4,8,1,512]{3,2,1,0:T(1,128)S(1)} %get-tuple-element.14), channel_id=1, source_target_pairs={{1,0},{2,1},{3,2},{4,3},{5,4},{6,5},{7,6},{0,7},{9,8},{10,9},{11,1... | collective-permute-start | bytes 196616 | tf_op jit(solution)/shard_map/ppermute | solution.py:28
  41.9 5.1 %collective-permute-start.11 = (f32[4,1,16,512]{3,2,1,0:T(8,128)S(1)}, f32[4,1,16,512]{3,2,1,0:T(8,128)S(1)}, u32[]{:S(2)}, u32[]{:S(2)}) collective-permute-start(f32[4,1,16,512]{3,2,1,0:T(8,128)S(1)} %slice.235), channel_id=1, source_target_pairs={{248,0},{0,8},{8,16},{16,24},{24,32},{32,40},{40,48},{48,56},{56,6... | collective-permute-start | bytes 393224 | tf_op jit(solution)/shard_map/ppermute | solution.py:16
  42.9 4.5 %copy-start.2 = (f32[4,7,16,512]{3,2,1,0:T(8,128)}, f32[4,7,16,512]{3,2,1,0:T(8,128)S(1)}, u32[]{:S(2)}) copy-start(f32[4,7,16,512]{3,2,1,0:T(8,128)S(1)} %slice.236) | copy-start | bytes 2752516
  48.2 27.6 %all-to-all-start = ((f32[256,1,128]{2,1,0:T(1,128)}), f32[256,1,128]{2,1,0:T(1,128)}, u32[]{:S(2)}, u32[]{:S(2)}) async-start(f32[256,1,128]{2,1,0:T(1,128)} %broadcast_in_dim.12), calls=%async_computation | async-start | bytes 262144 | tf_op jit(solution)/shard_map/all_to_all | solution.py:41
  65.6 13.1 %collective-permute-start = (f32[1,16,512]{2,1,0:T(8,128)}, f32[1,16,512]{2,1,0:T(8,128)}, u32[]{:S(2)}, u32[]{:S(2)}) collective-permute-start(f32[1,16,512]{2,1,0:T(8,128)} %get-tuple-element.20), channel_id=1, source_target_pairs={{8,0},{16,8},{24,16},{32,24},{40,32},{48,40},{56,48},{64,56},{72,6... | collective-permute-start | bytes 98312 | tf_op jit(solution)/shard_map/ppermute | solution.py:28
  67.8 10.9 %collective-permute-start.1 = (f32[1,16,512]{2,1,0:T(8,128)}, f32[1,16,512]{2,1,0:T(8,128)}, u32[]{:S(2)}, u32[]{:S(2)}) collective-permute-start(f32[1,16,512]{2,1,0:T(8,128)} %get-tuple-element.21), channel_id=1, source_target_pairs={{0,8},{8,16},{16,24},{24,32},{32,40},{40,48},{48,56},{56,64},{64,7... | collective-permute-start | bytes 98312 | tf_op jit(solution)/shard_map/ppermute | solution.py:25
  76.9 1.9 %copy-start.4 = (f32[8,16,512]{2,1,0:T(8,128)S(1)}, f32[8,16,512]{2,1,0:T(8,128)}, u32[]{:S(2)}) copy-start(f32[8,16,512]{2,1,0:T(8,128)} %param.6) | copy-start | bytes 786436
  76.9 1.9 %copy-start.7 = (f32[8,16,512]{2,1,0:T(8,128)S(1)}, f32[8,16,512]{2,1,0:T(8,128)}, u32[]{:S(2)}) copy-start(f32[8,16,512]{2,1,0:T(8,128)} %param.7) | copy-start | bytes 786436
  81.2 5.1 %copy-start.9 = (f32[256]{0:T(256)S(1)}, f32[256]{0:T(256)}, u32[]{:S(2)}) copy-start(f32[256]{0:T(256)} %param.8) | copy-start | bytes 3076
  81.2 18.6 %all-to-all-start.1 = ((f32[8,32,256]{2,0,1:T(8,128)}), f32[8,32,256]{2,0,1:T(8,128)S(1)}, u32[]{:S(2)}, u32[]{:S(2)}) async-start(f32[8,32,256]{2,0,1:T(8,128)} %copy.13), calls=%async_computation.1 | async-start | bytes 524288 | tf_op jit(solution)/shard_map/all_to_all | solution.py:112
  118.0 1.0 copy-start.5
  (1 other events, 0.7 us)

commit v2 on v0

v2 whole, which is shorter than its diff:
```python
import jax
import jax.numpy as jnp
from jax import lax
from jax.experimental import pallas as pl
from jax.experimental.pallas import tpu as pltpu
from jax.sharding import PartitionSpec as P

hopping = 0.1
coupling = 0.2
restore = 0.25
spring = 0.25
stepsize = 0.5

LANES = 128
WIDE = 24
EARLY = 3
VMEM = pl.BlockSpec(memory_space=pltpu.VMEM)
PARAMS = pltpu.CompilerParams(vmem_limit_bytes=28 * 2**20)


def layout(entries):
    at, row = {}, 0
    for key, rows in entries:
        at[key] = (row, rows)
        row += rows
    return at, -(-row // 8) * 8


def side_layout(count, slices):
    depth = lambda t: min(3, slices - t)
    entries = [((i, t), depth(t)) for i in range(count) for t in range(slices)]
    entries += [((count, t), min(2, depth(t))) for t in range(slices)]
    return layout(entries + [(("bond", 0), 2), (("bond", 1), 3)])


def corner_layout(count):
    entries = [((i, t), 2 if t == -3 else 3) for i in range(count) for t in (-3, -2, -1)]
    return layout(entries + [((count, -2), 1), ((count, -1), 2)])


def pack_kernel(s_hbm, ph_hbm, pi_hbm, bond_hbm, up, down, up_corner, down_corner, ahead, s_ref, ph_ref, bond_ref, sems):
    count, slices, rows, _ = s_ref.shape
    copies = [
        pltpu.make_async_copy(ph_hbm, ph_ref, sems.at[0]),
        pltpu.make_async_copy(bond_hbm, bond_ref, sems.at[1]),
        pltpu.make_async_copy(pi_hbm.at[slices - 1], ahead.at[EARLY * count + 2], sems.at[2]),
    ]
    copies += [pltpu.make_async_copy(s_hbm.at[i], s_ref.at[i], sems.at[3 + i]) for i in range(count)]
    for copy in copies[3:] + copies[:3]:
        copy.start()
    side, _ = side_layout(count, slices)
    corner, _ = corner_layout(count)

    def rows_of(ref, n, last):
        return ref[pl.ds(rows - n if last else 0, n)]

    def field(source, entries, shift, out, last, wanted):
        for (key, t), (row, n) in entries.items():
            if key == wanted:
                out[pl.ds(row, n)] = rows_of(source.at[t + shift], n, last)

    for i in [*range(count), count]:
        if i < count:
            copies[3 + i].wait()
        else:
            copies[0].wait()
        source = s_ref.at[i] if i < count else ph_ref
        for last, out, out_corner in ((True, up, up_corner), (False, down, down_corner)):
            field(source, side, 0, out, last, i)
            field(source, corner, slices, out_corner, last, i)
        kept = EARLY if i < count else 2
        for j in range(kept):
            ahead[EARLY * i + j] = source[slices - kept + j]
    copies[1].wait()
    for k in range(2):
        for last, out in ((True, up), (False, down)):
            row, n = side[("bond", k)]
            out[pl.ds(row, n)] = rows_of(bond_ref.at[k], n, last).astype(jnp.float32)
    copies[2].wait()


def pack(sources, phonons, momenta, bonds):
    count, slices, rows, columns = sources.shape
    shape = lambda *n: jax.ShapeDtypeStruct(n + (columns,), jnp.float32)
    side, corner = side_layout(count, slices)[1], corner_layout(count)[1]
    return pl.pallas_call(
        pack_kernel,
        out_shape=[shape(side)] * 2 + [shape(corner)] * 2 + [shape(EARLY * count + 3, rows)],
        in_specs=[pl.BlockSpec(memory_space=pltpu.HBM)] * 4,
        out_specs=[VMEM] * 5,
        scratch_shapes=[
            pltpu.VMEM(sources.shape, jnp.float32),
            pltpu.VMEM(phonons.shape, jnp.float32),
            pltpu.VMEM(bonds.shape, bonds.dtype),
            pltpu.SemaphoreType.DMA((3 + count,)),
        ],
        compiler_params=pltpu.CompilerParams(vmem_limit_bytes=60 * 10**6),
        name="pack_halos",
    )(sources, phonons, momenta, bonds)


def operator_kernel(s_ref, ph_ref, bond_ref, above, below, above_corner, below_corner, before, *rest):
    p_ref, q_ref, t_ref, partial_ref, ext, weight, hh_ref, gg_ref, acc = rest
    count, slices, rows, columns = s_ref.shape
    side, _ = side_layout(count, slices)
    corner, _ = corner_layout(count)

    def widen(slot, key, t):
        row, n = (side if t >= 0 else corner)[key, t]
        lo, hi = (below, above) if t >= 0 else (below_corner, above_corner)
        slot[pl.ds(rows, n)] = lo[pl.ds(row, n)]
        slot[pl.ds(WIDE - n, n)] = hi[pl.ds(row, n)]

    for i in range(count):
        for t in range(-EARLY, slices):
            slot = ext.at[i, t + EARLY]
            slot[pl.ds(0, rows)] = before[EARLY * i + t + EARLY] if t < 0 else s_ref[i, t]
            widen(slot, i, t)
    for k, ref in ((0, hh_ref), (1, gg_ref)):
        row, n = side[("bond", k)]
        ref[pl.ds(0, rows)] = hopping * bond_ref[k].astype(jnp.float32)
        ref[pl.ds(rows, n)] = hopping * below[pl.ds(row, n)]
        ref[pl.ds(WIDE - n, n)] = hopping * above[pl.ds(row, n)]
    first = lax.axis_index("tm") == 0
    for t in range(-2, slices):
        slot = weight.at[t + 2]
        slot[pl.ds(0, rows)] = before[EARLY * count + t + 2] if t < 0 else ph_ref[t]
        widen(slot, count, t)
        value = jnp.exp(coupling * slot[...])
        slot[...] = value * jnp.where(first, -1.0, 1.0) if t == 0 else value

    def kinetic(v):
        hh, gg = hh_ref[...], gg_ref[...]
        beside = hh * pltpu.roll(v, columns - 1, 1) + pltpu.roll(hh * v, 1, 1)
        return v + (beside + gg * pltpu.roll(v, WIDE - 1, 0) + pltpu.roll(gg * v, 1, 0))

    def total(v):
        v = v[:8] + v[8:rows]
        return sum(v[:, c : c + LANES] for c in range(0, columns, LANES))

    def one_source(i, _):
        sums = [jnp.zeros((8, LANES), jnp.float32)] * 4
        p_old = q_old = None
        for t in range(-2, slices):
            s = ext[i, t + EARLY]
            w = weight[t + 2]
            p = s - w * kinetic(ext[i, t + EARLY - 1])
            if -1 <= t < slices - 1:
                p_ref[i, t + 1] = p[:rows]
                sums[0] += total(s[:rows] * s[:rows])
                sums[1] += total(p[:rows] * p[:rows])
            if t >= -1:
                q = p_old - kinetic(w * p)
                if t >= 0:
                    u = q - weight[t + 1] * kinetic(q_old)
                    q_ref[i, t] = q[:rows]
                    t_ref[i, t] = u[:rows]
                    sums[2] += total(q[:rows] * q[:rows])
                    sums[3] += total(u[:rows] * u[:rows])
                q_old = q
            p_old = p
        for k in range(4):
            acc[k * count + i] = sums[k]
        return 0

    lax.fori_loop(0, count, one_source, 0)
    lines = jnp.sum(acc[...], axis=1)
    lines = jnp.broadcast_to(jnp.sum(lines, axis=1, keepdims=True), lines.shape)
    at = lambda d: lax.broadcasted_iota(jnp.int32, lines.shape, d)
    row = jnp.sum(jnp.where(at(0) == at(1), lines, 0.0), axis=0, keepdims=True)
    partial_ref[...] = jnp.broadcast_to(row, partial_ref.shape)


def operators(sources, phonons, bonds, halos, everyone):
    count, slices, rows, columns = sources.shape
    f32 = lambda *shape: pltpu.VMEM(shape, jnp.float32)
    field = jax.ShapeDtypeStruct(sources.shape, jnp.float32)
    return pl.pallas_call(
        operator_kernel,
        out_shape=[field] * 3 + [jax.ShapeDtypeStruct((everyone, LANES), jnp.float32)],
        in_specs=[VMEM] * (3 + len(halos)),
        out_specs=[VMEM] * 4,
        scratch_shapes=[
            f32(count, slices + EARLY, WIDE, columns),
            f32(slices + 2, WIDE, columns),
            f32(WIDE, columns),
            f32(WIDE, columns),
            f32(4 * count, 8, LANES),
        ],
        compiler_params=PARAMS,
        name="operators",
    )(sources, phonons, bonds, *halos)


def force_kernel(mom_ref, s_ref, p_ref, q_ref, t_ref, ph_ref, before, pi_ref, half_ref, early_ref, send_ref):
    count, slices, rows, columns = s_ref.shape
    moments = jnp.sum(mom_ref[...], axis=0, keepdims=True)
    m = [moments] + [pltpu.roll(moments, LANES - count * k, 1) for k in range(1, 4)]
    alpha, square, cube = m[0] / m[1], m[2] / m[1], m[3] / m[1]
    spread = cube - square * square
    lane = lax.broadcasted_iota(jnp.int32, moments.shape, 1)

    def at(values, i):
        return jnp.sum(jnp.where(lane == i, values, 0.0))

    low = [at((alpha * cube - square) / spread, i) for i in range(count)]
    high = [at((1.0 - alpha * square) / spread, i) for i in range(count)]
    kept = EARLY * count
    phonon = lambda t: before[kept + 2 + t] if t < 0 else ph_ref[t]
    for t in range(-1, slices - 1):
        fermion = None
        for i in range(count):
            source = before[EARLY * i + EARLY - 1] if t < 0 else s_ref[i, t]
            x = low[i] * source + high[i] * q_ref[i, t + 1]
            y = low[i] * p_ref[i, t + 1] + high[i] * t_ref[i, t + 1]
            term = y * (x - y)
            fermion = term if fermion is None else fermion + term
        beside = phonon(t + 1) + phonon(t - 1)
        boson = restore * phonon(t) + spring * (2.0 * phonon(t) - beside)
        momentum = before[kept + 2] if t < 0 else pi_ref[t]
        half = momentum - 0.5 * stepsize * (boson + 2.0 * coupling * fermion)
        if t < 0:
            early_ref[...] = half
        else:
            half_ref[t] = half
        for r in range(0, rows, 2):
            for c in range(0, columns, LANES):
                send_ref[(r // 2) * (columns // LANES) + c // LANES, pl.ds(2 * (t + 1), 2)] = half[
                    r : r + 2, c : c + LANES
                ]


def force(received, sources, p, q, t, phonons, before, momenta, peers):
    slices, rows, columns = phonons.shape
    shape = lambda *n: jax.ShapeDtypeStruct(n, jnp.float32)
    return pl.pallas_call(
        force_kernel,
        out_shape=[shape(slices - 1, rows, columns), shape(rows, columns), shape(peers, 2 * slices, LANES)],
        in_specs=[VMEM] * 8,
        out_specs=[VMEM] * 3,
        compiler_params=PARAMS,
        name="force",
    )(received, sources, p, q, t, phonons, before, momenta)


def table_kernel(kernel_ref, table_ref):
    times = kernel_ref.shape[1]
    same = jnp.broadcast_to(pltpu.roll(kernel_ref[...], times - 1, 1), (times, times))
    shifted = pltpu.roll(same, 0, 1, stride=1, stride_axis=0)
    table_ref[...] = stepsize * jnp.transpose(shifted)


def circulant(kernel):
    times = kernel.shape[0]
    return pl.pallas_call(
        table_kernel,
        out_shape=jax.ShapeDtypeStruct((times, times), jnp.float32),
        in_specs=[VMEM],
        out_specs=VMEM,
        compiler_params=PARAMS,
        name="circulant",
    )(kernel[None])


def drift_kernel(table_ref, x_ref, out_ref):
    times = table_ref.shape[0]
    both = jnp.concatenate([x_ref[pl.ds(k, times, stride=2)] for k in range(2)], axis=1)
    mixed = jnp.dot(
        table_ref[...], both, precision=lax.Precision.HIGHEST, preferred_element_type=jnp.float32
    )
    for k in range(2):
        out_ref[pl.ds(k, times, stride=2)] = mixed[:, k * LANES : (k + 1) * LANES]


def drift(table, columns):
    flat = columns.reshape(-1, LANES)
    mixed = pl.pallas_call(
        drift_kernel,
        out_shape=jax.ShapeDtypeStruct(flat.shape, jnp.float32),
        in_specs=[VMEM] * 2,
        out_specs=VMEM,
        compiler_params=PARAMS,
        name="drift",
    )(table, flat)
    return mixed.reshape(columns.shape)


def add_kernel(ph_ref, back_ref, half_ref, late_ref, out_ref, all_ref):
    slices, rows, columns = ph_ref.shape
    for t in range(slices):
        all_ref[t] = half_ref[t] if t < slices - 1 else late_ref[...]
        for r in range(0, rows, 2):
            for c in range(0, columns, LANES):
                moved = back_ref[(r // 2) * (columns // LANES) + c // LANES, pl.ds(2 * t, 2)]
                out_ref[t, pl.ds(r, 2), pl.ds(c, LANES)] = ph_ref[t, pl.ds(r, 2), pl.ds(c, LANES)] + moved


def add_drift(phonons, back, half, late):
    field = jax.ShapeDtypeStruct(phonons.shape, jnp.float32)
    return pl.pallas_call(
        add_kernel,
        out_shape=[field] * 2,
        in_specs=[VMEM] * 4,
        out_specs=[VMEM] * 2,
        compiler_params=PARAMS,
        name="add_drift",
    )(phonons, back, half, late)


def passed_along(block, axis, distance):
    count = lax.axis_size(axis)
    return lax.ppermute(block, axis, [((i - distance) % count, i) for i in range(count)])


def passed_diagonally(block, times, slabs):
    nt, ns = lax.axis_size("tm"), lax.axis_size("slab")
    route = [
        (((i - times) % nt) * ns + (j - slabs) % ns, i * ns + j) for i in range(nt) for j in range(ns)
    ]
    return lax.ppermute(block, ("tm", "slab"), route)


def body(sources, phonons, momenta, kernel, bonds):
    peers = lax.axis_size("tm")
    everyone = peers * lax.axis_size("slab")
    up, down, up_corner, down_corner, ahead = pack(sources, phonons, momenta, bonds)
    above = passed_along(up, "slab", 1)
    below = passed_along(down, "slab", -1)
    above_corner = passed_diagonally(up_corner, 1, 1)
    below_corner = passed_diagonally(down_corner, 1, -1)
    before = passed_along(ahead, "tm", 1)
    table = circulant(kernel)
    halos = (above, below, above_corner, below_corner, before)
    halos, table = lax.optimization_barrier((halos, table))
    p, q, t, partial = operators(sources, phonons, bonds, halos, everyone)
    received = lax.all_to_all(partial, ("tm", "slab"), split_axis=0, concat_axis=0, tiled=True)
    half, early, send = force(received, sources, p, q, t, phonons, before, momenta, peers)
    columns = lax.all_to_all(send, "tm", split_axis=0, concat_axis=0, tiled=True)
    columns, late = lax.optimization_barrier((columns, passed_along(early, "tm", -1)))
    mixed = drift(table, columns)
    back = lax.all_to_all(mixed, "tm", split_axis=0, concat_axis=0, tiled=True)
    new_phonons, half_momenta = add_drift(phonons, back, half, late)
    return half_momenta, new_phonons


def solution(mesh):
    return jax.shard_map(
        body,
        mesh=mesh,
        in_specs=(
            P(None, "tm", "slab", None),
            P("tm", "slab", None),
            P("tm", "slab", None),
            P(),
            P(None, "slab", None),
        ),
        out_specs=(P("tm", "slab", None), P("tm", "slab", None)),
        check_vma=False,
    )
```

time: 349 us -> 92.8 us (0.27)
  blocking collectives: 249 us -> 40 us
  starting transfers between devices: 52 us -> 16.9 us
  other arithmetic: 11.9 us -> 0 us
  Pallas kernels: 0 us -> 11.1 us
  local copies, waits for them, and re-layouts: 9.07 us -> 0.03 us
    psum x3 -> x0, blocking collectives: 232 us -> none  [the longest x2 152 us: squares(): return expand(lax.psum(inner_local(field, field), ('tm', 'slab')))]
    ppermute x18 -> x6, starting transfers between devices: 41 us -> 12.3 us  [the longest x4 7.11 us: passed_along(): lax.ppermute(block, axis, [((i - distance) % count, i) for i in range(cou...]
    all_to_all x1 -> x2, blocking collectives: 17.7 us -> 40 us  [the longest x1 22.4 us: body(): lax.all_to_all(partial, ('tm', 'slab'), split_axis=0, concat_axis=0, tile...]
    pallas_call x0 -> x6, Pallas kernels: none -> 11.1 us  [the longest x1 5.74 us: operators(): pl.pallas_call(operator_kernel, out_shape=[field] * 3 + [jax.ShapeDtypeSt...]
    all_to_all x1, waiting for transfers between devices: 11.4 us -> 4.84 us  [body(): lax.all_to_all(send, 'tm', split_axis=0, concat_axis=0, tiled=True)]
    ppermute x18 -> x6, waiting for transfers between devices: 12.3 us -> 18.9 us  [the longest x2 10.6 us: passed_diagonally(): return lax.ppermute(block, ('tm', 'slab'), route)]
    all_to_all x1, starting transfers between devices: 11 us -> 4.55 us  [body(): lax.all_to_all(send, 'tm', split_axis=0, concat_axis=0, tiled=True)]
    slice x31 -> x0, local copies, waits for them, and re-layouts: 5.78 us -> none  [the longest x4 2.19 us: extended(): lax.slice_in_dim(block, 0, width, axis=dim)]
  transfers between devices with their start and end apart: 19 -> 7, of which waited for: 11 -> 4; matrix products, arithmetic and copies ran while one was open for 3% -> 0% of each run, Pallas kernels for 0% -> 0%
where the time goes in v2:
time: 92.8 us; the launch traced here: 92.5 us
  blocking collectives  40 us (43%)
  waiting for transfers between devices  23.7 us (26%)
  starting transfers between devices  16.9 us (18%)
  Pallas kernels  11.1 us (12%)
    all_to_all x1, blocking collectives, body(): lax.all_to_all(partial, ('tm', 'slab'), split_axis=0, concat_axis=0, tile...  22.4 us
    all_to_all x1, blocking collectives, body(): back = lax.all_to_all(mixed, 'tm', split_axis=0, concat_axis=0, tiled=True)  17.7 us
    ppermute x2, waiting for transfers between devices, passed_diagonally(): return lax.ppermute(block, ('tm', 'slab'), route)  10.6 us
    ppermute x4, waiting for transfers between devices, passed_along(): lax.ppermute(block, axis, [((i - distance) % count, i) for i in range(cou...  8.28 us
    ppermute x4, starting transfers between devices, passed_along(): lax.ppermute(block, axis, [((i - distance) % count, i) for i in range(cou...  7.11 us
    pallas_call x1, Pallas kernels, operators(): pl.pallas_call(operator_kernel, out_shape=[field] * 3 + [jax.ShapeDtypeSt...  5.74 us
    ppermute x2, starting transfers between devices, passed_diagonally(): return lax.ppermute(block, ('tm', 'slab'), route)  5.21 us
    all_to_all x1, waiting for transfers between devices, body(): lax.all_to_all(send, 'tm', split_axis=0, concat_axis=0, tiled=True)  4.84 us
  transfers between devices with their start and end apart: 7, of which 4 were waited for; matrix products, arithmetic and copies ran while one was open for 0% of the time, Pallas kernels for 0%

profile of v2, /device:TPU:1, one launch (start us, length us, event | category | flops | bytes accessed | tf_op | source)
XLA Modules:
  0.0 92.5 jit_solution(2805496348511936457)
XLA Ops:
  0.7 2.4 %pack_halos.1 = (f32[104,512]{1,0:T(8,128)}, f32[104,512]{1,0:T(8,128)}, f32[40,512]{1,0:T(8,128)}, f32[40,512]{1,0:T(8,128)}, f32[15,16,512]{2,1,0:T(8,128)}) custom-call(f32[4,8,16,512]{3,2,1,0:T(8,128)} %s_ref.3, f32[8,16,512]{2,1,0:T(8,128)} %ph_ref.5, f32[8,16,512]{2,1,0:T(8,128)} %pi_ref.1, s32[2,16,512]{2,1,0:T(8,128)} %bond_ref.1), custom_call_target="tpu_custom_call" | custom-call | tf_op jit(solution)/shard_map/pack_halos/pallas_call | solution.py:86
  3.1 0.0 copy-start.1
  3.1 3.1 %collective-permute-start.4 = (f32[15,16,512]{2,1,0:T(8,128)}, f32[15,16,512]{2,1,0:T(8,128)S(1)}, u32[]{:S(2)}, u32[]{:S(2)}) collective-permute-start(f32[15,16,512]{2,1,0:T(8,128)} %get-tuple-element.28), channel_id=1, source_target_pairs={{248,0},{0,8},{8,16},{16,24},{24,32},{32,40},{40,48},{48,56},{56,6... | collective-permute-start | bytes 1474568 | tf_op jit(solution)/shard_map/ppermute | solution.py:312
  6.2 1.3 %collective-permute-start = (f32[104,512]{1,0:T(8,128)}, f32[104,512]{1,0:T(8,128)S(1)}, u32[]{:S(2)}, u32[]{:S(2)}) collective-permute-start(f32[104,512]{1,0:T(8,128)} %get-tuple-element.24), channel_id=1, source_target_pairs={{7,0},{0,1},{1,2},{2,3},{3,4},{4,5},{5,6},{6,7},{15,8},{8,9},{9,10... | collective-permute-start | bytes 638984 | tf_op jit(solution)/shard_map/ppermute | solution.py:312
  7.5 2.3 %collective-permute-start.1 = (f32[104,512]{1,0:T(8,128)}, f32[104,512]{1,0:T(8,128)S(1)}, u32[]{:S(2)}, u32[]{:S(2)}) collective-permute-start(f32[104,512]{1,0:T(8,128)} %get-tuple-element.25), channel_id=1, source_target_pairs={{1,0},{2,1},{3,2},{4,3},{5,4},{6,5},{7,6},{0,7},{9,8},{10,9},{11,1... | collective-permute-start | bytes 638984 | tf_op jit(solution)/shard_map/ppermute | solution.py:312
  9.8 0.0 collective-permute-start.2
  9.8 5.2 %collective-permute-start.3 = (f32[40,512]{1,0:T(8,128)}, f32[40,512]{1,0:T(8,128)S(1)}, u32[]{:S(2)}, u32[]{:S(2)}) collective-permute-start(f32[40,512]{1,0:T(8,128)} %get-tuple-element.27), channel_id=1, source_target_pairs={{249,0},{250,1},{251,2},{252,3},{253,4},{254,5},{255,6},{248,7},{1... | collective-permute-start | bytes 245768 | tf_op jit(solution)/shard_map/ppermute | solution.py:320
  15.0 0.2 circulant.1.table_ref
  15.3 5.9 %collective-permute-done.2.above_corner = f32[40,512]{1,0:T(8,128)S(1)} collective-permute-done((f32[40,512]{1,0:T(8,128)}, f32[40,512]{1,0:T(8,128)S(1)}, u32[]{:S(2)}, u32[]{:S(2)}) %collective-permute-start.2) | collective-permute-done | bytes 81952 | tf_op jit(solution)/shard_map/ppermute | solution.py:320
  21.1 4.7 %collective-permute-done.3.below_corner = f32[40,512]{1,0:T(8,128)S(1)} collective-permute-done((f32[40,512]{1,0:T(8,128)}, f32[40,512]{1,0:T(8,128)S(1)}, u32[]{:S(2)}, u32[]{:S(2)}) %collective-permute-start.3) | collective-permute-done | bytes 81952 | tf_op jit(solution)/shard_map/ppermute | solution.py:320
  25.8 0.0 collective-permute-done.above
  25.9 0.0 collective-permute-done.1.below
  25.9 0.0 collective-permute-done.4.before
  25.9 5.7 %operators.1 = (f32[4,8,16,512]{3,2,1,0:T(8,128)S(1)}, f32[4,8,16,512]{3,2,1,0:T(8,128)S(1)}, f32[4,8,16,512]{3,2,1,0:T(8,128)S(1)}, f32[256,128]{1,0:T(8,128)S(1)}) custom-call(f32[4,8,16,512]{3,2,1,0:T(8,128)S(1)} %copy-done, f32[8,16,512]{2,1,0:T(8,128)S(1)} %copy-done.1, s32[2,16,512]{2,1,0:T(8,128)S(1)} %copy-done.3, ...), custom_call_target="tpu_custom_call" | custom-call | tf_op jit(solution)/shard_map/operators/pallas_call | solution.py:178
  31.6 0.0 copy-start.2
  31.6 22.4 %all_to_all.21 = f32[256,1,128]{2,1,0:T(1,128)S(1)} all-to-all(f32[256,1,128]{2,1,0:T(1,128)S(1)} %bitcast.10), channel_id=1, replica_groups=mesh['tm'=32,'slab'=8] {'tm','slab'}, dimensions={0} | all-to-all | bytes 262144 | tf_op jit(solution)/shard_map/all_to_all | solution.py:336
  54.0 1.4 %force.1 = (f32[7,16,512]{2,1,0:T(8,128)S(1)}, f32[16,512]{1,0:T(8,128)S(1)}, f32[32,16,128]{2,1,0:T(8,128)}) custom-call(f32[256,128]{1,0:T(8,128)S(1)} %bitcast.9, f32[4,8,16,512]{3,2,1,0:T(8,128)S(1)} %copy-done, f32[4,8,16,512]{3,2,1,0:T(8,128)S(1)} %get-tuple-element.36.p_ref, f32[4,8,16,512]{3,2,1,0:T(8,128)S(1)} %get-tuple-element.37.q_ref, ...), custom_call_target="tpu_custom_call" | custom-call | tf_op jit(solution)/shard_map/force/pallas_call | solution.py:236
  55.4 4.5 %all-to-all-start.1 = ((f32[32,16,128]{2,1,0:T(8,128)}), f32[32,16,128]{2,1,0:T(8,128)S(1)}, u32[]{:S(2)}, u32[]{:S(2)}) async-start(f32[32,16,128]{2,1,0:T(8,128)} %get-tuple-element.39), calls=%async_computation.1 | async-start | bytes 524288 | tf_op jit(solution)/shard_map/all_to_all | solution.py:338
  60.0 0.4 collective-permute-start.5
  60.4 8.3 %collective-permute-done.5.late_ref = f32[16,512]{1,0:T(8,128)S(1)} collective-permute-done((f32[16,512]{1,0:T(8,128)S(1)}, f32[16,512]{1,0:T(8,128)S(1)}, u32[]{:S(2)}, u32[]{:S(2)}) %collective-permute-start.5) | collective-permute-done | bytes 32800 | tf_op jit(solution)/shard_map/ppermute | solution.py:312
  68.7 4.8 %all-to-all-done.1 = f32[32,16,128]{2,1,0:T(8,128)S(1)} async-done(((f32[32,16,128]{2,1,0:T(8,128)}), f32[32,16,128]{2,1,0:T(8,128)S(1)}, u32[]{:S(2)}, u32[]{:S(2)}) %all-to-all-start.1) | async-done | bytes 262176 | tf_op jit(solution)/shard_map/all_to_all | solution.py:338
  73.5 0.4 drift.1
  73.9 17.7 %all_to_all.22.back_ref = f32[32,16,128]{2,1,0:T(8,128)S(1)} all-to-all(f32[32,16,128]{2,1,0:T(8,128)S(1)} %bitcast.8), channel_id=1, replica_groups=mesh['tm'=32,'slab'=8] {'tm'}, dimensions={0} | all-to-all | bytes 524288 | tf_op jit(solution)/shard_map/all_to_all | solution.py:341
  91.6 1.0 %add_drift.1 = (f32[8,16,512]{2,1,0:T(8,128)}, f32[8,16,512]{2,1,0:T(8,128)}) custom-call(f32[8,16,512]{2,1,0:T(8,128)S(1)} %copy-done.1, f32[32,16,128]{2,1,0:T(8,128)S(1)} %all_to_all.22.back_ref, f32[7,16,512]{2,1,0:T(8,128)S(1)} %get-tuple-element.42.half_ref, f32[16,512]{1,0:T(8,128)S(1)} %collective-permute-done.5.late_ref), custom_call_target="tpu_custom_call" | custom-call | tf_op jit(solution)/shard_map/add_drift/pallas_call | solution.py:300
  (8 shorter events, 0.0 us)
Async XLA Ops:
  0.6 25.2 %copy-start = (f32[4,8,16,512]{3,2,1,0:T(8,128)S(1)}, f32[4,8,16,512]{3,2,1,0:T(8,128)}, u32[]{:S(2)}) copy-start(f32[4,8,16,512]{3,2,1,0:T(8,128)} %s_ref.3) | copy-start | bytes 3145732
  0.6 14.4 %copy-start.4 = (f32[256]{0:T(256)S(1)}, f32[256]{0:T(256)}, u32[]{:S(2)}) copy-start(f32[256]{0:T(256)} %param.8) | copy-start | bytes 3076
  0.6 25.2 %copy-start.3 = (s32[2,16,512]{2,1,0:T(8,128)S(1)}, s32[2,16,512]{2,1,0:T(8,128)}, u32[]{:S(2)}) copy-start(s32[2,16,512]{2,1,0:T(8,128)} %bond_ref.1) | copy-start | bytes 196612
  3.1 22.8 %copy-start.1 = (f32[8,16,512]{2,1,0:T(8,128)S(1)}, f32[8,16,512]{2,1,0:T(8,128)}, u32[]{:S(2)}) copy-start(f32[8,16,512]{2,1,0:T(8,128)} %ph_ref.5) | copy-start | bytes 786436
  3.1 22.7 %collective-permute-start.4 = (f32[15,16,512]{2,1,0:T(8,128)}, f32[15,16,512]{2,1,0:T(8,128)S(1)}, u32[]{:S(2)}, u32[]{:S(2)}) collective-permute-start(f32[15,16,512]{2,1,0:T(8,128)} %get-tuple-element.28), channel_id=1, source_target_pairs={{248,0},{0,8},{8,16},{16,24},{24,32},{32,40},{40,48},{48,56},{56,6... | collective-permute-start | bytes 1474568 | tf_op jit(solution)/shard_map/ppermute | solution.py:312
  6.2 19.6 %collective-permute-start = (f32[104,512]{1,0:T(8,128)}, f32[104,512]{1,0:T(8,128)S(1)}, u32[]{:S(2)}, u32[]{:S(2)}) collective-permute-start(f32[104,512]{1,0:T(8,128)} %get-tuple-element.24), channel_id=1, source_target_pairs={{7,0},{0,1},{1,2},{2,3},{3,4},{4,5},{5,6},{6,7},{15,8},{8,9},{9,10... | collective-permute-start | bytes 638984 | tf_op jit(solution)/shard_map/ppermute | solution.py:312
  7.5 18.3 %collective-permute-start.1 = (f32[104,512]{1,0:T(8,128)}, f32[104,512]{1,0:T(8,128)S(1)}, u32[]{:S(2)}, u32[]{:S(2)}) collective-permute-start(f32[104,512]{1,0:T(8,128)} %get-tuple-element.25), channel_id=1, source_target_pairs={{1,0},{2,1},{3,2},{4,3},{5,4},{6,5},{7,6},{0,7},{9,8},{10,9},{11,1... | collective-permute-start | bytes 638984 | tf_op jit(solution)/shard_map/ppermute | solution.py:312
  9.8 11.3 %collective-permute-start.2 = (f32[40,512]{1,0:T(8,128)}, f32[40,512]{1,0:T(8,128)S(1)}, u32[]{:S(2)}, u32[]{:S(2)}) collective-permute-start(f32[40,512]{1,0:T(8,128)} %get-tuple-element.26), channel_id=1, source_target_pairs={{255,0},{248,1},{249,2},{250,3},{251,4},{252,5},{253,6},{254,7},{7... | collective-permute-start | bytes 245768 | tf_op jit(solution)/shard_map/ppermute | solution.py:320
  9.8 16.0 %collective-permute-start.3 = (f32[40,512]{1,0:T(8,128)}, f32[40,512]{1,0:T(8,128)S(1)}, u32[]{:S(2)}, u32[]{:S(2)}) collective-permute-start(f32[40,512]{1,0:T(8,128)} %get-tuple-element.27), channel_id=1, source_target_pairs={{249,0},{250,1},{251,2},{252,3},{253,4},{254,5},{255,6},{248,7},{1... | collective-permute-start | bytes 245768 | tf_op jit(solution)/shard_map/ppermute | solution.py:320
  31.6 22.4 %copy-start.2 = (f32[8,16,512]{2,1,0:T(8,128)S(1)}, f32[8,16,512]{2,1,0:T(8,128)}, u32[]{:S(2)}) copy-start(f32[8,16,512]{2,1,0:T(8,128)} %pi_ref.1) | copy-start | bytes 786436
  55.4 18.1 %all-to-all-start.1 = ((f32[32,16,128]{2,1,0:T(8,128)}), f32[32,16,128]{2,1,0:T(8,128)S(1)}, u32[]{:S(2)}, u32[]{:S(2)}) async-start(f32[32,16,128]{2,1,0:T(8,128)} %get-tuple-element.39), calls=%async_computation.1 | async-start | bytes 524288 | tf_op jit(solution)/shard_map/all_to_all | solution.py:338
  60.0 8.7 %collective-permute-start.5 = (f32[16,512]{1,0:T(8,128)S(1)}, f32[16,512]{1,0:T(8,128)S(1)}, u32[]{:S(2)}, u32[]{:S(2)}) collective-permute-start(f32[16,512]{1,0:T(8,128)S(1)} %get-tuple-element.40), channel_id=1, source_target_pairs={{8,0},{16,8},{24,16},{32,24},{40,32},{48,40},{56,48},{64,56},{72,6... | collective-permute-start | bytes 98312 | tf_op jit(solution)/shard_map/ppermute | solution.py:312

commit v3 on v2

v3 whole, which is shorter than its diff:
```python
import jax
import jax.numpy as jnp
from jax import lax
from jax.experimental import pallas as pl
from jax.experimental.pallas import tpu as pltpu
from jax.sharding import PartitionSpec as P

hopping = 0.1
coupling = 0.2
restore = 0.25
spring = 0.25
stepsize = 0.5

LANES = 128
WIDE = 24
EARLY = 3
VMEM = pl.BlockSpec(memory_space=pltpu.VMEM)
PARAMS = pltpu.CompilerParams(vmem_limit_bytes=28 * 2**20)


def layout(entries):
    at, row = {}, 0
    for key, rows in entries:
        at[key] = (row, rows)
        row += rows
    return at, -(-row // 8) * 8


def side_layout(count, slices):
    depth = lambda t: min(3, slices - t)
    entries = [((i, t), depth(t)) for i in range(count) for t in range(slices)]
    entries += [((count, t), min(2, depth(t))) for t in range(slices)]
    return layout(entries + [(("bond", 0), 2), (("bond", 1), 3)])


def corner_layout(count):
    entries = [((i, t), 2 if t == -3 else 3) for i in range(count) for t in (-3, -2, -1)]
    return layout(entries + [((count, -2), 1), ((count, -1), 2)])


def rows_of(ref, n, last):
    return ref[pl.ds(ref.shape[0] - n if last else 0, n)]


def side_kernel(s_hbm, ph_hbm, bond_hbm, up, down, s_ref, ph_ref, bond_ref, sems):
    count, slices = s_ref.shape[:2]
    copies = [pltpu.make_async_copy(s_hbm.at[i], s_ref.at[i], sems.at[i]) for i in range(count)]
    copies.append(pltpu.make_async_copy(ph_hbm, ph_ref, sems.at[count]))
    copies.append(pltpu.make_async_copy(bond_hbm, bond_ref, sems.at[count + 1]))
    for copy in copies:
        copy.start()
    side, _ = side_layout(count, slices)
    for i in range(count + 1):
        copies[i].wait()
        source = s_ref.at[i] if i < count else ph_ref
        for t in range(slices):
            row, n = side[i, t]
            up[pl.ds(row, n)] = rows_of(source.at[t], n, True)
            down[pl.ds(row, n)] = rows_of(source.at[t], n, False)
    copies[count + 1].wait()
    for k in range(2):
        row, n = side["bond", k]
        up[pl.ds(row, n)] = rows_of(bond_ref.at[k], n, True).astype(jnp.float32)
        down[pl.ds(row, n)] = rows_of(bond_ref.at[k], n, False).astype(jnp.float32)


def pack_sides(sources, phonons, bonds):
    count, slices, rows, columns = sources.shape
    side = jax.ShapeDtypeStruct((side_layout(count, slices)[1], columns), jnp.float32)
    whole = [jax.ShapeDtypeStruct(x.shape, x.dtype) for x in (sources, phonons, bonds)]
    return pl.pallas_call(
        side_kernel,
        out_shape=[side, side, *whole],
        in_specs=[pl.BlockSpec(memory_space=pltpu.HBM)] * 3,
        out_specs=[VMEM] * 5,
        scratch_shapes=[pltpu.SemaphoreType.DMA((count + 2,))],
        compiler_params=PARAMS,
        name="pack_sides",
    )(*(pltpu.with_memory_space_constraint(x, pltpu.HBM) for x in (sources, phonons, bonds)))


def ahead_kernel(s_ref, ph_ref, pi_hbm, ahead, sem):
    count, slices = s_ref.shape[:2]
    last = pltpu.make_async_copy(pi_hbm.at[slices - 1], ahead.at[EARLY * count + 2], sem)
    last.start()
    for i in range(count):
        for j in range(EARLY):
            ahead[EARLY * i + j] = s_ref[i, slices - EARLY + j]
    for j in range(2):
        ahead[EARLY * count + j] = ph_ref[slices - 2 + j]
    last.wait()


def pack_ahead(sources, phonons, momenta):
    count, _, rows, columns = sources.shape
    return pl.pallas_call(
        ahead_kernel,
        out_shape=jax.ShapeDtypeStruct((EARLY * count + 3, rows, columns), jnp.float32),
        in_specs=[VMEM, VMEM, pl.BlockSpec(memory_space=pltpu.HBM)],
        out_specs=VMEM,
        scratch_shapes=[pltpu.SemaphoreType.DMA(())],
        compiler_params=PARAMS,
        name="pack_ahead",
    )(sources, phonons, pltpu.with_memory_space_constraint(momenta, pltpu.HBM))


def corner_kernel(ahead, up, down):
    count = (ahead.shape[0] - 3) // EARLY
    corner, _ = corner_layout(count)
    for (i, t), (row, n) in corner.items():
        source = ahead.at[EARLY * i + (EARLY if i < count else 2) + t]
        up[pl.ds(row, n)] = rows_of(source, n, True)
        down[pl.ds(row, n)] = rows_of(source, n, False)


def pack_corners(ahead):
    rows = corner_layout((ahead.shape[0] - 3) // EARLY)[1]
    return pl.pallas_call(
        corner_kernel,
        out_shape=[jax.ShapeDtypeStruct((rows, ahead.shape[2]), jnp.float32)] * 2,
        in_specs=[VMEM],
        out_specs=[VMEM] * 2,
        compiler_params=PARAMS,
        name="pack_corners",
    )(ahead)


def kinetic(v, hh, gg):
    rows, columns = v.shape
    beside = hh * pltpu.roll(v, columns - 1, 1) + pltpu.roll(hh * v, 1, 1)
    return v + (beside + gg * pltpu.roll(v, rows - 1, 0) + pltpu.roll(gg * v, 1, 0))


def squares(v):
    columns = v.shape[1]
    v = v[:8] * v[:8] + v[8 : WIDE - 8] * v[8 : WIDE - 8]
    return sum(v[:, c : c + LANES] for c in range(0, columns, LANES))


def widen(slot, own, below, above, at):
    row, n = at
    slot[pl.ds(0, own.shape[0])] = own
    slot[pl.ds(own.shape[0], n)] = below[pl.ds(row, n)]
    slot[pl.ds(WIDE - n, n)] = above[pl.ds(row, n)]


def inner_kernel(
    s_ref, ph_ref, bond_ref, above, below, p_ref, q_ref, t_ref, s_edge, kp_edge, shared, acc, ext, weight
):
    count, slices = s_ref.shape[:2]
    side, _ = side_layout(count, slices)
    for k in range(2):
        widen(shared.at[k], bond_ref[k].astype(jnp.float32), below, above, side["bond", k])
        shared[k] = hopping * shared[k]
    first = lax.axis_index("tm") == 0
    for t in range(slices):
        slot = weight.at[t]
        widen(slot, ph_ref[t], below, above, side[count, t])
        value = jnp.exp(coupling * slot[...])
        slot[...] = value * jnp.where(first, -1.0, 1.0) if t == 0 else value
        for i in range(count):
            widen(ext.at[i, t], s_ref[i, t], below, above, side[i, t])
    for j in range(2):
        shared[2 + j] = weight[j]

    def one_source(i, _):
        moved = lambda v: kinetic(v, shared[0], shared[1])
        sums = [jnp.zeros((8, LANES), jnp.float32)] * 4
        own = s_ref.shape[2]
        p_old = q_old = None
        s_edge[i] = ext[i, 0]
        for t in range(1, slices):
            s = ext[i, t]
            p = s - weight[t] * moved(ext[i, t - 1])
            if t < slices - 1:
                p_ref[i, t - 1] = p[:own]
                sums[0] += squares(s)
                sums[1] += squares(p)
            back = moved(weight[t] * p)
            if t == 1:
                kp_edge[i] = back
            else:
                q = p_old - back
                q_ref[i, t - 2] = q[:own]
                sums[2] += squares(q)
                if t > 2:
                    u = q - weight[t - 1] * moved(q_old)
                    t_ref[i, t - 3] = u[:own]
                    sums[3] += squares(u)
                q_old = q
            p_old = p
        for k in range(4):
            acc[k * count + i] = sums[k]
        return 0

    lax.fori_loop(0, count, one_source, 0)


def inner_operators(sources, phonons, bonds, above, below):
    count, slices, rows, columns = sources.shape
    shape = lambda *n: jax.ShapeDtypeStruct(n, jnp.float32)
    field = lambda times: shape(count, times, rows, columns)
    wide = lambda n: shape(n, WIDE, columns)
    return pl.pallas_call(
        inner_kernel,
        out_shape=[
            field(slices - 2),
            field(slices - 2),
            field(slices - 3),
            wide(count),
            wide(count),
            wide(4),
            shape(4 * count, 8, LANES),
        ],
        in_specs=[VMEM] * 5,
        out_specs=[VMEM] * 7,
        scratch_shapes=[
            pltpu.VMEM((count, slices, WIDE, columns), jnp.float32),
            pltpu.VMEM((slices, WIDE, columns), jnp.float32),
        ],
        compiler_params=PARAMS,
        name="inner_operators",
    )(sources, phonons, bonds, above, below)


def outer_kernel(
    before, above, below, q_inner, s_edge, kp_edge, shared, acc_inner, p_ref, q_ref, t_ref, partial_ref, ext, weight, acc
):
    count = s_edge.shape[0]
    own = before.shape[1]
    corner, _ = corner_layout(count)
    for i in range(count):
        for j in range(EARLY):
            widen(ext.at[i, j], before[EARLY * i + j], below, above, corner[i, j - EARLY])
    for j in range(2):
        widen(weight.at[j], before[EARLY * count + j], below, above, corner[count, j - 2])
        weight[j] = jnp.exp(coupling * weight[j])

    def one_source(i, _):
        moved = lambda v: kinetic(v, shared[0], shared[1])
        w = [weight[0], weight[1], shared[2], shared[3]]
        s = [ext[i, 0], ext[i, 1], ext[i, 2], s_edge[i]]
        p = [s[j + 1] - w[j] * moved(s[j]) for j in range(3)]
        q = [p[0] - moved(w[1] * p[1]), p[1] - moved(w[2] * p[2]), p[2] - kp_edge[i]]
        u = [q[1] - w[1] * moved(q[0]), q[2] - w[2] * moved(q[1])]
        u.append(q_inner[i, 0] - w[3][:own] * moved(q[2])[:own])
        for j in range(2):
            p_ref[i, j] = p[j + 1][:own]
            q_ref[i, j] = q[j + 1][:own]
        for j in range(3):
            t_ref[i, j] = u[j][:own]
        for k, fields in enumerate((s[2:], p[1:], q[1:], u)):
            acc[k * count + i] = acc_inner[k * count + i] + sum(squares(v) for v in fields)
        return 0

    lax.fori_loop(0, count, one_source, 0)
    lines = jnp.sum(acc[...], axis=1)
    lines = jnp.broadcast_to(jnp.sum(lines, axis=1, keepdims=True), lines.shape)
    at = lambda d: lax.broadcasted_iota(jnp.int32, lines.shape, d)
    row = jnp.sum(jnp.where(at(0) == at(1), lines, 0.0), axis=0, keepdims=True)
    partial_ref[...] = jnp.broadcast_to(row, partial_ref.shape)


def outer_operators(before, above, below, inner, everyone):
    _, q_inner, _, s_edge, kp_edge, shared, acc = inner
    count, _, rows, columns = q_inner.shape
    field = lambda times: jax.ShapeDtypeStruct((count, times, rows, columns), jnp.float32)
    return pl.pallas_call(
        outer_kernel,
        out_shape=[field(2), field(2), field(3), jax.ShapeDtypeStruct((everyone, LANES), jnp.float32)],
        in_specs=[VMEM] * 8,
        out_specs=[VMEM] * 4,
        scratch_shapes=[
            pltpu.VMEM((count, EARLY, WIDE, columns), jnp.float32),
            pltpu.VMEM((2, WIDE, columns), jnp.float32),
            pltpu.VMEM((4 * count, 8, LANES), jnp.float32),
        ],
        compiler_params=PARAMS,
        name="outer_operators",
    )(before, above, below, q_inner, s_edge, kp_edge, shared, acc)


def force_kernel(
    mom_ref, s_ref, p_in, q_in, t_in, p_out, q_out, t_out, ph_ref, before, pi_ref, half_ref, early_ref, send_ref
):
    count, slices, rows, columns = s_ref.shape
    moments = jnp.sum(mom_ref[...], axis=0, keepdims=True)
    m = [moments] + [pltpu.roll(moments, LANES - count * k, 1) for k in range(1, 4)]
    alpha, square, cube = m[0] / m[1], m[2] / m[1], m[3] / m[1]
    spread = cube - square * square
    lane = lax.broadcasted_iota(jnp.int32, moments.shape, 1)

    def at(values, i):
        return jnp.sum(jnp.where(lane == i, values, 0.0))

    low = [at((alpha * cube - square) / spread, i) for i in range(count)]
    high = [at((1.0 - alpha * square) / spread, i) for i in range(count)]
    kept = EARLY * count
    phonon = lambda t: before[kept + 2 + t] if t < 0 else ph_ref[t]
    for t in range(-1, slices - 1):
        fermion = None
        for i in range(count):
            source = before[EARLY * i + EARLY - 1] if t < 0 else s_ref[i, t]
            p, q = (p_out[i, t + 1], q_out[i, t + 1]) if t < 1 else (p_in[i, t - 1], q_in[i, t - 1])
            x = low[i] * source + high[i] * q
            y = low[i] * p + high[i] * (t_out[i, t + 1] if t < 2 else t_in[i, t - 2])
            term = y * (x - y)
            fermion = term if fermion is None else fermion + term
        beside = phonon(t + 1) + phonon(t - 1)
        boson = restore * phonon(t) + spring * (2.0 * phonon(t) - beside)
        momentum = before[kept + 2] if t < 0 else pi_ref[t]
        half = momentum - 0.5 * stepsize * (boson + 2.0 * coupling * fermion)
        if t < 0:
            early_ref[...] = half
        else:
            half_ref[t] = half
        for r in range(0, rows, 2):
            for c in range(0, columns, LANES):
                send_ref[(r // 2) * (columns // LANES) + c // LANES, pl.ds(2 * (t + 1), 2)] = half[
                    r : r + 2, c : c + LANES
                ]


def force(received, sources, inner, outer, phonons, before, momenta, peers):
    slices, rows, columns = phonons.shape
    shape = lambda *n: jax.ShapeDtypeStruct(n, jnp.float32)
    return pl.pallas_call(
        force_kernel,
        out_shape=[shape(slices - 1, rows, columns), shape(rows, columns), shape(peers, 2 * slices, LANES)],
        in_specs=[VMEM] * 11,
        out_specs=[VMEM] * 3,
        compiler_params=PARAMS,
        name="force",
    )(received, sources, *inner[:3], *outer[:3], phonons, before, momenta)


def table_kernel(kernel_ref, table_ref):
    times = kernel_ref.shape[1]
    same = jnp.broadcast_to(pltpu.roll(kernel_ref[...], times - 1, 1), (times, times))
    shifted = pltpu.roll(same, 0, 1, stride=1, stride_axis=0)
    table_ref[...] = stepsize * jnp.transpose(shifted)


def circulant(kernel):
    times = kernel.shape[0]
    return pl.pallas_call(
        table_kernel,
        out_shape=jax.ShapeDtypeStruct((times, times), jnp.float32),
        in_specs=[VMEM],
        out_specs=VMEM,
        compiler_params=PARAMS,
        name="circulant",
        cost_estimate=pl.CostEstimate(flops=10**11, bytes_accessed=10**6, transcendentals=0),
    )(kernel[None])


def drift_kernel(table_ref, x_ref, out_ref):
    times = table_ref.shape[0]
    both = jnp.concatenate([x_ref[pl.ds(k, times, stride=2)] for k in range(2)], axis=1)
    mixed = jnp.dot(
        table_ref[...], both, precision=lax.Precision.HIGHEST, preferred_element_type=jnp.float32
    )
    for k in range(2):
        out_ref[pl.ds(k, times, stride=2)] = mixed[:, k * LANES : (k + 1) * LANES]


def drift(table, columns):
    flat = columns.reshape(-1, LANES)
    mixed = pl.pallas_call(
        drift_kernel,
        out_shape=jax.ShapeDtypeStruct(flat.shape, jnp.float32),
        in_specs=[VMEM] * 2,
        out_specs=VMEM,
        compiler_params=PARAMS,
        name="drift",
    )(table, flat)
    return mixed.reshape(columns.shape)


def add_kernel(ph_ref, back_ref, half_ref, late_ref, out_ref, all_ref):
    slices, rows, columns = ph_ref.shape
    for t in range(slices):
        all_ref[t] = half_ref[t] if t < slices - 1 else late_ref[...]
        for r in range(0, rows, 2):
            for c in range(0, columns, LANES):
                moved = back_ref[(r // 2) * (columns // LANES) + c // LANES, pl.ds(2 * t, 2)]
                out_ref[t, pl.ds(r, 2), pl.ds(c, LANES)] = ph_ref[t, pl.ds(r, 2), pl.ds(c, LANES)] + moved


def add_drift(phonons, back, half, late):
    field = jax.ShapeDtypeStruct(phonons.shape, jnp.float32)
    return pl.pallas_call(
        add_kernel,
        out_shape=[field] * 2,
        in_specs=[VMEM] * 4,
        out_specs=[VMEM] * 2,
        compiler_params=PARAMS,
        name="add_drift",
    )(phonons, back, half, late)


def passed_along(block, axis, distance):
    count = lax.axis_size(axis)
    return lax.ppermute(block, axis, [((i - distance) % count, i) for i in range(count)])


def passed_diagonally(block, times, slabs):
    nt, ns = lax.axis_size("tm"), lax.axis_size("slab")
    route = [
        (((i - times) % nt) * ns + (j - slabs) % ns, i * ns + j) for i in range(nt) for j in range(ns)
    ]
    return lax.ppermute(block, ("tm", "slab"), route)


def body(sources, phonons, momenta, kernel, bonds):
    peers = lax.axis_size("tm")
    everyone = peers * lax.axis_size("slab")
    up, down, sources, phonons, bonds = pack_sides(sources, phonons, bonds)
    above = passed_along(up, "slab", 1)
    below = passed_along(down, "slab", -1)
    ahead = pack_ahead(sources, phonons, momenta)
    before = passed_along(ahead, "tm", 1)
    up_corner, down_corner = pack_corners(ahead)
    above_corner = passed_diagonally(up_corner, 1, 1)
    below_corner = passed_diagonally(down_corner, 1, -1)
    (above, below), table = lax.optimization_barrier(((above, below), circulant(kernel)))
    inner = inner_operators(sources, phonons, bonds, above, below)
    outer = outer_operators(before, above_corner, below_corner, inner, everyone)
    received = lax.all_to_all(outer[3], ("tm", "slab"), split_axis=0, concat_axis=0, tiled=True)
    half, early, send = force(received, sources, inner, outer, phonons, before, momenta, peers)
    columns = lax.all_to_all(send, "tm", split_axis=0, concat_axis=0, tiled=True)
    columns, late = lax.optimization_barrier((columns, passed_along(early, "tm", -1)))
    mixed = drift(table, columns)
    back = lax.all_to_all(mixed, "tm", split_axis=0, concat_axis=0, tiled=True)
    new_phonons, half_momenta = add_drift(phonons, back, half, late)
    return half_momenta, new_phonons


def solution(mesh):
    return jax.shard_map(
        body,
        mesh=mesh,
        in_specs=(
            P(None, "tm", "slab", None),
            P("tm", "slab", None),
            P("tm", "slab", None),
            P(),
            P(None, "slab", None),
        ),
        out_specs=(P("tm", "slab", None), P("tm", "slab", None)),
        check_vma=False,
    )
```

time: 92.8 us -> 89.9 us (0.969)
  waiting for transfers between devices: 23.7 us -> 18.7 us
  blocking collectives: 40 us -> 41.8 us
    ppermute x2, waiting for transfers between devices: 10.6 us -> 0.01 us  [passed_diagonally(): return lax.ppermute(block, ('tm', 'slab'), route)]
    ppermute x4, waiting for transfers between devices: 8.28 us -> 13.9 us  [passed_along(): lax.ppermute(block, axis, [((i - distance) % count, i) for i in range(cou...]
    all_to_all x1, blocking collectives: 22.4 us -> 24.1 us  [body(): lax.all_to_all(outer[3], ('tm', 'slab'), split_axis=0, concat_axis=0, til...]
    pallas_call x2 -> x5, Pallas kernels: 8.17 us -> 7.87 us  [the longest x1 3.94 us: inner_operators(): pl.pallas_call(inner_kernel, out_shape=[field(slices - 2), field(slices -...]
  transfers between devices with their start and end apart: 7 -> 7, of which waited for: 4 -> 3; matrix products, arithmetic and copies ran while one was open for 0% -> 0% of each run, Pallas kernels for 0% -> 6%
where the time goes in v3:
time: 89.9 us; the launch traced here: 89.6 us
  blocking collectives  41.8 us (46%)
  waiting for transfers between devices  18.7 us (21%)
  starting transfers between devices  17.6 us (20%)
  Pallas kernels  10.8 us (12%)
    all_to_all x1, blocking collectives, body(): lax.all_to_all(outer[3], ('tm', 'slab'), split_axis=0, concat_axis=0, til...  24.1 us
    all_to_all x1, blocking collectives, body(): back = lax.all_to_all(mixed, 'tm', split_axis=0, concat_axis=0, tiled=True)  17.7 us
    ppermute x4, waiting for transfers between devices, passed_along(): lax.ppermute(block, axis, [((i - distance) % count, i) for i in range(cou...  13.9 us
    ppermute x4, starting transfers between devices, passed_along(): lax.ppermute(block, axis, [((i - distance) % count, i) for i in range(cou...  7.74 us
    ppermute x2, starting transfers between devices, passed_diagonally(): return lax.ppermute(block, ('tm', 'slab'), route)  5.27 us
    all_to_all x1, waiting for transfers between devices, body(): lax.all_to_all(send, 'tm', split_axis=0, concat_axis=0, tiled=True)  4.84 us
    all_to_all x1, starting transfers between devices, body(): lax.all_to_all(send, 'tm', split_axis=0, concat_axis=0, tiled=True)  4.55 us
    pallas_call x1, Pallas kernels, inner_operators(): pl.pallas_call(inner_kernel, out_shape=[field(slices - 2), field(slices -...  3.94 us
  transfers between devices with their start and end apart: 7, of which 3 were waited for; matrix products, arithmetic and copies ran while one was open for 0% of the time, Pallas kernels for 6%

profile of v3, /device:TPU:1, one launch (start us, length us, event | category | flops | bytes accessed | tf_op | source)
XLA Modules:
  0.0 89.6 jit_solution(9765489035153445870)
XLA Ops:
  0.6 1.4 %pack_sides.1 = (f32[104,512]{1,0:T(8,128)S(1)}, f32[104,512]{1,0:T(8,128)S(1)}, f32[4,8,16,512]{3,2,1,0:T(8,128)S(1)}, f32[8,16,512]{2,1,0:T(8,128)S(1)}, s32[2,16,512]{2,1,0:T(8,128)S(1)}) custom-call(f32[4,8,16,512]{3,2,1,0:T(8,128)} %s_hbm.1, f32[8,16,512]{2,1,0:T(8,128)} %ph_hbm.1, s32[2,16,512]{2,1,0:T(8,128)} %bond_hbm.1), custom_call_target="tpu_custom_call" | custom-call | tf_op jit(solution)/shard_map/pack_sides/pallas_call | solution.py:71
  2.0 2.2 %collective-permute-start = (f32[104,512]{1,0:T(8,128)S(1)}, f32[104,512]{1,0:T(8,128)S(1)}, u32[]{:S(2)}, u32[]{:S(2)}) collective-permute-start(f32[104,512]{1,0:T(8,128)S(1)} %get-tuple-element.31), channel_id=1, source_target_pairs={{7,0},{0,1},{1,2},{2,3},{3,4},{4,5},{5,6},{6,7},{15,8},{8,9},{9,10... | collective-permute-start | bytes 638984 | tf_op jit(solution)/shard_map/ppermute | solution.py:404
  4.2 2.3 %collective-permute-start.1 = (f32[104,512]{1,0:T(8,128)S(1)}, f32[104,512]{1,0:T(8,128)S(1)}, u32[]{:S(2)}, u32[]{:S(2)}) collective-permute-start(f32[104,512]{1,0:T(8,128)S(1)} %get-tuple-element.32), channel_id=1, source_target_pairs={{1,0},{2,1},{3,2},{4,3},{5,4},{6,5},{7,6},{0,7},{9,8},{10,9},{11,1... | collective-permute-start | bytes 638984 | tf_op jit(solution)/shard_map/ppermute | solution.py:404
  6.5 0.8 pack_ahead.1.ahead
  7.3 2.8 %collective-permute-start.2 = (f32[15,16,512]{2,1,0:T(8,128)S(1)}, f32[15,16,512]{2,1,0:T(8,128)S(1)}, u32[]{:S(2)}, u32[]{:S(2)}) collective-permute-start(f32[15,16,512]{2,1,0:T(8,128)S(1)} %pack_ahead.1.ahead), channel_id=1, source_target_pairs={{248,0},{0,8},{8,16},{16,24},{24,32},{32,40},{40,48},{48,56},{56,6... | collective-permute-start | bytes 1474568 | tf_op jit(solution)/shard_map/ppermute | solution.py:404
  10.1 0.1 collective-permute-start.3
  10.2 0.0 copy-start.1
  10.2 5.2 %collective-permute-start.4 = (f32[40,512]{1,0:T(8,128)S(1)}, f32[40,512]{1,0:T(8,128)S(1)}, u32[]{:S(2)}, u32[]{:S(2)}) collective-permute-start(f32[40,512]{1,0:T(8,128)S(1)} %get-tuple-element.36), channel_id=1, source_target_pairs={{249,0},{250,1},{251,2},{252,3},{253,4},{254,5},{255,6},{248,7},{1... | collective-permute-start | bytes 245768 | tf_op jit(solution)/shard_map/ppermute | solution.py:412
  15.4 0.2 circulant.1.table_ref
  15.7 0.0 collective-permute-done.above
  15.7 5.6 %collective-permute-done.1.below = f32[104,512]{1,0:T(8,128)S(1)} collective-permute-done((f32[104,512]{1,0:T(8,128)S(1)}, f32[104,512]{1,0:T(8,128)S(1)}, u32[]{:S(2)}, u32[]{:S(2)}) %collective-permute-start.1) | collective-permute-done | bytes 213024 | tf_op jit(solution)/shard_map/ppermute | solution.py:404
  21.3 3.9 %inner_operators.1 = (f32[4,6,16,512]{3,2,1,0:T(8,128)S(1)}, f32[4,6,16,512]{3,2,1,0:T(8,128)S(1)}, f32[4,5,16,512]{3,2,1,0:T(8,128)S(1)}, f32[4,24,512]{2,1,0:T...) custom-call(f32[4,8,16,512]{3,2,1,0:T(8,128)S(1)} %get-tuple-element.34.s_ref, ...), custom_call_target="tpu_custom_call" | custom-call | tf_op jit(solution)/shard_map/inner_operators/pallas_call | solution.py:204
  25.2 0.0 collective-permute-done.3.above
  25.3 1.8 %outer_operators.1 = (f32[4,2,16,512]{3,2,1,0:T(8,128)S(1)}, f32[4,2,16,512]{3,2,1,0:T(8,128)S(1)}, f32[4,3,16,512]{3,2,1,0:T(8,128)S(1)}, f32[256,128]{1,0:T(8,128)S(1)}) custom-call(f32[15,16,512]{2,1,0:T(8,128)S(1)} %collective-permute-done.2.before, f32[40,512]{1,0:T(8,128)S(1)} %collective-permute-done.3.above, ...), custom_call_target="tpu_custom_call" | custom-call | tf_op jit(solution)/shard_map/outer_operators/pallas_call | solution.py:268
  27.0 0.0 copy-start
  27.0 24.1 %all_to_all.21 = f32[256,1,128]{2,1,0:T(1,128)S(1)} all-to-all(f32[256,1,128]{2,1,0:T(1,128)S(1)} %bitcast.10), channel_id=1, replica_groups=mesh['tm'=32,'slab'=8] {'tm','slab'}, dimensions={0} | all-to-all | bytes 262144 | tf_op jit(solution)/shard_map/all_to_all | solution.py:429
  51.1 1.4 %force.1 = (f32[7,16,512]{2,1,0:T(8,128)S(1)}, f32[16,512]{1,0:T(8,128)S(1)}, f32[32,16,128]{2,1,0:T(8,128)}) custom-call(f32[256,128]{1,0:T(8,128)S(1)} %bitcast.9, f32[4,8,16,512]{3,2,1,0:T(8,128)S(1)} %get-tuple-element.34.s_ref, f32[4,6,16,512]{3,2,1,0:T(8,128)S(1)} %get-tuple-element.46.p_in, f32[4,6,16,512]{3,2,1,0:T(8,128)S(1)} %get-tuple-element.40.q_inner.q_in, ...), custom_call_target="tpu_custom_call" | custom-call | tf_op jit(solution)/shard_map/force/pallas_call | solution.py:327
  52.5 4.6 %all-to-all-start.1 = ((f32[32,16,128]{2,1,0:T(8,128)}), f32[32,16,128]{2,1,0:T(8,128)S(1)}, u32[]{:S(2)}, u32[]{:S(2)}) async-start(f32[32,16,128]{2,1,0:T(8,128)} %get-tuple-element.51), calls=%async_computation.1 | async-start | bytes 524288 | tf_op jit(solution)/shard_map/all_to_all | solution.py:431
  57.0 0.4 collective-permute-start.5
  57.5 8.3 %collective-permute-done.5.late_ref = f32[16,512]{1,0:T(8,128)S(1)} collective-permute-done((f32[16,512]{1,0:T(8,128)S(1)}, f32[16,512]{1,0:T(8,128)S(1)}, u32[]{:S(2)}, u32[]{:S(2)}) %collective-permute-start.5) | collective-permute-done | bytes 32800 | tf_op jit(solution)/shard_map/ppermute | solution.py:404
  65.7 4.8 %all-to-all-done.1 = f32[32,16,128]{2,1,0:T(8,128)S(1)} async-done(((f32[32,16,128]{2,1,0:T(8,128)}), f32[32,16,128]{2,1,0:T(8,128)S(1)}, u32[]{:S(2)}, u32[]{:S(2)}) %all-to-all-start.1) | async-done | bytes 262176 | tf_op jit(solution)/shard_map/all_to_all | solution.py:431
  70.6 0.4 drift.1
  71.0 17.7 %all_to_all.22.back_ref = f32[32,16,128]{2,1,0:T(8,128)S(1)} all-to-all(f32[32,16,128]{2,1,0:T(8,128)S(1)} %bitcast.8), channel_id=1, replica_groups=mesh['tm'=32,'slab'=8] {'tm'}, dimensions={0} | all-to-all | bytes 524288 | tf_op jit(solution)/shard_map/all_to_all | solution.py:434
  88.6 1.0 %add_drift.1 = (f32[8,16,512]{2,1,0:T(8,128)}, f32[8,16,512]{2,1,0:T(8,128)}) custom-call(f32[8,16,512]{2,1,0:T(8,128)S(1)} %get-tuple-element.30.ph_ref, f32[32,16,128]{2,1,0:T(8,128)S(1)} %all_to_all.22.back_ref, f32[7,16,512]{2,1,0:T(8,128)S(1)} %get-tuple-element.54.half_ref, f32[16,512]{1,0:T(8,128)S(1)} %collective-permute-done.5.late_ref), custom_call_target="tpu_custom_call" | custom-call | tf_op jit(solution)/shard_map/add_drift/pallas_call | solution.py:392
  (5 shorter events, 0.1 us)
Async XLA Ops:
  2.0 13.7 %collective-permute-start = (f32[104,512]{1,0:T(8,128)S(1)}, f32[104,512]{1,0:T(8,128)S(1)}, u32[]{:S(2)}, u32[]{:S(2)}) collective-permute-start(f32[104,512]{1,0:T(8,128)S(1)} %get-tuple-element.31), channel_id=1, source_target_pairs={{7,0},{0,1},{1,2},{2,3},{3,4},{4,5},{5,6},{6,7},{15,8},{8,9},{9,10... | collective-permute-start | bytes 638984 | tf_op jit(solution)/shard_map/ppermute | solution.py:404
  4.2 17.1 %collective-permute-start.1 = (f32[104,512]{1,0:T(8,128)S(1)}, f32[104,512]{1,0:T(8,128)S(1)}, u32[]{:S(2)}, u32[]{:S(2)}) collective-permute-start(f32[104,512]{1,0:T(8,128)S(1)} %get-tuple-element.32), channel_id=1, source_target_pairs={{1,0},{2,1},{3,2},{4,3},{5,4},{6,5},{7,6},{0,7},{9,8},{10,9},{11,1... | collective-permute-start | bytes 638984 | tf_op jit(solution)/shard_map/ppermute | solution.py:404
  7.3 18.0 %collective-permute-start.2 = (f32[15,16,512]{2,1,0:T(8,128)S(1)}, f32[15,16,512]{2,1,0:T(8,128)S(1)}, u32[]{:S(2)}, u32[]{:S(2)}) collective-permute-start(f32[15,16,512]{2,1,0:T(8,128)S(1)} %pack_ahead.1.ahead), channel_id=1, source_target_pairs={{248,0},{0,8},{8,16},{16,24},{24,32},{32,40},{40,48},{48,56},{56,6... | collective-permute-start | bytes 1474568 | tf_op jit(solution)/shard_map/ppermute | solution.py:404
  10.1 15.1 %collective-permute-start.3 = (f32[40,512]{1,0:T(8,128)S(1)}, f32[40,512]{1,0:T(8,128)S(1)}, u32[]{:S(2)}, u32[]{:S(2)}) collective-permute-start(f32[40,512]{1,0:T(8,128)S(1)} %get-tuple-element.35), channel_id=1, source_target_pairs={{255,0},{248,1},{249,2},{250,3},{251,4},{252,5},{253,6},{254,7},{7... | collective-permute-start | bytes 245768 | tf_op jit(solution)/shard_map/ppermute | solution.py:412
  10.2 5.2 %copy-start.1 = (f32[256]{0:T(256)S(1)}, f32[256]{0:T(256)}, u32[]{:S(2)}) copy-start(f32[256]{0:T(256)} %param.8) | copy-start | bytes 3076
  10.2 15.0 %collective-permute-start.4 = (f32[40,512]{1,0:T(8,128)S(1)}, f32[40,512]{1,0:T(8,128)S(1)}, u32[]{:S(2)}, u32[]{:S(2)}) collective-permute-start(f32[40,512]{1,0:T(8,128)S(1)} %get-tuple-element.36), channel_id=1, source_target_pairs={{249,0},{250,1},{251,2},{252,3},{253,4},{254,5},{255,6},{248,7},{1... | collective-permute-start | bytes 245768 | tf_op jit(solution)/shard_map/ppermute | solution.py:412
  27.0 24.1 %copy-start = (f32[8,16,512]{2,1,0:T(8,128)S(1)}, f32[8,16,512]{2,1,0:T(8,128)}, u32[]{:S(2)}) copy-start(f32[8,16,512]{2,1,0:T(8,128)} %pi_ref.1) | copy-start | bytes 786436
  52.5 18.1 %all-to-all-start.1 = ((f32[32,16,128]{2,1,0:T(8,128)}), f32[32,16,128]{2,1,0:T(8,128)S(1)}, u32[]{:S(2)}, u32[]{:S(2)}) async-start(f32[32,16,128]{2,1,0:T(8,128)} %get-tuple-element.51), calls=%async_computation.1 | async-start | bytes 524288 | tf_op jit(solution)/shard_map/all_to_all | solution.py:431
  57.0 8.7 %collective-permute-start.5 = (f32[16,512]{1,0:T(8,128)S(1)}, f32[16,512]{1,0:T(8,128)S(1)}, u32[]{:S(2)}, u32[]{:S(2)}) collective-permute-start(f32[16,512]{1,0:T(8,128)S(1)} %get-tuple-element.52), channel_id=1, source_target_pairs={{8,0},{16,8},{24,16},{32,24},{40,32},{48,40},{56,48},{64,56},{72,6... | collective-permute-start | bytes 98312 | tf_op jit(solution)/shard_map/ppermute | solution.py:404

commit v4 on v3

--- a/solution.py
+++ b/solution.py
@@ -125,10 +125,16 @@
     )(ahead)
 
 
+def horizontal(v, hh):
+    return v + (hh * pltpu.roll(v, v.shape[1] - 1, 1) + pltpu.roll(hh * v, 1, 1))
+
+
+def vertical(v, gg):
+    return gg * pltpu.roll(v, v.shape[0] - 1, 0) + pltpu.roll(gg * v, 1, 0)
+
+
 def kinetic(v, hh, gg):
-    rows, columns = v.shape
-    beside = hh * pltpu.roll(v, columns - 1, 1) + pltpu.roll(hh * v, 1, 1)
-    return v + (beside + gg * pltpu.roll(v, rows - 1, 0) + pltpu.roll(gg * v, 1, 0))
+    return horizontal(v, hh) + vertical(v, gg)
 
 
 def squares(v):
@@ -144,39 +150,101 @@
     slot[pl.ds(WIDE - n, n)] = above[pl.ds(row, n)]
 
 
+def own_kernel(s_ref, ph_ref, bond_ref, hs_ref, wp_ref, hwp_ref, q_ref, hq_ref, weight):
+    count, slices, rows, _ = s_ref.shape
+    first = lax.axis_index("tm") == 0
+    for t in range(slices):
+        value = jnp.exp(coupling * ph_ref[t])
+        weight[t] = value * jnp.where(first, -1.0, 1.0) if t == 0 else value
+    hh = hopping * bond_ref[0].astype(jnp.float32)
+    gg = hopping * bond_ref[1].astype(jnp.float32)
+    gg = jnp.where(lax.broadcasted_iota(jnp.int32, gg.shape, 0) < rows - 1, gg, 0.0)
+
+    def one_source(i, _):
+        p_old = None
+        for t in range(1, slices):
+            v = s_ref[i, t - 1]
+            along = horizontal(v, hh)
+            hs_ref[i, t - 1] = along
+            p = s_ref[i, t] - weight[t] * (along + vertical(v, gg))
+            v = weight[t] * p
+            along = horizontal(v, hh)
+            wp_ref[i, t - 1] = v
+            hwp_ref[i, t - 1] = along
+            if 2 <= t < slices - 1:
+                q = p_old - (along + vertical(v, gg))
+                q_ref[i, t - 2] = q
+                hq_ref[i, t - 2] = horizontal(q, hh)
+            p_old = p
+        return 0
+
+    lax.fori_loop(0, count, one_source, 0)
+
+
+def own_parts(sources, phonons, bonds):
+    count, slices, rows, columns = sources.shape
+    field = lambda n: jax.ShapeDtypeStruct((count, n, rows, columns), jnp.float32)
+    return pl.pallas_call(
+        own_kernel,
+        out_shape=[field(slices - 1)] * 3
+        + [field(slices - 3)] * 2
+        + [jax.ShapeDtypeStruct(phonons.shape, jnp.float32)],
+        in_specs=[VMEM] * 3,
+        out_specs=[VMEM] * 6,
+        compiler_params=PARAMS,
+        name="own_parts",
+    )(sources, phonons, bonds)
+
+
 def inner_kernel(
-    s_ref, ph_ref, bond_ref, above, below, p_ref, q_ref, t_ref, s_edge, kp_edge, shared, acc, ext, weight
+    s_ref, ph_ref, bond_ref, above, below, hs_ref, wp_own, hwp_ref, q_own, hq_ref, weight_own,
+    p_ref, q_ref, t_ref, s_edge, kp_edge, shared, acc, ext, weight, hh_two, hh_three,
 ):
-    count, slices = s_ref.shape[:2]
+    count, slices, own, columns = s_ref.shape
     side, _ = side_layout(count, slices)
     for k in range(2):
         widen(shared.at[k], bond_ref[k].astype(jnp.float32), below, above, side["bond", k])
         shared[k] = hopping * shared[k]
+    hh_two[...] = shared[0, pl.ds(own, 8)]
+    hh_two[pl.ds(3, 1)] = shared[0, pl.ds(own - 1, 1)]
+    hh_two[pl.ds(4, 1)] = shared[0, pl.ds(0, 1)]
+    hh_three[...] = jnp.zeros_like(hh_three)
+    hh_three[pl.ds(2, 2)] = shared[0, pl.ds(own - 2, 2)]
+    hh_three[pl.ds(4, 2)] = shared[0, pl.ds(0, 2)]
     first = lax.axis_index("tm") == 0
     for t in range(slices):
         slot = weight.at[t]
-        widen(slot, ph_ref[t], below, above, side[count, t])
-        value = jnp.exp(coupling * slot[...])
-        slot[...] = value * jnp.where(first, -1.0, 1.0) if t == 0 else value
+        widen(slot, weight_own[t], below, above, side[count, t])
+        value = jnp.exp(coupling * slot[pl.ds(own, 8)])
+        slot[pl.ds(own, 8)] = value * jnp.where(first, -1.0, 1.0) if t == 0 else value
         for i in range(count):
             widen(ext.at[i, t], s_ref[i, t], below, above, side[i, t])
     for j in range(2):
         shared[2 + j] = weight[j]
 
     def one_source(i, _):
-        moved = lambda v: kinetic(v, shared[0], shared[1])
+        sub = lax.broadcasted_iota(jnp.int32, (8, columns), 0)
+        turn = lambda v: pltpu.roll(v, 4, 0)
+        gg = shared[1]
         sums = [jnp.zeros((8, LANES), jnp.float32)] * 4
-        own = s_ref.shape[2]
         p_old = q_old = None
         s_edge[i] = ext[i, 0]
         for t in range(1, slices):
-            s = ext[i, t]
-            p = s - weight[t] * moved(ext[i, t - 1])
+            s, v = ext[i, t], ext[i, t - 1]
+            along = jnp.concatenate([hs_ref[i, t - 1], horizontal(v[own:], shared[0, pl.ds(own, 8)])], axis=0)
+            p = s - weight[t] * (along + vertical(v, gg))
             if t < slices - 1:
                 p_ref[i, t - 1] = p[:own]
                 sums[0] += squares(s)
                 sums[1] += squares(p)
-            back = moved(weight[t] * p)
+            v = weight[t] * p
+            change = v[:own] - wp_own[i, t - 1]
+            tile = jnp.where(sub == 3, turn(change[8:]), jnp.where(sub == 4, turn(change[:8]), v[own:]))
+            tile = horizontal(tile, hh_two[...])
+            turned, along = turn(tile), hwp_ref[i, t - 1]
+            top = along[:8] + jnp.where(sub == 0, turned, 0.0)
+            bottom = along[8:] + jnp.where(sub == 7, turned, 0.0)
+            back = jnp.concatenate([top, bottom, tile], axis=0) + vertical(v, gg)
             if t == 1:
                 kp_edge[i] = back
             else:
@@ -184,8 +252,14 @@
                 q_ref[i, t - 2] = q[:own]
                 sums[2] += squares(q)
                 if t > 2:
-                    u = q - weight[t - 1] * moved(q_old)
-                    t_ref[i, t - 3] = u[:own]
+                    change = q_old[:own] - q_own[i, t - 3]
+                    tile = jnp.where(sub < 4, turn(change[8:]), turn(change[:8]))
+                    turned, along = turn(horizontal(tile, hh_three[...])), hq_ref[i, t - 3]
+                    top = along[:8] + jnp.where(sub < 2, turned, 0.0)
+                    bottom = along[8:] + jnp.where(sub > 5, turned, 0.0)
+                    moved = jnp.concatenate([top, bottom], axis=0) + vertical(q_old, gg)[:own]
+                    u = q[:own] - weight[t - 1, pl.ds(0, own)] * moved
+                    t_ref[i, t - 3] = u
                     sums[3] += squares(u)
                 q_old = q
             p_old = p
@@ -196,7 +270,7 @@
     lax.fori_loop(0, count, one_source, 0)
 
 
-def inner_operators(sources, phonons, bonds, above, below):
+def inner_operators(sources, phonons, bonds, above, below, parts):
     count, slices, rows, columns = sources.shape
     shape = lambda *n: jax.ShapeDtypeStruct(n, jnp.float32)
     field = lambda times: shape(count, times, rows, columns)
@@ -212,15 +286,17 @@
             wide(4),
             shape(4 * count, 8, LANES),
         ],
-        in_specs=[VMEM] * 5,
+        in_specs=[VMEM] * 11,
         out_specs=[VMEM] * 7,
         scratch_shapes=[
             pltpu.VMEM((count, slices, WIDE, columns), jnp.float32),
             pltpu.VMEM((slices, WIDE, columns), jnp.float32),
+            pltpu.VMEM((8, columns), jnp.float32),
+            pltpu.VMEM((8, columns), jnp.float32),
         ],
         compiler_params=PARAMS,
         name="inner_operators",
-    )(sources, phonons, bonds, above, below)
+    )(sources, phonons, bonds, above, below, *parts)
 
 
 def outer_kernel(
@@ -377,26 +453,41 @@
     return mixed.reshape(columns.shape)
 
 
-def add_kernel(ph_ref, back_ref, half_ref, late_ref, out_ref, all_ref):
+def join_kernel(half_ref, late_ref, all_ref):
+    last = half_ref.shape[0]
+    all_ref[pl.ds(0, last)] = half_ref[...]
+    all_ref[last] = late_ref[...]
+
+
+def join_times(half, late):
+    return pl.pallas_call(
+        join_kernel,
+        out_shape=jax.ShapeDtypeStruct((half.shape[0] + 1,) + half.shape[1:], jnp.float32),
+        in_specs=[VMEM] * 2,
+        out_specs=VMEM,
+        compiler_params=PARAMS,
+        name="join_times",
+    )(half, late)
+
+
+def add_kernel(ph_ref, back_ref, out_ref):
     slices, rows, columns = ph_ref.shape
     for t in range(slices):
-        all_ref[t] = half_ref[t] if t < slices - 1 else late_ref[...]
         for r in range(0, rows, 2):
             for c in range(0, columns, LANES):
                 moved = back_ref[(r // 2) * (columns // LANES) + c // LANES, pl.ds(2 * t, 2)]
                 out_ref[t, pl.ds(r, 2), pl.ds(c, LANES)] = ph_ref[t, pl.ds(r, 2), pl.ds(c, LANES)] + moved
 
 
-def add_drift(phonons, back, half, late):
-    field = jax.ShapeDtypeStruct(phonons.shape, jnp.float32)
+def add_drift(phonons, back):
     return pl.pallas_call(
         add_kernel,
-        out_shape=[field] * 2,
-        in_specs=[VMEM] * 4,
-        out_specs=[VMEM] * 2,
+        out_shape=jax.ShapeDtypeStruct(phonons.shape, jnp.float32),
+        in_specs=[VMEM] * 2,
+        out_specs=VMEM,
         compiler_params=PARAMS,
         name="add_drift",
-    )(phonons, back, half, late)
+    )(phonons, back)
 
 
 def passed_along(block, axis, distance):
@@ -423,17 +514,19 @@
     up_corner, down_corner = pack_corners(ahead)
     above_corner = passed_diagonally(up_corner, 1, 1)
     below_corner = passed_diagonally(down_corner, 1, -1)
-    (above, below), table = lax.optimization_barrier(((above, below), circulant(kernel)))
-    inner = inner_operators(sources, phonons, bonds, above, below)
+    side_halos = (above, below)
+    own = own_parts(sources, phonons, bonds)
+    (above, below), table, own = lax.optimization_barrier((side_halos, circulant(kernel), own))
+    inner = inner_operators(sources, phonons, bonds, above, below, own)
     outer = outer_operators(before, above_corner, below_corner, inner, everyone)
     received = lax.all_to_all(outer[3], ("tm", "slab"), split_axis=0, concat_axis=0, tiled=True)
     half, early, send = force(received, sources, inner, outer, phonons, before, momenta, peers)
     columns = lax.all_to_all(send, "tm", split_axis=0, concat_axis=0, tiled=True)
-    columns, late = lax.optimization_barrier((columns, passed_along(early, "tm", -1)))
+    half_momenta = join_times(half, passed_along(early, "tm", -1))
+    columns, half_momenta = lax.optimization_barrier((columns, half_momenta))
     mixed = drift(table, columns)
     back = lax.all_to_all(mixed, "tm", split_axis=0, concat_axis=0, tiled=True)
-    new_phonons, half_momenta = add_drift(phonons, back, half, late)
-    return half_momenta, new_phonons
+    return half_momenta, add_drift(phonons, back)
 
 
 def solution(mesh):

time: 89.9 us -> 88.2 us (0.981)
  waiting for transfers between devices: 18.7 us -> 14.5 us
  Pallas kernels: 10.8 us -> 13.3 us
    pallas_call x1 -> x3, Pallas kernels: 0.96 us -> 5.09 us  [the longest x1 3.51 us: own_parts(): pl.pallas_call(own_kernel, out_shape=[field(slices - 1)] * 3 + [field(sli...]
    ppermute x4, waiting for transfers between devices: 13.9 us -> 10.4 us  [passed_along(): lax.ppermute(block, axis, [((i - distance) % count, i) for i in range(cou...]
    pallas_call x1, Pallas kernels: 3.94 us -> 2.3 us  [inner_operators(): pl.pallas_call(inner_kernel, out_shape=[field(slices - 2), field(slices -...]
  transfers between devices with their start and end apart: 7 -> 7, of which waited for: 3 -> 3; matrix products, arithmetic and copies ran while one was open for 0% -> 0% of each run, Pallas kernels for 6% -> 9%
where the time goes in v4:
time: 88.2 us; the launch traced here: 87.8 us
  blocking collectives  41.8 us (47%)
  starting transfers between devices  17.6 us (20%)
  waiting for transfers between devices  14.5 us (16%)
  Pallas kernels  13.3 us (15%)
    all_to_all x1, blocking collectives, body(): lax.all_to_all(outer[3], ('tm', 'slab'), split_axis=0, concat_axis=0, til...  24.1 us
    all_to_all x1, blocking collectives, body(): back = lax.all_to_all(mixed, 'tm', split_axis=0, concat_axis=0, tiled=True)  17.7 us
    ppermute x4, waiting for transfers between devices, passed_along(): lax.ppermute(block, axis, [((i - distance) % count, i) for i in range(cou...  10.4 us
    ppermute x4, starting transfers between devices, passed_along(): lax.ppermute(block, axis, [((i - distance) % count, i) for i in range(cou...  7.74 us
    ppermute x2, starting transfers between devices, passed_diagonally(): return lax.ppermute(block, ('tm', 'slab'), route)  5.27 us
    all_to_all x1, starting transfers between devices, body(): lax.all_to_all(send, 'tm', split_axis=0, concat_axis=0, tiled=True)  4.55 us
    all_to_all x1, waiting for transfers between devices, body(): lax.all_to_all(send, 'tm', split_axis=0, concat_axis=0, tiled=True)  4.12 us
    pallas_call x1, Pallas kernels, own_parts(): pl.pallas_call(own_kernel, out_shape=[field(slices - 1)] * 3 + [field(sli...  3.51 us
  transfers between devices with their start and end apart: 7, of which 3 were waited for; matrix products, arithmetic and copies ran while one was open for 0% of the time, Pallas kernels for 9%

profile of v4, /device:TPU:1, one launch (start us, length us, event | category | flops | bytes accessed | tf_op | source)
XLA Modules:
  0.0 87.8 jit_solution(9781729231366380561)
XLA Ops:
  0.6 1.4 %pack_sides.1 = (f32[104,512]{1,0:T(8,128)S(1)}, f32[104,512]{1,0:T(8,128)S(1)}, f32[4,8,16,512]{3,2,1,0:T(8,128)S(1)}, f32[8,16,512]{2,1,0:T(8,128)S(1)}, s32[2,16,512]{2,1,0:T(8,128)S(1)}) custom-call(f32[4,8,16,512]{3,2,1,0:T(8,128)} %s_hbm.1, f32[8,16,512]{2,1,0:T(8,128)} %ph_hbm.1, s32[2,16,512]{2,1,0:T(8,128)} %bond_hbm.1), custom_call_target="tpu_custom_call" | custom-call | tf_op jit(solution)/shard_map/pack_sides/pallas_call | solution.py:71
  2.0 2.2 %collective-permute-start.3 = (f32[104,512]{1,0:T(8,128)S(1)}, f32[104,512]{1,0:T(8,128)S(1)}, u32[]{:S(2)}, u32[]{:S(2)}) collective-permute-start(f32[104,512]{1,0:T(8,128)S(1)} %get-tuple-element.45), channel_id=1, source_target_pairs={{7,0},{0,1},{1,2},{2,3},{3,4},{4,5},{5,6},{6,7},{15,8},{8,9},{9,10... | collective-permute-start | bytes 638984 | tf_op jit(solution)/shard_map/ppermute | solution.py:495
  4.2 2.3 %collective-permute-start.4 = (f32[104,512]{1,0:T(8,128)S(1)}, f32[104,512]{1,0:T(8,128)S(1)}, u32[]{:S(2)}, u32[]{:S(2)}) collective-permute-start(f32[104,512]{1,0:T(8,128)S(1)} %get-tuple-element.46), channel_id=1, source_target_pairs={{1,0},{2,1},{3,2},{4,3},{5,4},{6,5},{7,6},{0,7},{9,8},{10,9},{11,1... | collective-permute-start | bytes 638984 | tf_op jit(solution)/shard_map/ppermute | solution.py:495
  6.5 0.8 pack_ahead.1.ahead
  7.3 2.8 %collective-permute-start = (f32[15,16,512]{2,1,0:T(8,128)S(1)}, f32[15,16,512]{2,1,0:T(8,128)S(1)}, u32[]{:S(2)}, u32[]{:S(2)}) collective-permute-start(f32[15,16,512]{2,1,0:T(8,128)S(1)} %pack_ahead.1.ahead), channel_id=1, source_target_pairs={{248,0},{0,8},{8,16},{16,24},{24,32},{32,40},{40,48},{48,56},{56,6... | collective-permute-start | bytes 1474568 | tf_op jit(solution)/shard_map/ppermute | solution.py:495
  10.1 0.1 collective-permute-start.1
  10.2 0.0 copy-start.1
  10.2 5.2 %collective-permute-start.2 = (f32[40,512]{1,0:T(8,128)S(1)}, f32[40,512]{1,0:T(8,128)S(1)}, u32[]{:S(2)}, u32[]{:S(2)}) collective-permute-start(f32[40,512]{1,0:T(8,128)S(1)} %get-tuple-element.43), channel_id=1, source_target_pairs={{249,0},{250,1},{251,2},{252,3},{253,4},{254,5},{255,6},{248,7},{1... | collective-permute-start | bytes 245768 | tf_op jit(solution)/shard_map/ppermute | solution.py:503
  15.4 0.2 circulant.1.table_ref
  15.7 3.5 %own_parts.1 = (f32[4,7,16,512]{3,2,1,0:T(8,128)S(1)}, f32[4,7,16,512]{3,2,1,0:T(8,128)S(1)}, f32[4,7,16,512]{3,2,1,0:T(8,128)S(1)}, f32[4,5,16,512]{3,2,1,0:T(8...) custom-call(f32[4,8,16,512]{3,2,1,0:T(8,128)S(1)} %get-tuple-element.40.s_ref, ...), custom_call_target="tpu_custom_call" | custom-call | tf_op jit(solution)/shard_map/own_parts/pallas_call | solution.py:187
  19.2 2.1 %collective-permute-done.4.below = f32[104,512]{1,0:T(8,128)S(1)} collective-permute-done((f32[104,512]{1,0:T(8,128)S(1)}, f32[104,512]{1,0:T(8,128)S(1)}, u32[]{:S(2)}, u32[]{:S(2)}) %collective-permute-start.4) | collective-permute-done | bytes 213024 | tf_op jit(solution)/shard_map/ppermute | solution.py:495
  21.3 2.3 %inner_operators.1 = (f32[4,6,16,512]{3,2,1,0:T(8,128)S(1)}, f32[4,6,16,512]{3,2,1,0:T(8,128)S(1)}, f32[4,5,16,512]{3,2,1,0:T(8,128)S(1)}, f32[4,24,512]{2,1,0:T...) custom-call(f32[4,8,16,512]{3,2,1,0:T(8,128)S(1)} %get-tuple-element.40.s_ref, ...), custom_call_target="tpu_custom_call" | custom-call | tf_op jit(solution)/shard_map/inner_operators/pallas_call | solution.py:278
  23.6 1.7 %outer_operators.1 = (f32[4,2,16,512]{3,2,1,0:T(8,128)S(1)}, f32[4,2,16,512]{3,2,1,0:T(8,128)S(1)}, f32[4,3,16,512]{3,2,1,0:T(8,128)S(1)}, f32[256,128]{1,0:T(8,128)S(1)}) custom-call(f32[15,16,512]{2,1,0:T(8,128)S(1)} %collective-permute-done.before, f32[40,512]{1,0:T(8,128)S(1)} %collective-permute-done.1.above, ...), custom_call_target="tpu_custom_call" | custom-call | tf_op jit(solution)/shard_map/outer_operators/pallas_call | solution.py:344
  25.4 0.0 copy-start
  25.4 24.1 %all_to_all.21 = f32[256,1,128]{2,1,0:T(1,128)S(1)} all-to-all(f32[256,1,128]{2,1,0:T(1,128)S(1)} %bitcast.10), channel_id=1, replica_groups=mesh['tm'=32,'slab'=8] {'tm','slab'}, dimensions={0} | all-to-all | bytes 262144 | tf_op jit(solution)/shard_map/all_to_all | solution.py:522
  49.5 1.4 %force.1 = (f32[7,16,512]{2,1,0:T(8,128)S(1)}, f32[16,512]{1,0:T(8,128)S(1)}, f32[32,16,128]{2,1,0:T(8,128)}) custom-call(f32[256,128]{1,0:T(8,128)S(1)} %bitcast.9, f32[4,8,16,512]{3,2,1,0:T(8,128)S(1)} %get-tuple-element.40.s_ref, f32[4,6,16,512]{3,2,1,0:T(8,128)S(1)} %get-tuple-element.67.p_in, f32[4,6,16,512]{3,2,1,0:T(8,128)S(1)} %get-tuple-element.61.q_inner.q_in, ...), custom_call_target="tpu_custom_call" | custom-call | tf_op jit(solution)/shard_map/force/pallas_call | solution.py:403
  50.8 4.6 %all-to-all-start.1 = ((f32[32,16,128]{2,1,0:T(8,128)}), f32[32,16,128]{2,1,0:T(8,128)S(1)}, u32[]{:S(2)}, u32[]{:S(2)}) async-start(f32[32,16,128]{2,1,0:T(8,128)} %get-tuple-element.72), calls=%async_computation.1 | async-start | bytes 524288 | tf_op jit(solution)/shard_map/all_to_all | solution.py:524
  55.4 0.4 collective-permute-start.5
  55.8 8.3 %collective-permute-done.5.late_ref = f32[16,512]{1,0:T(8,128)S(1)} collective-permute-done((f32[16,512]{1,0:T(8,128)S(1)}, f32[16,512]{1,0:T(8,128)S(1)}, u32[]{:S(2)}, u32[]{:S(2)}) %collective-permute-start.5) | collective-permute-done | bytes 32800 | tf_op jit(solution)/shard_map/ppermute | solution.py:495
  64.1 0.7 join_times.1
  64.8 4.1 %all-to-all-done.1 = f32[32,16,128]{2,1,0:T(8,128)S(1)} async-done(((f32[32,16,128]{2,1,0:T(8,128)}), f32[32,16,128]{2,1,0:T(8,128)S(1)}, u32[]{:S(2)}, u32[]{:S(2)}) %all-to-all-start.1) | async-done | bytes 262176 | tf_op jit(solution)/shard_map/all_to_all | solution.py:524
  68.9 0.4 drift.1
  69.3 17.7 %all_to_all.22.back_ref = f32[32,16,128]{2,1,0:T(8,128)S(1)} all-to-all(f32[32,16,128]{2,1,0:T(8,128)S(1)} %bitcast.8), channel_id=1, replica_groups=mesh['tm'=32,'slab'=8] {'tm'}, dimensions={0} | all-to-all | bytes 524288 | tf_op jit(solution)/shard_map/all_to_all | solution.py:528
  87.0 0.9 add_drift.1
  (7 shorter events, 0.1 us)
Async XLA Ops:
  2.0 17.2 %collective-permute-start.3 = (f32[104,512]{1,0:T(8,128)S(1)}, f32[104,512]{1,0:T(8,128)S(1)}, u32[]{:S(2)}, u32[]{:S(2)}) collective-permute-start(f32[104,512]{1,0:T(8,128)S(1)} %get-tuple-element.45), channel_id=1, source_target_pairs={{7,0},{0,1},{1,2},{2,3},{3,4},{4,5},{5,6},{6,7},{15,8},{8,9},{9,10... | collective-permute-start | bytes 638984 | tf_op jit(solution)/shard_map/ppermute | solution.py:495
  4.2 17.1 %collective-permute-start.4 = (f32[104,512]{1,0:T(8,128)S(1)}, f32[104,512]{1,0:T(8,128)S(1)}, u32[]{:S(2)}, u32[]{:S(2)}) collective-permute-start(f32[104,512]{1,0:T(8,128)S(1)} %get-tuple-element.46), channel_id=1, source_target_pairs={{1,0},{2,1},{3,2},{4,3},{5,4},{6,5},{7,6},{0,7},{9,8},{10,9},{11,1... | collective-permute-start | bytes 638984 | tf_op jit(solution)/shard_map/ppermute | solution.py:495
  7.3 16.4 %collective-permute-start = (f32[15,16,512]{2,1,0:T(8,128)S(1)}, f32[15,16,512]{2,1,0:T(8,128)S(1)}, u32[]{:S(2)}, u32[]{:S(2)}) collective-permute-start(f32[15,16,512]{2,1,0:T(8,128)S(1)} %pack_ahead.1.ahead), channel_id=1, source_target_pairs={{248,0},{0,8},{8,16},{16,24},{24,32},{32,40},{40,48},{48,56},{56,6... | collective-permute-start | bytes 1474568 | tf_op jit(solution)/shard_map/ppermute | solution.py:495
  10.1 13.5 %collective-permute-start.1 = (f32[40,512]{1,0:T(8,128)S(1)}, f32[40,512]{1,0:T(8,128)S(1)}, u32[]{:S(2)}, u32[]{:S(2)}) collective-permute-start(f32[40,512]{1,0:T(8,128)S(1)} %get-tuple-element.42), channel_id=1, source_target_pairs={{255,0},{248,1},{249,2},{250,3},{251,4},{252,5},{253,6},{254,7},{7... | collective-permute-start | bytes 245768 | tf_op jit(solution)/shard_map/ppermute | solution.py:503
  10.2 5.2 %copy-start.1 = (f32[256]{0:T(256)S(1)}, f32[256]{0:T(256)}, u32[]{:S(2)}) copy-start(f32[256]{0:T(256)} %param.8) | copy-start | bytes 3076
  10.2 13.4 %collective-permute-start.2 = (f32[40,512]{1,0:T(8,128)S(1)}, f32[40,512]{1,0:T(8,128)S(1)}, u32[]{:S(2)}, u32[]{:S(2)}) collective-permute-start(f32[40,512]{1,0:T(8,128)S(1)} %get-tuple-element.43), channel_id=1, source_target_pairs={{249,0},{250,1},{251,2},{252,3},{253,4},{254,5},{255,6},{248,7},{1... | collective-permute-start | bytes 245768 | tf_op jit(solution)/shard_map/ppermute | solution.py:503
  25.4 24.1 %copy-start = (f32[8,16,512]{2,1,0:T(8,128)S(1)}, f32[8,16,512]{2,1,0:T(8,128)}, u32[]{:S(2)}) copy-start(f32[8,16,512]{2,1,0:T(8,128)} %pi_ref.1) | copy-start | bytes 786436
  50.8 18.1 %all-to-all-start.1 = ((f32[32,16,128]{2,1,0:T(8,128)}), f32[32,16,128]{2,1,0:T(8,128)S(1)}, u32[]{:S(2)}, u32[]{:S(2)}) async-start(f32[32,16,128]{2,1,0:T(8,128)} %get-tuple-element.72), calls=%async_computation.1 | async-start | bytes 524288 | tf_op jit(solution)/shard_map/all_to_all | solution.py:524
  55.4 8.7 %collective-permute-start.5 = (f32[16,512]{1,0:T(8,128)S(1)}, f32[16,512]{1,0:T(8,128)S(1)}, u32[]{:S(2)}, u32[]{:S(2)}) collective-permute-start(f32[16,512]{1,0:T(8,128)S(1)} %get-tuple-element.74), channel_id=1, source_target_pairs={{8,0},{16,8},{24,16},{32,24},{40,32},{48,40},{56,48},{64,56},{72,6... | collective-permute-start | bytes 98312 | tf_op jit(solution)/shard_map/ppermute | solution.py:495

commit v5 on v4

--- a/solution.py
+++ b/solution.py
@@ -42,11 +42,12 @@
     return ref[pl.ds(ref.shape[0] - n if last else 0, n)]
 
 
-def side_kernel(s_hbm, ph_hbm, bond_hbm, up, down, s_ref, ph_ref, bond_ref, sems):
+def side_kernel(s_hbm, ph_hbm, bond_hbm, pi_hbm, up, down, s_ref, ph_ref, bond_ref, pi_ref, sems):
     count, slices = s_ref.shape[:2]
     copies = [pltpu.make_async_copy(s_hbm.at[i], s_ref.at[i], sems.at[i]) for i in range(count)]
     copies.append(pltpu.make_async_copy(ph_hbm, ph_ref, sems.at[count]))
     copies.append(pltpu.make_async_copy(bond_hbm, bond_ref, sems.at[count + 1]))
+    copies.append(pltpu.make_async_copy(pi_hbm.at[slices - 1], pi_ref, sems.at[count + 2]))
     for copy in copies:
         copy.start()
     side, _ = side_layout(count, slices)
@@ -62,46 +63,45 @@
         row, n = side["bond", k]
         up[pl.ds(row, n)] = rows_of(bond_ref.at[k], n, True).astype(jnp.float32)
         down[pl.ds(row, n)] = rows_of(bond_ref.at[k], n, False).astype(jnp.float32)
-
-
-def pack_sides(sources, phonons, bonds):
+    copies[count + 2].wait()
+
+
+def pack_sides(sources, phonons, bonds, momenta):
     count, slices, rows, columns = sources.shape
     side = jax.ShapeDtypeStruct((side_layout(count, slices)[1], columns), jnp.float32)
     whole = [jax.ShapeDtypeStruct(x.shape, x.dtype) for x in (sources, phonons, bonds)]
+    whole.append(jax.ShapeDtypeStruct(momenta.shape[1:], jnp.float32))
     return pl.pallas_call(
         side_kernel,
         out_shape=[side, side, *whole],
-        in_specs=[pl.BlockSpec(memory_space=pltpu.HBM)] * 3,
-        out_specs=[VMEM] * 5,
-        scratch_shapes=[pltpu.SemaphoreType.DMA((count + 2,))],
+        in_specs=[pl.BlockSpec(memory_space=pltpu.HBM)] * 4,
+        out_specs=[VMEM] * 6,
+        scratch_shapes=[pltpu.SemaphoreType.DMA((count + 3,))],
         compiler_params=PARAMS,
         name="pack_sides",
-    )(*(pltpu.with_memory_space_constraint(x, pltpu.HBM) for x in (sources, phonons, bonds)))
-
-
-def ahead_kernel(s_ref, ph_ref, pi_hbm, ahead, sem):
+    )(*(pltpu.with_memory_space_constraint(x, pltpu.HBM) for x in (sources, phonons, bonds, momenta)))
+
+
+def ahead_kernel(s_ref, ph_ref, pi_ref, ahead):
     count, slices = s_ref.shape[:2]
-    last = pltpu.make_async_copy(pi_hbm.at[slices - 1], ahead.at[EARLY * count + 2], sem)
-    last.start()
     for i in range(count):
         for j in range(EARLY):
             ahead[EARLY * i + j] = s_ref[i, slices - EARLY + j]
     for j in range(2):
         ahead[EARLY * count + j] = ph_ref[slices - 2 + j]
-    last.wait()
-
-
-def pack_ahead(sources, phonons, momenta):
+    ahead[EARLY * count + 2] = pi_ref[...]
+
+
+def pack_ahead(sources, phonons, last_momenta):
     count, _, rows, columns = sources.shape
     return pl.pallas_call(
         ahead_kernel,
         out_shape=jax.ShapeDtypeStruct((EARLY * count + 3, rows, columns), jnp.float32),
-        in_specs=[VMEM, VMEM, pl.BlockSpec(memory_space=pltpu.HBM)],
+        in_specs=[VMEM] * 3,
         out_specs=VMEM,
-        scratch_shapes=[pltpu.SemaphoreType.DMA(())],
         compiler_params=PARAMS,
         name="pack_ahead",
-    )(sources, phonons, pltpu.with_memory_space_constraint(momenta, pltpu.HBM))
+    )(sources, phonons, last_momenta)
 
 
 def corner_kernel(ahead, up, down):
@@ -357,7 +357,8 @@
 
 
 def force_kernel(
-    mom_ref, s_ref, p_in, q_in, t_in, p_out, q_out, t_out, ph_ref, before, pi_ref, half_ref, early_ref, send_ref
+    mom_ref, s_ref, p_in, q_in, t_in, p_out, q_out, t_out, ph_ref, before, pi_ref, half_ref, early_ref, send_hbm,
+    send_ref, sems,
 ):
     count, slices, rows, columns = s_ref.shape
     moments = jnp.sum(mom_ref[...], axis=0, keepdims=True)
@@ -373,6 +374,7 @@
     high = [at((1.0 - alpha * square) / spread, i) for i in range(count)]
     kept = EARLY * count
     phonon = lambda t: before[kept + 2 + t] if t < 0 else ph_ref[t]
+    copies = []
     for t in range(-1, slices - 1):
         fermion = None
         for i in range(count):
@@ -395,6 +397,13 @@
                 send_ref[(r // 2) * (columns // LANES) + c // LANES, pl.ds(2 * (t + 1), 2)] = half[
                     r : r + 2, c : c + LANES
                 ]
+        if t % 4 == 2:
+            tile = pl.ds(8 * (t // 4), 8)
+            copy = pltpu.make_async_copy(send_ref.at[:, tile], send_hbm.at[:, tile], sems.at[t // 4])
+            copy.start()
+            copies.append(copy)
+    for copy in copies:
+        copy.wait()
 
 
 def force(received, sources, inner, outer, phonons, before, momenta, peers):
@@ -404,7 +413,11 @@
         force_kernel,
         out_shape=[shape(slices - 1, rows, columns), shape(rows, columns), shape(peers, 2 * slices, LANES)],
         in_specs=[VMEM] * 11,
-        out_specs=[VMEM] * 3,
+        out_specs=[VMEM, VMEM, pl.BlockSpec(memory_space=pltpu.HBM)],
+        scratch_shapes=[
+            pltpu.VMEM((peers, 2 * slices, LANES), jnp.float32),
+            pltpu.SemaphoreType.DMA((slices // 4,)),
+        ],
         compiler_params=PARAMS,
         name="force",
     )(received, sources, *inner[:3], *outer[:3], phonons, before, momenta)
@@ -470,13 +483,18 @@
     )(half, late)
 
 
-def add_kernel(ph_ref, back_ref, out_ref):
+def add_kernel(ph_ref, back_ref, out_hbm, out_ref, sems):
     slices, rows, columns = ph_ref.shape
+    copies = []
     for t in range(slices):
         for r in range(0, rows, 2):
             for c in range(0, columns, LANES):
                 moved = back_ref[(r // 2) * (columns // LANES) + c // LANES, pl.ds(2 * t, 2)]
                 out_ref[t, pl.ds(r, 2), pl.ds(c, LANES)] = ph_ref[t, pl.ds(r, 2), pl.ds(c, LANES)] + moved
+        copies.append(pltpu.make_async_copy(out_ref.at[t], out_hbm.at[t], sems.at[t]))
+        copies[t].start()
+    for copy in copies:
+        copy.wait()
 
 
 def add_drift(phonons, back):
@@ -484,7 +502,11 @@
         add_kernel,
         out_shape=jax.ShapeDtypeStruct(phonons.shape, jnp.float32),
         in_specs=[VMEM] * 2,
-        out_specs=VMEM,
+        out_specs=pl.BlockSpec(memory_space=pltpu.HBM),
+        scratch_shapes=[
+            pltpu.VMEM(phonons.shape, jnp.float32),
+            pltpu.SemaphoreType.DMA((phonons.shape[0],)),
+        ],
         compiler_params=PARAMS,
         name="add_drift",
     )(phonons, back)
@@ -506,10 +528,10 @@
 def body(sources, phonons, momenta, kernel, bonds):
     peers = lax.axis_size("tm")
     everyone = peers * lax.axis_size("slab")
-    up, down, sources, phonons, bonds = pack_sides(sources, phonons, bonds)
+    up, down, sources, phonons, bonds, last_momenta = pack_sides(sources, phonons, bonds, momenta)
     above = passed_along(up, "slab", 1)
     below = passed_along(down, "slab", -1)
-    ahead = pack_ahead(sources, phonons, momenta)
+    ahead = pack_ahead(sources, phonons, last_momenta)
     before = passed_along(ahead, "tm", 1)
     up_corner, down_corner = pack_corners(ahead)
     above_corner = passed_diagonally(up_corner, 1, 1)

time: 88.2 us -> 88.1 us (level)
  transfers between devices with their start and end apart: 7 -> 7, of which waited for: 3 -> 3; matrix products, arithmetic and copies ran while one was open for 0% -> 0% of each run, Pallas kernels for 9% -> 8%
where the time goes in v5:
time: 88.1 us; the launch traced here: 87.8 us
  blocking collectives  41.8 us (47%)
  starting transfers between devices  17.6 us (20%)
  waiting for transfers between devices  15.2 us (17%)
  Pallas kernels  12.5 us (14%)
    all_to_all x1, blocking collectives, body(): lax.all_to_all(outer[3], ('tm', 'slab'), split_axis=0, concat_axis=0, til...  24.1 us
    all_to_all x1, blocking collectives, body(): back = lax.all_to_all(mixed, 'tm', split_axis=0, concat_axis=0, tiled=True)  17.7 us
    ppermute x4, waiting for transfers between devices, passed_along(): lax.ppermute(block, axis, [((i - distance) % count, i) for i in range(cou...  11.1 us
    ppermute x4, starting transfers between devices, passed_along(): lax.ppermute(block, axis, [((i - distance) % count, i) for i in range(cou...  7.74 us
    ppermute x2, starting transfers between devices, passed_diagonally(): return lax.ppermute(block, ('tm', 'slab'), route)  5.27 us
    all_to_all x1, starting transfers between devices, body(): lax.all_to_all(send, 'tm', split_axis=0, concat_axis=0, tiled=True)  4.56 us
    all_to_all x1, waiting for transfers between devices, body(): lax.all_to_all(send, 'tm', split_axis=0, concat_axis=0, tiled=True)  4.12 us
    pallas_call x1, Pallas kernels, own_parts(): pl.pallas_call(own_kernel, out_shape=[field(slices - 1)] * 3 + [field(sli...  3.51 us
  transfers between devices with their start and end apart: 7, of which 3 were waited for; matrix products, arithmetic and copies ran while one was open for 0% of the time, Pallas kernels for 8%

profile of v5, /device:TPU:1, one launch (start us, length us, event | category | flops | bytes accessed | tf_op | source)
XLA Modules:
  0.0 87.8 jit_solution(4938118975021984645)
XLA Ops:
  0.6 1.4 %pack_sides.1 = (f32[104,512]{1,0:T(8,128)S(1)}, f32[104,512]{1,0:T(8,128)S(1)}, f32[4,8,16,512]{3,2,1,0:T(8,128)S(1)}, f32[8,16,512]{2,1,0:T(8,128)S(1)}, s32[2...) custom-call(f32[4,8,16,512]{3,2,1,0:T(8,128)} %s_hbm.1, f32[8,16,512]{2,1,0:T(8,128)} %ph_hbm.1, s32[2,16,512]{2,1,0:T(8,128)} %bond_hbm.1, ...), custom_call_target="tpu_custom_call" | custom-call | tf_op jit(solution)/shard_map/pack_sides/pallas_call | solution.py:74
  2.0 2.2 %collective-permute-start.3 = (f32[104,512]{1,0:T(8,128)S(1)}, f32[104,512]{1,0:T(8,128)S(1)}, u32[]{:S(2)}, u32[]{:S(2)}) collective-permute-start(f32[104,512]{1,0:T(8,128)S(1)} %get-tuple-element.47), channel_id=1, source_target_pairs={{7,0},{0,1},{1,2},{2,3},{3,4},{4,5},{5,6},{6,7},{15,8},{8,9},{9,10... | collective-permute-start | bytes 638984 | tf_op jit(solution)/shard_map/ppermute | solution.py:517
  4.2 2.3 %collective-permute-start.4 = (f32[104,512]{1,0:T(8,128)S(1)}, f32[104,512]{1,0:T(8,128)S(1)}, u32[]{:S(2)}, u32[]{:S(2)}) collective-permute-start(f32[104,512]{1,0:T(8,128)S(1)} %get-tuple-element.48), channel_id=1, source_target_pairs={{1,0},{2,1},{3,2},{4,3},{5,4},{6,5},{7,6},{0,7},{9,8},{10,9},{11,1... | collective-permute-start | bytes 638984 | tf_op jit(solution)/shard_map/ppermute | solution.py:517
  6.5 2.8 %collective-permute-start = (f32[15,16,512]{2,1,0:T(8,128)S(1)}, f32[15,16,512]{2,1,0:T(8,128)S(1)}, u32[]{:S(2)}, u32[]{:S(2)}) collective-permute-start(f32[15,16,512]{2,1,0:T(8,128)S(1)} %pack_ahead.1.ahead), channel_id=1, source_target_pairs={{248,0},{0,8},{8,16},{16,24},{24,32},{32,40},{40,48},{48,56},{56,6... | collective-permute-start | bytes 1474568 | tf_op jit(solution)/shard_map/ppermute | solution.py:517
  9.4 0.1 collective-permute-start.1
  9.5 0.0 copy-start.1
  9.5 5.2 %collective-permute-start.2 = (f32[40,512]{1,0:T(8,128)S(1)}, f32[40,512]{1,0:T(8,128)S(1)}, u32[]{:S(2)}, u32[]{:S(2)}) collective-permute-start(f32[40,512]{1,0:T(8,128)S(1)} %get-tuple-element.45), channel_id=1, source_target_pairs={{249,0},{250,1},{251,2},{252,3},{253,4},{254,5},{255,6},{248,7},{1... | collective-permute-start | bytes 245768 | tf_op jit(solution)/shard_map/ppermute | solution.py:525
  14.7 0.2 circulant.1.table_ref
  14.9 3.5 %own_parts.1 = (f32[4,7,16,512]{3,2,1,0:T(8,128)S(1)}, f32[4,7,16,512]{3,2,1,0:T(8,128)S(1)}, f32[4,7,16,512]{3,2,1,0:T(8,128)S(1)}, f32[4,5,16,512]{3,2,1,0:T(8...) custom-call(f32[4,8,16,512]{3,2,1,0:T(8,128)S(1)} %get-tuple-element.41.s_ref, ...), custom_call_target="tpu_custom_call" | custom-call | tf_op jit(solution)/shard_map/own_parts/pallas_call | solution.py:187
  18.5 2.8 %collective-permute-done.4.below = f32[104,512]{1,0:T(8,128)S(1)} collective-permute-done((f32[104,512]{1,0:T(8,128)S(1)}, f32[104,512]{1,0:T(8,128)S(1)}, u32[]{:S(2)}, u32[]{:S(2)}) %collective-permute-start.4) | collective-permute-done | bytes 213024 | tf_op jit(solution)/shard_map/ppermute | solution.py:517
  21.3 2.3 %inner_operators.1 = (f32[4,6,16,512]{3,2,1,0:T(8,128)S(1)}, f32[4,6,16,512]{3,2,1,0:T(8,128)S(1)}, f32[4,5,16,512]{3,2,1,0:T(8,128)S(1)}, f32[4,24,512]{2,1,0:T...) custom-call(f32[4,8,16,512]{3,2,1,0:T(8,128)S(1)} %get-tuple-element.41.s_ref, ...), custom_call_target="tpu_custom_call" | custom-call | tf_op jit(solution)/shard_map/inner_operators/pallas_call | solution.py:278
  23.6 0.0 collective-permute-done.1.above
  23.6 1.7 %outer_operators.1 = (f32[4,2,16,512]{3,2,1,0:T(8,128)S(1)}, f32[4,2,16,512]{3,2,1,0:T(8,128)S(1)}, f32[4,3,16,512]{3,2,1,0:T(8,128)S(1)}, f32[256,128]{1,0:T(8,128)S(1)}) custom-call(f32[15,16,512]{2,1,0:T(8,128)S(1)} %collective-permute-done.before, f32[40,512]{1,0:T(8,128)S(1)} %collective-permute-done.1.above, ...), custom_call_target="tpu_custom_call" | custom-call | tf_op jit(solution)/shard_map/outer_operators/pallas_call | solution.py:344
  25.4 0.0 copy-start
  25.4 24.1 %all_to_all.21 = f32[256,1,128]{2,1,0:T(1,128)S(1)} all-to-all(f32[256,1,128]{2,1,0:T(1,128)S(1)} %bitcast.10), channel_id=1, replica_groups=mesh['tm'=32,'slab'=8] {'tm','slab'}, dimensions={0} | all-to-all | bytes 262144 | tf_op jit(solution)/shard_map/all_to_all | solution.py:544
  49.5 1.3 %force.1 = (f32[7,16,512]{2,1,0:T(8,128)S(1)}, f32[16,512]{1,0:T(8,128)S(1)}, f32[32,16,128]{2,1,0:T(8,128)}) custom-call(f32[256,128]{1,0:T(8,128)S(1)} %bitcast.9, f32[4,8,16,512]{3,2,1,0:T(8,128)S(1)} %get-tuple-element.41.s_ref, f32[4,6,16,512]{3,2,1,0:T(8,128)S(1)} %get-tuple-element.69.p_in, f32[4,6,16,512]{3,2,1,0:T(8,128)S(1)} %get-tuple-element.63.q_inner.q_in, ...), custom_call_target="tpu_custom_call" | custom-call | tf_op jit(solution)/shard_map/force/pallas_call | solution.py:412
  50.8 4.6 %all-to-all-start.1 = ((f32[32,16,128]{2,1,0:T(8,128)}), f32[32,16,128]{2,1,0:T(8,128)S(1)}, u32[]{:S(2)}, u32[]{:S(2)}) async-start(f32[32,16,128]{2,1,0:T(8,128)} %get-tuple-element.74), calls=%async_computation.1 | async-start | bytes 524288 | tf_op jit(solution)/shard_map/all_to_all | solution.py:546
  55.4 0.4 collective-permute-start.5
  55.8 8.3 %collective-permute-done.5.late_ref = f32[16,512]{1,0:T(8,128)S(1)} collective-permute-done((f32[16,512]{1,0:T(8,128)S(1)}, f32[16,512]{1,0:T(8,128)S(1)}, u32[]{:S(2)}, u32[]{:S(2)}) %collective-permute-start.5) | collective-permute-done | bytes 32800 | tf_op jit(solution)/shard_map/ppermute | solution.py:517
  64.1 0.7 join_times.1
  64.8 4.1 %all-to-all-done.1 = f32[32,16,128]{2,1,0:T(8,128)S(1)} async-done(((f32[32,16,128]{2,1,0:T(8,128)}), f32[32,16,128]{2,1,0:T(8,128)S(1)}, u32[]{:S(2)}, u32[]{:S(2)}) %all-to-all-start.1) | async-done | bytes 262176 | tf_op jit(solution)/shard_map/all_to_all | solution.py:546
  68.9 0.4 drift.1
  69.3 17.7 %all_to_all.22.back_ref = f32[32,16,128]{2,1,0:T(8,128)S(1)} all-to-all(f32[32,16,128]{2,1,0:T(8,128)S(1)} %bitcast.8), channel_id=1, replica_groups=mesh['tm'=32,'slab'=8] {'tm'}, dimensions={0} | all-to-all | bytes 524288 | tf_op jit(solution)/shard_map/all_to_all | solution.py:550
  87.0 0.9 add_drift.1
  (7 shorter events, 0.1 us)
Async XLA Ops:
  2.0 16.5 %collective-permute-start.3 = (f32[104,512]{1,0:T(8,128)S(1)}, f32[104,512]{1,0:T(8,128)S(1)}, u32[]{:S(2)}, u32[]{:S(2)}) collective-permute-start(f32[104,512]{1,0:T(8,128)S(1)} %get-tuple-element.47), channel_id=1, source_target_pairs={{7,0},{0,1},{1,2},{2,3},{3,4},{4,5},{5,6},{6,7},{15,8},{8,9},{9,10... | collective-permute-start | bytes 638984 | tf_op jit(solution)/shard_map/ppermute | solution.py:517
  4.2 17.1 %collective-permute-start.4 = (f32[104,512]{1,0:T(8,128)S(1)}, f32[104,512]{1,0:T(8,128)S(1)}, u32[]{:S(2)}, u32[]{:S(2)}) collective-permute-start(f32[104,512]{1,0:T(8,128)S(1)} %get-tuple-element.48), channel_id=1, source_target_pairs={{1,0},{2,1},{3,2},{4,3},{5,4},{6,5},{7,6},{0,7},{9,8},{10,9},{11,1... | collective-permute-start | bytes 638984 | tf_op jit(solution)/shard_map/ppermute | solution.py:517
  6.5 17.1 %collective-permute-start = (f32[15,16,512]{2,1,0:T(8,128)S(1)}, f32[15,16,512]{2,1,0:T(8,128)S(1)}, u32[]{:S(2)}, u32[]{:S(2)}) collective-permute-start(f32[15,16,512]{2,1,0:T(8,128)S(1)} %pack_ahead.1.ahead), channel_id=1, source_target_pairs={{248,0},{0,8},{8,16},{16,24},{24,32},{32,40},{40,48},{48,56},{56,6... | collective-permute-start | bytes 1474568 | tf_op jit(solution)/shard_map/ppermute | solution.py:517
  9.4 14.2 %collective-permute-start.1 = (f32[40,512]{1,0:T(8,128)S(1)}, f32[40,512]{1,0:T(8,128)S(1)}, u32[]{:S(2)}, u32[]{:S(2)}) collective-permute-start(f32[40,512]{1,0:T(8,128)S(1)} %get-tuple-element.44), channel_id=1, source_target_pairs={{255,0},{248,1},{249,2},{250,3},{251,4},{252,5},{253,6},{254,7},{7... | collective-permute-start | bytes 245768 | tf_op jit(solution)/shard_map/ppermute | solution.py:525
  9.5 5.2 %copy-start.1 = (f32[256]{0:T(256)S(1)}, f32[256]{0:T(256)}, u32[]{:S(2)}) copy-start(f32[256]{0:T(256)} %param.8) | copy-start | bytes 3076
  9.5 14.1 %collective-permute-start.2 = (f32[40,512]{1,0:T(8,128)S(1)}, f32[40,512]{1,0:T(8,128)S(1)}, u32[]{:S(2)}, u32[]{:S(2)}) collective-permute-start(f32[40,512]{1,0:T(8,128)S(1)} %get-tuple-element.45), channel_id=1, source_target_pairs={{249,0},{250,1},{251,2},{252,3},{253,4},{254,5},{255,6},{248,7},{1... | collective-permute-start | bytes 245768 | tf_op jit(solution)/shard_map/ppermute | solution.py:525
  25.4 24.1 %copy-start = (f32[8,16,512]{2,1,0:T(8,128)S(1)}, f32[8,16,512]{2,1,0:T(8,128)}, u32[]{:S(2)}) copy-start(f32[8,16,512]{2,1,0:T(8,128)} %pi_ref.1) | copy-start | bytes 786436
  50.8 18.1 %all-to-all-start.1 = ((f32[32,16,128]{2,1,0:T(8,128)}), f32[32,16,128]{2,1,0:T(8,128)S(1)}, u32[]{:S(2)}, u32[]{:S(2)}) async-start(f32[32,16,128]{2,1,0:T(8,128)} %get-tuple-element.74), calls=%async_computation.1 | async-start | bytes 524288 | tf_op jit(solution)/shard_map/all_to_all | solution.py:546
  55.4 8.7 %collective-permute-start.5 = (f32[16,512]{1,0:T(8,128)S(1)}, f32[16,512]{1,0:T(8,128)S(1)}, u32[]{:S(2)}, u32[]{:S(2)}) collective-permute-start(f32[16,512]{1,0:T(8,128)S(1)} %get-tuple-element.76), channel_id=1, source_target_pairs={{8,0},{16,8},{24,16},{32,24},{40,32},{48,40},{56,48},{64,56},{72,6... | collective-permute-start | bytes 98312 | tf_op jit(solution)/shard_map/ppermute | solution.py:517

commit v6 on v5

--- a/solution.py
+++ b/solution.py
@@ -196,6 +196,49 @@
     )(sources, phonons, bonds)
 
 
+def build_tiles(hh_two, hh_three, hh, own):
+    hh_two[...] = hh[pl.ds(own, 8)]
+    hh_two[pl.ds(3, 1)] = hh[pl.ds(own - 1, 1)]
+    hh_two[pl.ds(4, 1)] = hh[pl.ds(0, 1)]
+    hh_three[...] = jnp.zeros_like(hh_three)
+    hh_three[pl.ds(2, 2)] = hh[pl.ds(own - 2, 2)]
+    hh_three[pl.ds(4, 2)] = hh[pl.ds(0, 2)]
+
+
+def turn(v):
+    return pltpu.roll(v, 4, 0)
+
+
+def place_in(v):
+    return lax.broadcasted_iota(jnp.int32, (8, v.shape[1]), 0)
+
+
+def moved_sources(v, along, hh_halo, gg):
+    own = along.shape[0]
+    return jnp.concatenate([along, horizontal(v[own:], hh_halo)], axis=0) + vertical(v, gg)
+
+
+def moved_weighted(v, v_own, along, hh_two, gg):
+    own, sub = along.shape[0], place_in(v)
+    change = v[:own] - v_own
+    tile = jnp.where(sub == 3, turn(change[8:]), jnp.where(sub == 4, turn(change[:8]), v[own:]))
+    tile = horizontal(tile, hh_two)
+    turned = turn(tile)
+    top = along[:8] + jnp.where(sub == 0, turned, 0.0)
+    bottom = along[8:] + jnp.where(sub == 7, turned, 0.0)
+    return jnp.concatenate([top, bottom, tile], axis=0) + vertical(v, gg)
+
+
+def moved_normal(q, q_own, along, hh_three, gg):
+    own, sub = along.shape[0], place_in(q)
+    change = q[:own] - q_own
+    tile = jnp.where(sub < 4, turn(change[8:]), turn(change[:8]))
+    turned = turn(horizontal(tile, hh_three))
+    top = along[:8] + jnp.where(sub < 2, turned, 0.0)
+    bottom = along[8:] + jnp.where(sub > 5, turned, 0.0)
+    return jnp.concatenate([top, bottom], axis=0) + vertical(q, gg)[:own]
+
+
 def inner_kernel(
     s_ref, ph_ref, bond_ref, above, below, hs_ref, wp_own, hwp_ref, q_own, hq_ref, weight_own,
     p_ref, q_ref, t_ref, s_edge, kp_edge, shared, acc, ext, weight, hh_two, hh_three,
@@ -205,12 +248,7 @@
     for k in range(2):
         widen(shared.at[k], bond_ref[k].astype(jnp.float32), below, above, side["bond", k])
         shared[k] = hopping * shared[k]
-    hh_two[...] = shared[0, pl.ds(own, 8)]
-    hh_two[pl.ds(3, 1)] = shared[0, pl.ds(own - 1, 1)]
-    hh_two[pl.ds(4, 1)] = shared[0, pl.ds(0, 1)]
-    hh_three[...] = jnp.zeros_like(hh_three)
-    hh_three[pl.ds(2, 2)] = shared[0, pl.ds(own - 2, 2)]
-    hh_three[pl.ds(4, 2)] = shared[0, pl.ds(0, 2)]
+    build_tiles(hh_two, hh_three, shared.at[0], own)
     first = lax.axis_index("tm") == 0
     for t in range(slices):
         slot = weight.at[t]
@@ -223,28 +261,18 @@
         shared[2 + j] = weight[j]
 
     def one_source(i, _):
-        sub = lax.broadcasted_iota(jnp.int32, (8, columns), 0)
-        turn = lambda v: pltpu.roll(v, 4, 0)
         gg = shared[1]
         sums = [jnp.zeros((8, LANES), jnp.float32)] * 4
         p_old = q_old = None
         s_edge[i] = ext[i, 0]
         for t in range(1, slices):
-            s, v = ext[i, t], ext[i, t - 1]
-            along = jnp.concatenate([hs_ref[i, t - 1], horizontal(v[own:], shared[0, pl.ds(own, 8)])], axis=0)
-            p = s - weight[t] * (along + vertical(v, gg))
+            s = ext[i, t]
+            p = s - weight[t] * moved_sources(ext[i, t - 1], hs_ref[i, t - 1], shared[0, pl.ds(own, 8)], gg)
             if t < slices - 1:
                 p_ref[i, t - 1] = p[:own]
                 sums[0] += squares(s)
                 sums[1] += squares(p)
-            v = weight[t] * p
-            change = v[:own] - wp_own[i, t - 1]
-            tile = jnp.where(sub == 3, turn(change[8:]), jnp.where(sub == 4, turn(change[:8]), v[own:]))
-            tile = horizontal(tile, hh_two[...])
-            turned, along = turn(tile), hwp_ref[i, t - 1]
-            top = along[:8] + jnp.where(sub == 0, turned, 0.0)
-            bottom = along[8:] + jnp.where(sub == 7, turned, 0.0)
-            back = jnp.concatenate([top, bottom, tile], axis=0) + vertical(v, gg)
+            back = moved_weighted(weight[t] * p, wp_own[i, t - 1], hwp_ref[i, t - 1], hh_two[...], gg)
             if t == 1:
                 kp_edge[i] = back
             else:
@@ -252,12 +280,7 @@
                 q_ref[i, t - 2] = q[:own]
                 sums[2] += squares(q)
                 if t > 2:
-                    change = q_old[:own] - q_own[i, t - 3]
-                    tile = jnp.where(sub < 4, turn(change[8:]), turn(change[:8]))
-                    turned, along = turn(horizontal(tile, hh_three[...])), hq_ref[i, t - 3]
-                    top = along[:8] + jnp.where(sub < 2, turned, 0.0)
-                    bottom = along[8:] + jnp.where(sub > 5, turned, 0.0)
-                    moved = jnp.concatenate([top, bottom], axis=0) + vertical(q_old, gg)[:own]
+                    moved = moved_normal(q_old, q_own[i, t - 3], hq_ref[i, t - 3], hh_three[...], gg)
                     u = q[:own] - weight[t - 1, pl.ds(0, own)] * moved
                     t_ref[i, t - 3] = u
                     sums[3] += squares(u)
@@ -299,27 +322,83 @@
     )(sources, phonons, bonds, above, below, *parts)
 
 
+def early_kernel(
+    before, s_ref, bond_ref, wp_own, hwp_own, weight_own, hs_ref, wp_ref, hwp_ref, q_ref, hq_ref, weight
+):
+    count, _, rows, _ = s_ref.shape
+    for j in range(2):
+        weight[j] = jnp.exp(coupling * before[EARLY * count + j])
+    hh = hopping * bond_ref[0].astype(jnp.float32)
+    gg = hopping * bond_ref[1].astype(jnp.float32)
+    gg = jnp.where(lax.broadcasted_iota(jnp.int32, gg.shape, 0) < rows - 1, gg, 0.0)
+
+    def one_source(i, _):
+        s = [before[EARLY * i + j] for j in range(EARLY)] + [s_ref[i, 0]]
+        w = [weight[0], weight[1], weight_own[0]]
+        p, back = [], []
+        for j in range(3):
+            along = horizontal(s[j], hh)
+            hs_ref[i, j] = along
+            p.append(s[j + 1] - w[j] * (along + vertical(s[j], gg)))
+        for j in range(1, 3):
+            v = w[j] * p[j]
+            along = horizontal(v, hh)
+            wp_ref[i, j - 1] = v
+            hwp_ref[i, j - 1] = along
+            back.append(along + vertical(v, gg))
+        back.append(hwp_own[i, 0] + vertical(wp_own[i, 0], gg))
+        for j in range(3):
+            q = p[j] - back[j]
+            q_ref[i, j] = q
+            hq_ref[i, j] = horizontal(q, hh)
+        return 0
+
+    lax.fori_loop(0, count, one_source, 0)
+
+
+def early_parts(before, sources, bonds, own):
+    count, _, rows, columns = sources.shape
+    field = lambda n: jax.ShapeDtypeStruct((count, n, rows, columns), jnp.float32)
+    return pl.pallas_call(
+        early_kernel,
+        out_shape=[field(3), field(2), field(2), field(3), field(3)]
+        + [jax.ShapeDtypeStruct((2, rows, columns), jnp.float32)],
+        in_specs=[VMEM] * 6,
+        out_specs=[VMEM] * 6,
+        compiler_params=PARAMS,
+        name="early_parts",
+    )(before, sources, bonds, own[1], own[2], own[5])
+
+
 def outer_kernel(
-    before, above, below, q_inner, s_edge, kp_edge, shared, acc_inner, p_ref, q_ref, t_ref, partial_ref, ext, weight, acc
+    before, above, below, hs_ref, wp_own, hwp_ref, q_own, hq_ref, weight_own, q_inner, s_edge, kp_edge, shared, acc_inner,
+    p_ref, q_ref, t_ref, partial_ref, ext, weight, acc, hh_two, hh_three,
 ):
     count = s_edge.shape[0]
     own = before.shape[1]
     corner, _ = corner_layout(count)
+    build_tiles(hh_two, hh_three, shared.at[0], own)
     for i in range(count):
         for j in range(EARLY):
             widen(ext.at[i, j], before[EARLY * i + j], below, above, corner[i, j - EARLY])
     for j in range(2):
-        widen(weight.at[j], before[EARLY * count + j], below, above, corner[count, j - 2])
-        weight[j] = jnp.exp(coupling * weight[j])
+        slot = weight.at[j]
+        row, n = corner[count, j - 2]
+        slot[pl.ds(own, n)] = below[pl.ds(row, n)]
+        slot[pl.ds(WIDE - n, n)] = above[pl.ds(row, n)]
+        slot[pl.ds(own, 8)] = jnp.exp(coupling * slot[pl.ds(own, 8)])
+        slot[pl.ds(0, own)] = weight_own[j]
 
     def one_source(i, _):
-        moved = lambda v: kinetic(v, shared[0], shared[1])
+        gg, hh_halo = shared[1], shared[0, pl.ds(own, 8)]
+        two, three = hh_two[...], hh_three[...]
         w = [weight[0], weight[1], shared[2], shared[3]]
         s = [ext[i, 0], ext[i, 1], ext[i, 2], s_edge[i]]
-        p = [s[j + 1] - w[j] * moved(s[j]) for j in range(3)]
-        q = [p[0] - moved(w[1] * p[1]), p[1] - moved(w[2] * p[2]), p[2] - kp_edge[i]]
-        u = [q[1] - w[1] * moved(q[0]), q[2] - w[2] * moved(q[1])]
-        u.append(q_inner[i, 0] - w[3][:own] * moved(q[2])[:own])
+        p = [s[j + 1] - w[j] * moved_sources(s[j], hs_ref[i, j], hh_halo, gg) for j in range(3)]
+        back = [moved_weighted(w[j] * p[j], wp_own[i, j - 1], hwp_ref[i, j - 1], two, gg) for j in (1, 2)]
+        q = [p[0] - back[0], p[1] - back[1], p[2] - kp_edge[i]]
+        moved = [moved_normal(q[j], q_own[i, j], hq_ref[i, j], three, gg) for j in range(3)]
+        u = [x[:own] - w[j + 1][:own] * moved[j] for j, x in enumerate((q[1], q[2], q_inner[i, 0]))]
         for j in range(2):
             p_ref[i, j] = p[j + 1][:own]
             q_ref[i, j] = q[j + 1][:own]
@@ -337,23 +416,25 @@
     partial_ref[...] = jnp.broadcast_to(row, partial_ref.shape)
 
 
-def outer_operators(before, above, below, inner, everyone):
+def outer_operators(before, above, below, early, inner, everyone):
     _, q_inner, _, s_edge, kp_edge, shared, acc = inner
     count, _, rows, columns = q_inner.shape
     field = lambda times: jax.ShapeDtypeStruct((count, times, rows, columns), jnp.float32)
     return pl.pallas_call(
         outer_kernel,
         out_shape=[field(2), field(2), field(3), jax.ShapeDtypeStruct((everyone, LANES), jnp.float32)],
-        in_specs=[VMEM] * 8,
+        in_specs=[VMEM] * 14,
         out_specs=[VMEM] * 4,
         scratch_shapes=[
             pltpu.VMEM((count, EARLY, WIDE, columns), jnp.float32),
             pltpu.VMEM((2, WIDE, columns), jnp.float32),
             pltpu.VMEM((4 * count, 8, LANES), jnp.float32),
+            pltpu.VMEM((8, columns), jnp.float32),
+            pltpu.VMEM((8, columns), jnp.float32),
         ],
         compiler_params=PARAMS,
         name="outer_operators",
-    )(before, above, below, q_inner, s_edge, kp_edge, shared, acc)
+    )(before, above, below, *early, q_inner, s_edge, kp_edge, shared, acc)
 
 
 def force_kernel(
@@ -365,13 +446,13 @@
     m = [moments] + [pltpu.roll(moments, LANES - count * k, 1) for k in range(1, 4)]
     alpha, square, cube = m[0] / m[1], m[2] / m[1], m[3] / m[1]
     spread = cube - square * square
-    lane = lax.broadcasted_iota(jnp.int32, moments.shape, 1)
-
-    def at(values, i):
-        return jnp.sum(jnp.where(lane == i, values, 0.0))
-
-    low = [at((alpha * cube - square) / spread, i) for i in range(count)]
-    high = [at((1.0 - alpha * square) / spread, i) for i in range(count)]
+    rows_of_both = [(alpha * cube - square) / spread] * count + [(1.0 - alpha * square) / spread] * count
+    both = jnp.concatenate(rows_of_both, axis=0)
+    at = lambda d: lax.broadcasted_iota(jnp.int32, both.shape, d)
+    picked = jnp.where(at(1) == lax.rem(at(0), count), both, 0.0)
+    picked = jnp.sum(picked, axis=1, keepdims=True)
+    low = [picked[i : i + 1] for i in range(count)]
+    high = [picked[count + i : count + i + 1] for i in range(count)]
     kept = EARLY * count
     phonon = lambda t: before[kept + 2 + t] if t < 0 else ph_ref[t]
     copies = []
@@ -535,16 +616,17 @@
     before = passed_along(ahead, "tm", 1)
     up_corner, down_corner = pack_corners(ahead)
     above_corner = passed_diagonally(up_corner, 1, 1)
+    own, down_corner = lax.optimization_barrier((own_parts(sources, phonons, bonds), down_corner))
     below_corner = passed_diagonally(down_corner, 1, -1)
     side_halos = (above, below)
-    own = own_parts(sources, phonons, bonds)
-    (above, below), table, own = lax.optimization_barrier((side_halos, circulant(kernel), own))
+    early = early_parts(before, sources, bonds, own)
+    (above, below), table, own, early = lax.optimization_barrier((side_halos, circulant(kernel), own, early))
     inner = inner_operators(sources, phonons, bonds, above, below, own)
-    outer = outer_operators(before, above_corner, below_corner, inner, everyone)
+    outer = outer_operators(before, above_corner, below_corner, early, inner, everyone)
     received = lax.all_to_all(outer[3], ("tm", "slab"), split_axis=0, concat_axis=0, tiled=True)
-    half, early, send = force(received, sources, inner, outer, phonons, before, momenta, peers)
+    half, half_before, send = force(received, sources, inner, outer, phonons, before, momenta, peers)
     columns = lax.all_to_all(send, "tm", split_axis=0, concat_axis=0, tiled=True)
-    half_momenta = join_times(half, passed_along(early, "tm", -1))
+    half_momenta = join_times(half, passed_along(half_before, "tm", -1))
     columns, half_momenta = lax.optimization_barrier((columns, half_momenta))
     mixed = drift(table, columns)
     back = lax.all_to_all(mixed, "tm", split_axis=0, concat_axis=0, tiled=True)

time: 88.1 us -> 87.8 us (level)
  waiting for transfers between devices: 15.2 us -> 13.8 us
  Pallas kernels: 12.5 us -> 13.5 us
    ppermute x4, waiting for transfers between devices: 11.1 us -> 9.68 us  [passed_along(): lax.ppermute(block, axis, [((i - distance) % count, i) for i in range(cou...]
    pallas_call x0 -> x1, Pallas kernels: none -> 1.3 us  [early_parts(): pl.pallas_call(early_kernel, out_shape=[field(3), field(2), field(2), fie...]
  transfers between devices with their start and end apart: 7 -> 7, of which waited for: 3 -> 3; matrix products, arithmetic and copies ran while one was open for 0% -> 0% of each run, Pallas kernels for 8% -> 9%
where the time goes in v6:
time: 87.8 us; the launch traced here: 87.5 us
  blocking collectives  41.8 us (48%)
  starting transfers between devices  17.7 us (20%)
  waiting for transfers between devices  13.8 us (16%)
  Pallas kernels  13.5 us (15%)
    all_to_all x1, blocking collectives, body(): lax.all_to_all(outer[3], ('tm', 'slab'), split_axis=0, concat_axis=0, til...  24.1 us
    all_to_all x1, blocking collectives, body(): back = lax.all_to_all(mixed, 'tm', split_axis=0, concat_axis=0, tiled=True)  17.7 us
    ppermute x4, waiting for transfers between devices, passed_along(): lax.ppermute(block, axis, [((i - distance) % count, i) for i in range(cou...  9.68 us
    ppermute x4, starting transfers between devices, passed_along(): lax.ppermute(block, axis, [((i - distance) % count, i) for i in range(cou...  7.74 us
    ppermute x2, starting transfers between devices, passed_diagonally(): return lax.ppermute(block, ('tm', 'slab'), route)  5.35 us
    all_to_all x1, starting transfers between devices, body(): lax.all_to_all(send, 'tm', split_axis=0, concat_axis=0, tiled=True)  4.56 us
    all_to_all x1, waiting for transfers between devices, body(): lax.all_to_all(send, 'tm', split_axis=0, concat_axis=0, tiled=True)  4.12 us
    pallas_call x1, Pallas kernels, own_parts(): pl.pallas_call(own_kernel, out_shape=[field(slices - 1)] * 3 + [field(sli...  3.52 us
  transfers between devices with their start and end apart: 7, of which 3 were waited for; matrix products, arithmetic and copies ran while one was open for 0% of the time, Pallas kernels for 9%

profile of v6, /device:TPU:1, one launch (start us, length us, event | category | flops | bytes accessed | tf_op | source)
XLA Modules:
  0.0 87.5 jit_solution(2857045927681744119)
XLA Ops:
  0.6 1.4 %pack_sides.1 = (f32[104,512]{1,0:T(8,128)S(1)}, f32[104,512]{1,0:T(8,128)S(1)}, f32[4,8,16,512]{3,2,1,0:T(8,128)S(1)}, f32[8,16,512]{2,1,0:T(8,128)S(1)}, s32[2...) custom-call(f32[4,8,16,512]{3,2,1,0:T(8,128)} %s_hbm.1, f32[8,16,512]{2,1,0:T(8,128)} %ph_hbm.1, s32[2,16,512]{2,1,0:T(8,128)} %bond_hbm.1, ...), custom_call_target="tpu_custom_call" | custom-call | tf_op jit(solution)/shard_map/pack_sides/pallas_call | solution.py:74
  2.0 2.2 %collective-permute-start.3 = (f32[104,512]{1,0:T(8,128)S(1)}, f32[104,512]{1,0:T(8,128)S(1)}, u32[]{:S(2)}, u32[]{:S(2)}) collective-permute-start(f32[104,512]{1,0:T(8,128)S(1)} %get-tuple-element.73), channel_id=1, source_target_pairs={{7,0},{0,1},{1,2},{2,3},{3,4},{4,5},{5,6},{6,7},{15,8},{8,9},{9,10... | collective-permute-start | bytes 638984 | tf_op jit(solution)/shard_map/ppermute | solution.py:598
  4.2 2.3 %collective-permute-start.4 = (f32[104,512]{1,0:T(8,128)S(1)}, f32[104,512]{1,0:T(8,128)S(1)}, u32[]{:S(2)}, u32[]{:S(2)}) collective-permute-start(f32[104,512]{1,0:T(8,128)S(1)} %get-tuple-element.74), channel_id=1, source_target_pairs={{1,0},{2,1},{3,2},{4,3},{5,4},{6,5},{7,6},{0,7},{9,8},{10,9},{11,1... | collective-permute-start | bytes 638984 | tf_op jit(solution)/shard_map/ppermute | solution.py:598
  6.5 2.8 %collective-permute-start = (f32[15,16,512]{2,1,0:T(8,128)S(1)}, f32[15,16,512]{2,1,0:T(8,128)S(1)}, u32[]{:S(2)}, u32[]{:S(2)}) collective-permute-start(f32[15,16,512]{2,1,0:T(8,128)S(1)} %pack_ahead.1.ahead), channel_id=1, source_target_pairs={{248,0},{0,8},{8,16},{16,24},{24,32},{32,40},{40,48},{48,56},{56,6... | collective-permute-start | bytes 1474568 | tf_op jit(solution)/shard_map/ppermute | solution.py:598
  9.4 0.1 collective-permute-start.1
  9.5 3.5 %own_parts.1 = (f32[4,7,16,512]{3,2,1,0:T(8,128)S(1)}, f32[4,7,16,512]{3,2,1,0:T(8,128)S(1)}, f32[4,7,16,512]{3,2,1,0:T(8,128)S(1)}, f32[4,5,16,512]{3,2,1,0:T(8...) custom-call(f32[4,8,16,512]{3,2,1,0:T(8,128)S(1)} %get-tuple-element.60.s_ref, ...), custom_call_target="tpu_custom_call" | custom-call | tf_op jit(solution)/shard_map/own_parts/pallas_call | solution.py:187
  13.0 0.0 copy-start.1
  13.0 5.3 %collective-permute-start.2 = (f32[40,512]{1,0:T(8,128)S(1)}, f32[40,512]{1,0:T(8,128)S(1)}, u32[]{:S(2)}, u32[]{:S(2)}) collective-permute-start(f32[40,512]{1,0:T(8,128)S(1)} %get-tuple-element.72), channel_id=1, source_target_pairs={{249,0},{250,1},{251,2},{252,3},{253,4},{254,5},{255,6},{248,7},{1... | collective-permute-start | bytes 245768 | tf_op jit(solution)/shard_map/ppermute | solution.py:606
  18.3 0.2 circulant.1.table_ref
  18.6 1.3 %early_parts.1 = (f32[4,3,16,512]{3,2,1,0:T(8,128)S(1)}, f32[4,2,16,512]{3,2,1,0:T(8,128)S(1)}, f32[4,2,16,512]{3,2,1,0:T(8,128)S(1)}, f32[4,3,16,512]{3,2,1,0:T...) custom-call(f32[15,16,512]{2,1,0:T(8,128)S(1)} %collective-permute-done.before, ...), custom_call_target="tpu_custom_call" | custom-call | tf_op jit(solution)/shard_map/early_parts/pallas_call | solution.py:362
  19.9 1.4 %collective-permute-done.4.below = f32[104,512]{1,0:T(8,128)S(1)} collective-permute-done((f32[104,512]{1,0:T(8,128)S(1)}, f32[104,512]{1,0:T(8,128)S(1)}, u32[]{:S(2)}, u32[]{:S(2)}) %collective-permute-start.4) | collective-permute-done | bytes 213024 | tf_op jit(solution)/shard_map/ppermute | solution.py:598
  21.3 2.3 %inner_operators.1 = (f32[4,6,16,512]{3,2,1,0:T(8,128)S(1)}, f32[4,6,16,512]{3,2,1,0:T(8,128)S(1)}, f32[4,5,16,512]{3,2,1,0:T(8,128)S(1)}, f32[4,24,512]{2,1,0:T...) custom-call(f32[4,8,16,512]{3,2,1,0:T(8,128)S(1)} %get-tuple-element.60.s_ref, ...), custom_call_target="tpu_custom_call" | custom-call | tf_op jit(solution)/shard_map/inner_operators/pallas_call | solution.py:301
  23.6 1.4 %outer_operators.1 = (f32[4,2,16,512]{3,2,1,0:T(8,128)S(1)}, f32[4,2,16,512]{3,2,1,0:T(8,128)S(1)}, f32[4,3,16,512]{3,2,1,0:T(8,128)S(1)}, f32[256,128]{1,0:T(8,128)S(1)}) custom-call(f32[15,16,512]{2,1,0:T(8,128)S(1)} %collective-permute-done.before, f32[40,512]{1,0:T(8,128)S(1)} %collective-permute-done.1.above, ...), custom_call_target="tpu_custom_call" | custom-call | tf_op jit(solution)/shard_map/outer_operators/pallas_call | solution.py:423
  25.1 0.0 copy-start
  25.1 24.1 %all_to_all.21 = f32[256,1,128]{2,1,0:T(1,128)S(1)} all-to-all(f32[256,1,128]{2,1,0:T(1,128)S(1)} %bitcast.10), channel_id=1, replica_groups=mesh['tm'=32,'slab'=8] {'tm','slab'}, dimensions={0} | all-to-all | bytes 262144 | tf_op jit(solution)/shard_map/all_to_all | solution.py:626
  49.2 1.3 %force.1 = (f32[7,16,512]{2,1,0:T(8,128)S(1)}, f32[16,512]{1,0:T(8,128)S(1)}, f32[32,16,128]{2,1,0:T(8,128)}) custom-call(f32[256,128]{1,0:T(8,128)S(1)} %bitcast.9, f32[4,8,16,512]{3,2,1,0:T(8,128)S(1)} %get-tuple-element.60.s_ref, f32[4,6,16,512]{3,2,1,0:T(8,128)S(1)} %get-tuple-element.107.p_in, f32[4,6,16,512]{3,2,1,0:T(8,128)S(1)} %get-tuple-element.101.q_inner.q_in, ...), custom_call_target="tpu_custom_call" | custom-call | tf_op jit(solution)/shard_map/force/pallas_call | solution.py:493
  50.5 4.6 %all-to-all-start.1 = ((f32[32,16,128]{2,1,0:T(8,128)}), f32[32,16,128]{2,1,0:T(8,128)S(1)}, u32[]{:S(2)}, u32[]{:S(2)}) async-start(f32[32,16,128]{2,1,0:T(8,128)} %get-tuple-element.112), calls=%async_computation.1 | async-start | bytes 524288 | tf_op jit(solution)/shard_map/all_to_all | solution.py:628
  55.0 0.4 collective-permute-start.5
  55.5 8.3 %collective-permute-done.5.late_ref = f32[16,512]{1,0:T(8,128)S(1)} collective-permute-done((f32[16,512]{1,0:T(8,128)S(1)}, f32[16,512]{1,0:T(8,128)S(1)}, u32[]{:S(2)}, u32[]{:S(2)}) %collective-permute-start.5) | collective-permute-done | bytes 32800 | tf_op jit(solution)/shard_map/ppermute | solution.py:598
  63.7 0.7 join_times.1
  64.5 4.1 %all-to-all-done.1 = f32[32,16,128]{2,1,0:T(8,128)S(1)} async-done(((f32[32,16,128]{2,1,0:T(8,128)}), f32[32,16,128]{2,1,0:T(8,128)S(1)}, u32[]{:S(2)}, u32[]{:S(2)}) %all-to-all-start.1) | async-done | bytes 262176 | tf_op jit(solution)/shard_map/all_to_all | solution.py:628
  68.6 0.4 drift.1
  69.0 17.7 %all_to_all.22.back_ref = f32[32,16,128]{2,1,0:T(8,128)S(1)} all-to-all(f32[32,16,128]{2,1,0:T(8,128)S(1)} %bitcast.8), channel_id=1, replica_groups=mesh['tm'=32,'slab'=8] {'tm'}, dimensions={0} | all-to-all | bytes 524288 | tf_op jit(solution)/shard_map/all_to_all | solution.py:632
  86.6 0.9 add_drift.1
  (8 shorter events, 0.1 us)
Async XLA Ops:
  2.0 17.9 %collective-permute-start.3 = (f32[104,512]{1,0:T(8,128)S(1)}, f32[104,512]{1,0:T(8,128)S(1)}, u32[]{:S(2)}, u32[]{:S(2)}) collective-permute-start(f32[104,512]{1,0:T(8,128)S(1)} %get-tuple-element.73), channel_id=1, source_target_pairs={{7,0},{0,1},{1,2},{2,3},{3,4},{4,5},{5,6},{6,7},{15,8},{8,9},{9,10... | collective-permute-start | bytes 638984 | tf_op jit(solution)/shard_map/ppermute | solution.py:598
  4.2 17.1 %collective-permute-start.4 = (f32[104,512]{1,0:T(8,128)S(1)}, f32[104,512]{1,0:T(8,128)S(1)}, u32[]{:S(2)}, u32[]{:S(2)}) collective-permute-start(f32[104,512]{1,0:T(8,128)S(1)} %get-tuple-element.74), channel_id=1, source_target_pairs={{1,0},{2,1},{3,2},{4,3},{5,4},{6,5},{7,6},{0,7},{9,8},{10,9},{11,1... | collective-permute-start | bytes 638984 | tf_op jit(solution)/shard_map/ppermute | solution.py:598
  6.5 12.0 %collective-permute-start = (f32[15,16,512]{2,1,0:T(8,128)S(1)}, f32[15,16,512]{2,1,0:T(8,128)S(1)}, u32[]{:S(2)}, u32[]{:S(2)}) collective-permute-start(f32[15,16,512]{2,1,0:T(8,128)S(1)} %pack_ahead.1.ahead), channel_id=1, source_target_pairs={{248,0},{0,8},{8,16},{16,24},{24,32},{32,40},{40,48},{48,56},{56,6... | collective-permute-start | bytes 1474568 | tf_op jit(solution)/shard_map/ppermute | solution.py:598
  9.4 14.2 %collective-permute-start.1 = (f32[40,512]{1,0:T(8,128)S(1)}, f32[40,512]{1,0:T(8,128)S(1)}, u32[]{:S(2)}, u32[]{:S(2)}) collective-permute-start(f32[40,512]{1,0:T(8,128)S(1)} %get-tuple-element.63), channel_id=1, source_target_pairs={{255,0},{248,1},{249,2},{250,3},{251,4},{252,5},{253,6},{254,7},{7... | collective-permute-start | bytes 245768 | tf_op jit(solution)/shard_map/ppermute | solution.py:606
  13.0 5.3 %copy-start.1 = (f32[256]{0:T(256)S(1)}, f32[256]{0:T(256)}, u32[]{:S(2)}) copy-start(f32[256]{0:T(256)} %param.8) | copy-start | bytes 3076
  13.0 10.6 %collective-permute-start.2 = (f32[40,512]{1,0:T(8,128)S(1)}, f32[40,512]{1,0:T(8,128)S(1)}, u32[]{:S(2)}, u32[]{:S(2)}) collective-permute-start(f32[40,512]{1,0:T(8,128)S(1)} %get-tuple-element.72), channel_id=1, source_target_pairs={{249,0},{250,1},{251,2},{252,3},{253,4},{254,5},{255,6},{248,7},{1... | collective-permute-start | bytes 245768 | tf_op jit(solution)/shard_map/ppermute | solution.py:606
  25.1 24.1 %copy-start = (f32[8,16,512]{2,1,0:T(8,128)S(1)}, f32[8,16,512]{2,1,0:T(8,128)}, u32[]{:S(2)}) copy-start(f32[8,16,512]{2,1,0:T(8,128)} %pi_ref.1) | copy-start | bytes 786436
  50.5 18.1 %all-to-all-start.1 = ((f32[32,16,128]{2,1,0:T(8,128)}), f32[32,16,128]{2,1,0:T(8,128)S(1)}, u32[]{:S(2)}, u32[]{:S(2)}) async-start(f32[32,16,128]{2,1,0:T(8,128)} %get-tuple-element.112), calls=%async_computation.1 | async-start | bytes 524288 | tf_op jit(solution)/shard_map/all_to_all | solution.py:628
  55.0 8.7 %collective-permute-start.5 = (f32[16,512]{1,0:T(8,128)S(1)}, f32[16,512]{1,0:T(8,128)S(1)}, u32[]{:S(2)}, u32[]{:S(2)}) collective-permute-start(f32[16,512]{1,0:T(8,128)S(1)} %get-tuple-element.114), channel_id=1, source_target_pairs={{8,0},{16,8},{24,16},{32,24},{40,32},{48,40},{56,48},{64,56},{72,6... | collective-permute-start | bytes 98312 | tf_op jit(solution)/shard_map/ppermute | solution.py:598

commit v7 on v6

--- a/solution.py
+++ b/solution.py
@@ -290,7 +290,8 @@
             acc[k * count + i] = sums[k]
         return 0
 
-    lax.fori_loop(0, count, one_source, 0)
+    for i in range(count):
+        one_source(i, 0)
 
 
 def inner_operators(sources, phonons, bonds, above, below, parts):
@@ -408,7 +409,8 @@
             acc[k * count + i] = acc_inner[k * count + i] + sum(squares(v) for v in fields)
         return 0
 
-    lax.fori_loop(0, count, one_source, 0)
+    for i in range(count):
+        one_source(i, 0)
     lines = jnp.sum(acc[...], axis=1)
     lines = jnp.broadcast_to(jnp.sum(lines, axis=1, keepdims=True), lines.shape)
     at = lambda d: lax.broadcasted_iota(jnp.int32, lines.shape, d)

time: 87.8 us -> 87.6 us (level)
  transfers between devices with their start and end apart: 7 -> 7, of which waited for: 3 -> 3; matrix products, arithmetic and copies ran while one was open for 0% -> 0% of each run, Pallas kernels for 9% -> 10%
where the time goes in v7:
time: 87.6 us; the launch traced here: 87.3 us
  blocking collectives  41.8 us (48%)
  starting transfers between devices  17.7 us (20%)
  waiting for transfers between devices  13.8 us (16%)
  Pallas kernels  13.3 us (15%)
    all_to_all x1, blocking collectives, body(): lax.all_to_all(outer[3], ('tm', 'slab'), split_axis=0, concat_axis=0, til...  24.1 us
    all_to_all x1, blocking collectives, body(): back = lax.all_to_all(mixed, 'tm', split_axis=0, concat_axis=0, tiled=True)  17.7 us
    ppermute x4, waiting for transfers between devices, passed_along(): lax.ppermute(block, axis, [((i - distance) % count, i) for i in range(cou...  9.68 us
    ppermute x4, starting transfers between devices, passed_along(): lax.ppermute(block, axis, [((i - distance) % count, i) for i in range(cou...  7.74 us
    ppermute x2, starting transfers between devices, passed_diagonally(): return lax.ppermute(block, ('tm', 'slab'), route)  5.35 us
    all_to_all x1, starting transfers between devices, body(): lax.all_to_all(send, 'tm', split_axis=0, concat_axis=0, tiled=True)  4.56 us
    all_to_all x1, waiting for transfers between devices, body(): lax.all_to_all(send, 'tm', split_axis=0, concat_axis=0, tiled=True)  4.12 us
    pallas_call x1, Pallas kernels, own_parts(): pl.pallas_call(own_kernel, out_shape=[field(slices - 1)] * 3 + [field(sli...  3.52 us
  transfers between devices with their start and end apart: 7, of which 3 were waited for; matrix products, arithmetic and copies ran while one was open for 0% of the time, Pallas kernels for 10%

profile of v7, /device:TPU:1, one launch (start us, length us, event | category | flops | bytes accessed | tf_op | source)
XLA Modules:
  0.0 87.3 jit_solution(12846460911673252775)
XLA Ops:
  0.6 1.4 %pack_sides.1 = (f32[104,512]{1,0:T(8,128)S(1)}, f32[104,512]{1,0:T(8,128)S(1)}, f32[4,8,16,512]{3,2,1,0:T(8,128)S(1)}, f32[8,16,512]{2,1,0:T(8,128)S(1)}, s32[2...) custom-call(f32[4,8,16,512]{3,2,1,0:T(8,128)} %s_hbm.1, f32[8,16,512]{2,1,0:T(8,128)} %ph_hbm.1, s32[2,16,512]{2,1,0:T(8,128)} %bond_hbm.1, ...), custom_call_target="tpu_custom_call" | custom-call | tf_op jit(solution)/shard_map/pack_sides/pallas_call | solution.py:74
  2.0 2.2 %collective-permute-start.3 = (f32[104,512]{1,0:T(8,128)S(1)}, f32[104,512]{1,0:T(8,128)S(1)}, u32[]{:S(2)}, u32[]{:S(2)}) collective-permute-start(f32[104,512]{1,0:T(8,128)S(1)} %get-tuple-element.73), channel_id=1, source_target_pairs={{7,0},{0,1},{1,2},{2,3},{3,4},{4,5},{5,6},{6,7},{15,8},{8,9},{9,10... | collective-permute-start | bytes 638984 | tf_op jit(solution)/shard_map/ppermute | solution.py:600
  4.2 2.3 %collective-permute-start.4 = (f32[104,512]{1,0:T(8,128)S(1)}, f32[104,512]{1,0:T(8,128)S(1)}, u32[]{:S(2)}, u32[]{:S(2)}) collective-permute-start(f32[104,512]{1,0:T(8,128)S(1)} %get-tuple-element.74), channel_id=1, source_target_pairs={{1,0},{2,1},{3,2},{4,3},{5,4},{6,5},{7,6},{0,7},{9,8},{10,9},{11,1... | collective-permute-start | bytes 638984 | tf_op jit(solution)/shard_map/ppermute | solution.py:600
  6.5 2.8 %collective-permute-start = (f32[15,16,512]{2,1,0:T(8,128)S(1)}, f32[15,16,512]{2,1,0:T(8,128)S(1)}, u32[]{:S(2)}, u32[]{:S(2)}) collective-permute-start(f32[15,16,512]{2,1,0:T(8,128)S(1)} %pack_ahead.1.ahead), channel_id=1, source_target_pairs={{248,0},{0,8},{8,16},{16,24},{24,32},{32,40},{40,48},{48,56},{56,6... | collective-permute-start | bytes 1474568 | tf_op jit(solution)/shard_map/ppermute | solution.py:600
  9.4 0.1 collective-permute-start.1
  9.5 3.5 %own_parts.1 = (f32[4,7,16,512]{3,2,1,0:T(8,128)S(1)}, f32[4,7,16,512]{3,2,1,0:T(8,128)S(1)}, f32[4,7,16,512]{3,2,1,0:T(8,128)S(1)}, f32[4,5,16,512]{3,2,1,0:T(8...) custom-call(f32[4,8,16,512]{3,2,1,0:T(8,128)S(1)} %get-tuple-element.60.s_ref, ...), custom_call_target="tpu_custom_call" | custom-call | tf_op jit(solution)/shard_map/own_parts/pallas_call | solution.py:187
  13.0 0.0 copy-start.1
  13.0 5.3 %collective-permute-start.2 = (f32[40,512]{1,0:T(8,128)S(1)}, f32[40,512]{1,0:T(8,128)S(1)}, u32[]{:S(2)}, u32[]{:S(2)}) collective-permute-start(f32[40,512]{1,0:T(8,128)S(1)} %get-tuple-element.72), channel_id=1, source_target_pairs={{249,0},{250,1},{251,2},{252,3},{253,4},{254,5},{255,6},{248,7},{1... | collective-permute-start | bytes 245768 | tf_op jit(solution)/shard_map/ppermute | solution.py:608
  18.3 0.2 circulant.1.table_ref
  18.6 1.3 %early_parts.1 = (f32[4,3,16,512]{3,2,1,0:T(8,128)S(1)}, f32[4,2,16,512]{3,2,1,0:T(8,128)S(1)}, f32[4,2,16,512]{3,2,1,0:T(8,128)S(1)}, f32[4,3,16,512]{3,2,1,0:T...) custom-call(f32[15,16,512]{2,1,0:T(8,128)S(1)} %collective-permute-done.before, ...), custom_call_target="tpu_custom_call" | custom-call | tf_op jit(solution)/shard_map/early_parts/pallas_call | solution.py:363
  19.9 1.4 %collective-permute-done.4.below = f32[104,512]{1,0:T(8,128)S(1)} collective-permute-done((f32[104,512]{1,0:T(8,128)S(1)}, f32[104,512]{1,0:T(8,128)S(1)}, u32[]{:S(2)}, u32[]{:S(2)}) %collective-permute-start.4) | collective-permute-done | bytes 213024 | tf_op jit(solution)/shard_map/ppermute | solution.py:600
  21.3 2.5 %inner_operators.1 = (f32[4,6,16,512]{3,2,1,0:T(8,128)S(1)}, f32[4,6,16,512]{3,2,1,0:T(8,128)S(1)}, f32[4,5,16,512]{3,2,1,0:T(8,128)S(1)}, f32[4,24,512]{2,1,0:T...) custom-call(f32[4,8,16,512]{3,2,1,0:T(8,128)S(1)} %get-tuple-element.60.s_ref, ...), custom_call_target="tpu_custom_call" | custom-call | tf_op jit(solution)/shard_map/inner_operators/pallas_call | solution.py:302
  23.8 1.0 %outer_operators.1 = (f32[4,2,16,512]{3,2,1,0:T(8,128)S(1)}, f32[4,2,16,512]{3,2,1,0:T(8,128)S(1)}, f32[4,3,16,512]{3,2,1,0:T(8,128)S(1)}, f32[256,128]{1,0:T(8,128)S(1)}) custom-call(f32[15,16,512]{2,1,0:T(8,128)S(1)} %collective-permute-done.before, f32[40,512]{1,0:T(8,128)S(1)} %collective-permute-done.1.above, ...), custom_call_target="tpu_custom_call" | custom-call | tf_op jit(solution)/shard_map/outer_operators/pallas_call | solution.py:425
  24.9 0.0 copy-start
  24.9 24.1 %all_to_all.21 = f32[256,1,128]{2,1,0:T(1,128)S(1)} all-to-all(f32[256,1,128]{2,1,0:T(1,128)S(1)} %bitcast.10), channel_id=1, replica_groups=mesh['tm'=32,'slab'=8] {'tm','slab'}, dimensions={0} | all-to-all | bytes 262144 | tf_op jit(solution)/shard_map/all_to_all | solution.py:628
  49.0 1.3 %force.1 = (f32[7,16,512]{2,1,0:T(8,128)S(1)}, f32[16,512]{1,0:T(8,128)S(1)}, f32[32,16,128]{2,1,0:T(8,128)}) custom-call(f32[256,128]{1,0:T(8,128)S(1)} %bitcast.9, f32[4,8,16,512]{3,2,1,0:T(8,128)S(1)} %get-tuple-element.60.s_ref, f32[4,6,16,512]{3,2,1,0:T(8,128)S(1)} %get-tuple-element.107.p_in, f32[4,6,16,512]{3,2,1,0:T(8,128)S(1)} %get-tuple-element.101.q_inner.q_in, ...), custom_call_target="tpu_custom_call" | custom-call | tf_op jit(solution)/shard_map/force/pallas_call | solution.py:495
  50.3 4.6 %all-to-all-start.1 = ((f32[32,16,128]{2,1,0:T(8,128)}), f32[32,16,128]{2,1,0:T(8,128)S(1)}, u32[]{:S(2)}, u32[]{:S(2)}) async-start(f32[32,16,128]{2,1,0:T(8,128)} %get-tuple-element.112), calls=%async_computation.1 | async-start | bytes 524288 | tf_op jit(solution)/shard_map/all_to_all | solution.py:630
  54.9 0.4 collective-permute-start.5
  55.3 8.3 %collective-permute-done.5.late_ref = f32[16,512]{1,0:T(8,128)S(1)} collective-permute-done((f32[16,512]{1,0:T(8,128)S(1)}, f32[16,512]{1,0:T(8,128)S(1)}, u32[]{:S(2)}, u32[]{:S(2)}) %collective-permute-start.5) | collective-permute-done | bytes 32800 | tf_op jit(solution)/shard_map/ppermute | solution.py:600
  63.6 0.7 join_times.1
  64.3 4.1 %all-to-all-done.1 = f32[32,16,128]{2,1,0:T(8,128)S(1)} async-done(((f32[32,16,128]{2,1,0:T(8,128)}), f32[32,16,128]{2,1,0:T(8,128)S(1)}, u32[]{:S(2)}, u32[]{:S(2)}) %all-to-all-start.1) | async-done | bytes 262176 | tf_op jit(solution)/shard_map/all_to_all | solution.py:630
  68.4 0.4 drift.1
  68.8 17.7 %all_to_all.22.back_ref = f32[32,16,128]{2,1,0:T(8,128)S(1)} all-to-all(f32[32,16,128]{2,1,0:T(8,128)S(1)} %bitcast.8), channel_id=1, replica_groups=mesh['tm'=32,'slab'=8] {'tm'}, dimensions={0} | all-to-all | bytes 524288 | tf_op jit(solution)/shard_map/all_to_all | solution.py:634
  86.4 0.9 add_drift.1
  (8 shorter events, 0.1 us)
Async XLA Ops:
  2.0 17.9 %collective-permute-start.3 = (f32[104,512]{1,0:T(8,128)S(1)}, f32[104,512]{1,0:T(8,128)S(1)}, u32[]{:S(2)}, u32[]{:S(2)}) collective-permute-start(f32[104,512]{1,0:T(8,128)S(1)} %get-tuple-element.73), channel_id=1, source_target_pairs={{7,0},{0,1},{1,2},{2,3},{3,4},{4,5},{5,6},{6,7},{15,8},{8,9},{9,10... | collective-permute-start | bytes 638984 | tf_op jit(solution)/shard_map/ppermute | solution.py:600
  4.2 17.1 %collective-permute-start.4 = (f32[104,512]{1,0:T(8,128)S(1)}, f32[104,512]{1,0:T(8,128)S(1)}, u32[]{:S(2)}, u32[]{:S(2)}) collective-permute-start(f32[104,512]{1,0:T(8,128)S(1)} %get-tuple-element.74), channel_id=1, source_target_pairs={{1,0},{2,1},{3,2},{4,3},{5,4},{6,5},{7,6},{0,7},{9,8},{10,9},{11,1... | collective-permute-start | bytes 638984 | tf_op jit(solution)/shard_map/ppermute | solution.py:600
  6.5 12.0 %collective-permute-start = (f32[15,16,512]{2,1,0:T(8,128)S(1)}, f32[15,16,512]{2,1,0:T(8,128)S(1)}, u32[]{:S(2)}, u32[]{:S(2)}) collective-permute-start(f32[15,16,512]{2,1,0:T(8,128)S(1)} %pack_ahead.1.ahead), channel_id=1, source_target_pairs={{248,0},{0,8},{8,16},{16,24},{24,32},{32,40},{40,48},{48,56},{56,6... | collective-permute-start | bytes 1474568 | tf_op jit(solution)/shard_map/ppermute | solution.py:600
  9.4 14.4 %collective-permute-start.1 = (f32[40,512]{1,0:T(8,128)S(1)}, f32[40,512]{1,0:T(8,128)S(1)}, u32[]{:S(2)}, u32[]{:S(2)}) collective-permute-start(f32[40,512]{1,0:T(8,128)S(1)} %get-tuple-element.63), channel_id=1, source_target_pairs={{255,0},{248,1},{249,2},{250,3},{251,4},{252,5},{253,6},{254,7},{7... | collective-permute-start | bytes 245768 | tf_op jit(solution)/shard_map/ppermute | solution.py:608
  13.0 5.3 %copy-start.1 = (f32[256]{0:T(256)S(1)}, f32[256]{0:T(256)}, u32[]{:S(2)}) copy-start(f32[256]{0:T(256)} %param.8) | copy-start | bytes 3076
  13.0 10.8 %collective-permute-start.2 = (f32[40,512]{1,0:T(8,128)S(1)}, f32[40,512]{1,0:T(8,128)S(1)}, u32[]{:S(2)}, u32[]{:S(2)}) collective-permute-start(f32[40,512]{1,0:T(8,128)S(1)} %get-tuple-element.72), channel_id=1, source_target_pairs={{249,0},{250,1},{251,2},{252,3},{253,4},{254,5},{255,6},{248,7},{1... | collective-permute-start | bytes 245768 | tf_op jit(solution)/shard_map/ppermute | solution.py:608
  24.9 24.1 %copy-start = (f32[8,16,512]{2,1,0:T(8,128)S(1)}, f32[8,16,512]{2,1,0:T(8,128)}, u32[]{:S(2)}) copy-start(f32[8,16,512]{2,1,0:T(8,128)} %pi_ref.1) | copy-start | bytes 786436
  50.3 18.1 %all-to-all-start.1 = ((f32[32,16,128]{2,1,0:T(8,128)}), f32[32,16,128]{2,1,0:T(8,128)S(1)}, u32[]{:S(2)}, u32[]{:S(2)}) async-start(f32[32,16,128]{2,1,0:T(8,128)} %get-tuple-element.112), calls=%async_computation.1 | async-start | bytes 524288 | tf_op jit(solution)/shard_map/all_to_all | solution.py:630
  54.9 8.7 %collective-permute-start.5 = (f32[16,512]{1,0:T(8,128)S(1)}, f32[16,512]{1,0:T(8,128)S(1)}, u32[]{:S(2)}, u32[]{:S(2)}) collective-permute-start(f32[16,512]{1,0:T(8,128)S(1)} %get-tuple-element.114), channel_id=1, source_target_pairs={{8,0},{16,8},{24,16},{32,24},{40,32},{48,40},{56,48},{64,56},{72,6... | collective-permute-start | bytes 98312 | tf_op jit(solution)/shard_map/ppermute | solution.py:600

commit v8 on v6

--- a/solution.py
+++ b/solution.py
@@ -614,9 +614,9 @@
     below = passed_along(down, "slab", -1)
     ahead = pack_ahead(sources, phonons, last_momenta)
     before = passed_along(ahead, "tm", 1)
-    up_corner, down_corner = pack_corners(ahead)
+    own, corner_slices = lax.optimization_barrier((own_parts(sources, phonons, bonds), ahead))
+    up_corner, down_corner = pack_corners(corner_slices)
     above_corner = passed_diagonally(up_corner, 1, 1)
-    own, down_corner = lax.optimization_barrier((own_parts(sources, phonons, bonds), down_corner))
     below_corner = passed_diagonally(down_corner, 1, -1)
     side_halos = (above, below)
     early = early_parts(before, sources, bonds, own)

time: 87.8 us -> 87.7 us (level)
  no operation moved by 1% of the time
where the time goes in v8:
time: 87.7 us; the launch traced here: 87.5 us
  blocking collectives  41.8 us (48%)
  starting transfers between devices  17.6 us (20%)
  waiting for transfers between devices  13.9 us (16%)
  Pallas kernels  13.5 us (15%)
    all_to_all x1, blocking collectives, body(): lax.all_to_all(outer[3], ('tm', 'slab'), split_axis=0, concat_axis=0, til...  24.1 us
    all_to_all x1, blocking collectives, body(): back = lax.all_to_all(mixed, 'tm', split_axis=0, concat_axis=0, tiled=True)  17.7 us
    ppermute x4, waiting for transfers between devices, passed_along(): lax.ppermute(block, axis, [((i - distance) % count, i) for i in range(cou...  9.78 us
    ppermute x4, starting transfers between devices, passed_along(): lax.ppermute(block, axis, [((i - distance) % count, i) for i in range(cou...  7.74 us
    ppermute x2, starting transfers between devices, passed_diagonally(): return lax.ppermute(block, ('tm', 'slab'), route)  5.27 us
    all_to_all x1, starting transfers between devices, body(): lax.all_to_all(send, 'tm', split_axis=0, concat_axis=0, tiled=True)  4.56 us
    all_to_all x1, waiting for transfers between devices, body(): lax.all_to_all(send, 'tm', split_axis=0, concat_axis=0, tiled=True)  4.12 us
    pallas_call x1, Pallas kernels, own_parts(): pl.pallas_call(own_kernel, out_shape=[field(slices - 1)] * 3 + [field(sli...  3.5 us
  transfers between devices with their start and end apart: 7, of which 3 were waited for; matrix products, arithmetic and copies ran while one was open for 0% of the time, Pallas kernels for 9%

profile of v8, /device:TPU:1, one launch (start us, length us, event | category | flops | bytes accessed | tf_op | source)
XLA Modules:
  0.0 87.5 jit_solution(3107554633231968747)
XLA Ops:
  0.6 1.4 %pack_sides.1 = (f32[104,512]{1,0:T(8,128)S(1)}, f32[104,512]{1,0:T(8,128)S(1)}, f32[4,8,16,512]{3,2,1,0:T(8,128)S(1)}, f32[8,16,512]{2,1,0:T(8,128)S(1)}, s32[2...) custom-call(f32[4,8,16,512]{3,2,1,0:T(8,128)} %s_hbm.1, f32[8,16,512]{2,1,0:T(8,128)} %ph_hbm.1, s32[2,16,512]{2,1,0:T(8,128)} %bond_hbm.1, ...), custom_call_target="tpu_custom_call" | custom-call | tf_op jit(solution)/shard_map/pack_sides/pallas_call | solution.py:74
  2.0 2.2 %collective-permute-start.3 = (f32[104,512]{1,0:T(8,128)S(1)}, f32[104,512]{1,0:T(8,128)S(1)}, u32[]{:S(2)}, u32[]{:S(2)}) collective-permute-start(f32[104,512]{1,0:T(8,128)S(1)} %get-tuple-element.73), channel_id=1, source_target_pairs={{7,0},{0,1},{1,2},{2,3},{3,4},{4,5},{5,6},{6,7},{15,8},{8,9},{9,10... | collective-permute-start | bytes 638984 | tf_op jit(solution)/shard_map/ppermute | solution.py:598
  4.2 2.3 %collective-permute-start.4 = (f32[104,512]{1,0:T(8,128)S(1)}, f32[104,512]{1,0:T(8,128)S(1)}, u32[]{:S(2)}, u32[]{:S(2)}) collective-permute-start(f32[104,512]{1,0:T(8,128)S(1)} %get-tuple-element.74), channel_id=1, source_target_pairs={{1,0},{2,1},{3,2},{4,3},{5,4},{6,5},{7,6},{0,7},{9,8},{10,9},{11,1... | collective-permute-start | bytes 638984 | tf_op jit(solution)/shard_map/ppermute | solution.py:598
  6.5 2.8 %collective-permute-start = (f32[15,16,512]{2,1,0:T(8,128)S(1)}, f32[15,16,512]{2,1,0:T(8,128)S(1)}, u32[]{:S(2)}, u32[]{:S(2)}) collective-permute-start(f32[15,16,512]{2,1,0:T(8,128)S(1)} %pack_ahead.1.ahead), channel_id=1, source_target_pairs={{248,0},{0,8},{8,16},{16,24},{24,32},{32,40},{40,48},{48,56},{56,6... | collective-permute-start | bytes 1474568 | tf_op jit(solution)/shard_map/ppermute | solution.py:598
  9.4 3.5 %own_parts.1 = (f32[4,7,16,512]{3,2,1,0:T(8,128)S(1)}, f32[4,7,16,512]{3,2,1,0:T(8,128)S(1)}, f32[4,7,16,512]{3,2,1,0:T(8,128)S(1)}, f32[4,5,16,512]{3,2,1,0:T(8...) custom-call(f32[4,8,16,512]{3,2,1,0:T(8,128)S(1)} %get-tuple-element.60.s_ref, ...), custom_call_target="tpu_custom_call" | custom-call | tf_op jit(solution)/shard_map/own_parts/pallas_call | solution.py:187
  12.9 0.1 collective-permute-start.1
  13.0 0.0 copy-start.1
  13.0 5.2 %collective-permute-start.2 = (f32[40,512]{1,0:T(8,128)S(1)}, f32[40,512]{1,0:T(8,128)S(1)}, u32[]{:S(2)}, u32[]{:S(2)}) collective-permute-start(f32[40,512]{1,0:T(8,128)S(1)} %get-tuple-element.72), channel_id=1, source_target_pairs={{249,0},{250,1},{251,2},{252,3},{253,4},{254,5},{255,6},{248,7},{1... | collective-permute-start | bytes 245768 | tf_op jit(solution)/shard_map/ppermute | solution.py:606
  18.2 0.2 circulant.1.table_ref
  18.5 1.3 %early_parts.1 = (f32[4,3,16,512]{3,2,1,0:T(8,128)S(1)}, f32[4,2,16,512]{3,2,1,0:T(8,128)S(1)}, f32[4,2,16,512]{3,2,1,0:T(8,128)S(1)}, f32[4,3,16,512]{3,2,1,0:T...) custom-call(f32[15,16,512]{2,1,0:T(8,128)S(1)} %collective-permute-done.before, ...), custom_call_target="tpu_custom_call" | custom-call | tf_op jit(solution)/shard_map/early_parts/pallas_call | solution.py:362
  19.8 1.5 %collective-permute-done.4.below = f32[104,512]{1,0:T(8,128)S(1)} collective-permute-done((f32[104,512]{1,0:T(8,128)S(1)}, f32[104,512]{1,0:T(8,128)S(1)}, u32[]{:S(2)}, u32[]{:S(2)}) %collective-permute-start.4) | collective-permute-done | bytes 213024 | tf_op jit(solution)/shard_map/ppermute | solution.py:598
  21.3 2.3 %inner_operators.1 = (f32[4,6,16,512]{3,2,1,0:T(8,128)S(1)}, f32[4,6,16,512]{3,2,1,0:T(8,128)S(1)}, f32[4,5,16,512]{3,2,1,0:T(8,128)S(1)}, f32[4,24,512]{2,1,0:T...) custom-call(f32[4,8,16,512]{3,2,1,0:T(8,128)S(1)} %get-tuple-element.60.s_ref, ...), custom_call_target="tpu_custom_call" | custom-call | tf_op jit(solution)/shard_map/inner_operators/pallas_call | solution.py:301
  23.6 1.4 %outer_operators.1 = (f32[4,2,16,512]{3,2,1,0:T(8,128)S(1)}, f32[4,2,16,512]{3,2,1,0:T(8,128)S(1)}, f32[4,3,16,512]{3,2,1,0:T(8,128)S(1)}, f32[256,128]{1,0:T(8,128)S(1)}) custom-call(f32[15,16,512]{2,1,0:T(8,128)S(1)} %collective-permute-done.before, f32[40,512]{1,0:T(8,128)S(1)} %collective-permute-done.1.above, ...), custom_call_target="tpu_custom_call" | custom-call | tf_op jit(solution)/shard_map/outer_operators/pallas_call | solution.py:423
  25.1 0.0 copy-start
  25.1 24.1 %all_to_all.21 = f32[256,1,128]{2,1,0:T(1,128)S(1)} all-to-all(f32[256,1,128]{2,1,0:T(1,128)S(1)} %bitcast.10), channel_id=1, replica_groups=mesh['tm'=32,'slab'=8] {'tm','slab'}, dimensions={0} | all-to-all | bytes 262144 | tf_op jit(solution)/shard_map/all_to_all | solution.py:626
  49.2 1.3 %force.1 = (f32[7,16,512]{2,1,0:T(8,128)S(1)}, f32[16,512]{1,0:T(8,128)S(1)}, f32[32,16,128]{2,1,0:T(8,128)}) custom-call(f32[256,128]{1,0:T(8,128)S(1)} %bitcast.9, f32[4,8,16,512]{3,2,1,0:T(8,128)S(1)} %get-tuple-element.60.s_ref, f32[4,6,16,512]{3,2,1,0:T(8,128)S(1)} %get-tuple-element.107.p_in, f32[4,6,16,512]{3,2,1,0:T(8,128)S(1)} %get-tuple-element.101.q_inner.q_in, ...), custom_call_target="tpu_custom_call" | custom-call | tf_op jit(solution)/shard_map/force/pallas_call | solution.py:493
  50.5 4.6 %all-to-all-start.1 = ((f32[32,16,128]{2,1,0:T(8,128)}), f32[32,16,128]{2,1,0:T(8,128)S(1)}, u32[]{:S(2)}, u32[]{:S(2)}) async-start(f32[32,16,128]{2,1,0:T(8,128)} %get-tuple-element.112), calls=%async_computation.1 | async-start | bytes 524288 | tf_op jit(solution)/shard_map/all_to_all | solution.py:628
  55.0 0.4 collective-permute-start.5
  55.5 8.3 %collective-permute-done.5.late_ref = f32[16,512]{1,0:T(8,128)S(1)} collective-permute-done((f32[16,512]{1,0:T(8,128)S(1)}, f32[16,512]{1,0:T(8,128)S(1)}, u32[]{:S(2)}, u32[]{:S(2)}) %collective-permute-start.5) | collective-permute-done | bytes 32800 | tf_op jit(solution)/shard_map/ppermute | solution.py:598
  63.7 0.7 join_times.1
  64.5 4.1 %all-to-all-done.1 = f32[32,16,128]{2,1,0:T(8,128)S(1)} async-done(((f32[32,16,128]{2,1,0:T(8,128)}), f32[32,16,128]{2,1,0:T(8,128)S(1)}, u32[]{:S(2)}, u32[]{:S(2)}) %all-to-all-start.1) | async-done | bytes 262176 | tf_op jit(solution)/shard_map/all_to_all | solution.py:628
  68.6 0.4 drift.1
  69.0 17.7 %all_to_all.22.back_ref = f32[32,16,128]{2,1,0:T(8,128)S(1)} all-to-all(f32[32,16,128]{2,1,0:T(8,128)S(1)} %bitcast.8), channel_id=1, replica_groups=mesh['tm'=32,'slab'=8] {'tm'}, dimensions={0} | all-to-all | bytes 524288 | tf_op jit(solution)/shard_map/all_to_all | solution.py:632
  86.6 0.9 add_drift.1
  (8 shorter events, 0.1 us)
Async XLA Ops:
  2.0 17.8 %collective-permute-start.3 = (f32[104,512]{1,0:T(8,128)S(1)}, f32[104,512]{1,0:T(8,128)S(1)}, u32[]{:S(2)}, u32[]{:S(2)}) collective-permute-start(f32[104,512]{1,0:T(8,128)S(1)} %get-tuple-element.73), channel_id=1, source_target_pairs={{7,0},{0,1},{1,2},{2,3},{3,4},{4,5},{5,6},{6,7},{15,8},{8,9},{9,10... | collective-permute-start | bytes 638984 | tf_op jit(solution)/shard_map/ppermute | solution.py:598
  4.2 17.1 %collective-permute-start.4 = (f32[104,512]{1,0:T(8,128)S(1)}, f32[104,512]{1,0:T(8,128)S(1)}, u32[]{:S(2)}, u32[]{:S(2)}) collective-permute-start(f32[104,512]{1,0:T(8,128)S(1)} %get-tuple-element.74), channel_id=1, source_target_pairs={{1,0},{2,1},{3,2},{4,3},{5,4},{6,5},{7,6},{0,7},{9,8},{10,9},{11,1... | collective-permute-start | bytes 638984 | tf_op jit(solution)/shard_map/ppermute | solution.py:598
  6.5 11.9 %collective-permute-start = (f32[15,16,512]{2,1,0:T(8,128)S(1)}, f32[15,16,512]{2,1,0:T(8,128)S(1)}, u32[]{:S(2)}, u32[]{:S(2)}) collective-permute-start(f32[15,16,512]{2,1,0:T(8,128)S(1)} %pack_ahead.1.ahead), channel_id=1, source_target_pairs={{248,0},{0,8},{8,16},{16,24},{24,32},{32,40},{40,48},{48,56},{56,6... | collective-permute-start | bytes 1474568 | tf_op jit(solution)/shard_map/ppermute | solution.py:598
  12.9 10.7 %collective-permute-start.1 = (f32[40,512]{1,0:T(8,128)S(1)}, f32[40,512]{1,0:T(8,128)S(1)}, u32[]{:S(2)}, u32[]{:S(2)}) collective-permute-start(f32[40,512]{1,0:T(8,128)S(1)} %get-tuple-element.71), channel_id=1, source_target_pairs={{255,0},{248,1},{249,2},{250,3},{251,4},{252,5},{253,6},{254,7},{7... | collective-permute-start | bytes 245768 | tf_op jit(solution)/shard_map/ppermute | solution.py:606
  13.0 5.2 %copy-start.1 = (f32[256]{0:T(256)S(1)}, f32[256]{0:T(256)}, u32[]{:S(2)}) copy-start(f32[256]{0:T(256)} %param.8) | copy-start | bytes 3076
  13.0 10.6 %collective-permute-start.2 = (f32[40,512]{1,0:T(8,128)S(1)}, f32[40,512]{1,0:T(8,128)S(1)}, u32[]{:S(2)}, u32[]{:S(2)}) collective-permute-start(f32[40,512]{1,0:T(8,128)S(1)} %get-tuple-element.72), channel_id=1, source_target_pairs={{249,0},{250,1},{251,2},{252,3},{253,4},{254,5},{255,6},{248,7},{1... | collective-permute-start | bytes 245768 | tf_op jit(solution)/shard_map/ppermute | solution.py:606
  25.1 24.1 %copy-start = (f32[8,16,512]{2,1,0:T(8,128)S(1)}, f32[8,16,512]{2,1,0:T(8,128)}, u32[]{:S(2)}) copy-start(f32[8,16,512]{2,1,0:T(8,128)} %pi_ref.1) | copy-start | bytes 786436
  50.5 18.1 %all-to-all-start.1 = ((f32[32,16,128]{2,1,0:T(8,128)}), f32[32,16,128]{2,1,0:T(8,128)S(1)}, u32[]{:S(2)}, u32[]{:S(2)}) async-start(f32[32,16,128]{2,1,0:T(8,128)} %get-tuple-element.112), calls=%async_computation.1 | async-start | bytes 524288 | tf_op jit(solution)/shard_map/all_to_all | solution.py:628
  55.0 8.7 %collective-permute-start.5 = (f32[16,512]{1,0:T(8,128)S(1)}, f32[16,512]{1,0:T(8,128)S(1)}, u32[]{:S(2)}, u32[]{:S(2)}) collective-permute-start(f32[16,512]{1,0:T(8,128)S(1)} %get-tuple-element.114), channel_id=1, source_target_pairs={{8,0},{16,8},{24,16},{32,24},{40,32},{48,40},{56,48},{64,56},{72,6... | collective-permute-start | bytes 98312 | tf_op jit(solution)/shard_map/ppermute | solution.py:598

commit v9 on v7

--- a/solution.py
+++ b/solution.py
@@ -616,9 +616,9 @@
     below = passed_along(down, "slab", -1)
     ahead = pack_ahead(sources, phonons, last_momenta)
     before = passed_along(ahead, "tm", 1)
-    up_corner, down_corner = pack_corners(ahead)
+    own, corner_slices = lax.optimization_barrier((own_parts(sources, phonons, bonds), ahead))
+    up_corner, down_corner = pack_corners(corner_slices)
     above_corner = passed_diagonally(up_corner, 1, 1)
-    own, down_corner = lax.optimization_barrier((own_parts(sources, phonons, bonds), down_corner))
     below_corner = passed_diagonally(down_corner, 1, -1)
     side_halos = (above, below)
     early = early_parts(before, sources, bonds, own)

time: 87.6 us -> 87.5 us (level)
  no operation moved by 1% of the time
where the time goes in v9:
time: 87.5 us; the launch traced here: 87.3 us
  blocking collectives  41.8 us (48%)
  starting transfers between devices  17.6 us (20%)
  waiting for transfers between devices  13.9 us (16%)
  Pallas kernels  13.3 us (15%)
    all_to_all x1, blocking collectives, body(): lax.all_to_all(outer[3], ('tm', 'slab'), split_axis=0, concat_axis=0, til...  24.1 us
    all_to_all x1, blocking collectives, body(): back = lax.all_to_all(mixed, 'tm', split_axis=0, concat_axis=0, tiled=True)  17.7 us
    ppermute x4, waiting for transfers between devices, passed_along(): lax.ppermute(block, axis, [((i - distance) % count, i) for i in range(cou...  9.78 us
    ppermute x4, starting transfers between devices, passed_along(): lax.ppermute(block, axis, [((i - distance) % count, i) for i in range(cou...  7.74 us
    ppermute x2, starting transfers between devices, passed_diagonally(): return lax.ppermute(block, ('tm', 'slab'), route)  5.27 us
    all_to_all x1, starting transfers between devices, body(): lax.all_to_all(send, 'tm', split_axis=0, concat_axis=0, tiled=True)  4.56 us
    all_to_all x1, waiting for transfers between devices, body(): lax.all_to_all(send, 'tm', split_axis=0, concat_axis=0, tiled=True)  4.12 us
    pallas_call x1, Pallas kernels, own_parts(): pl.pallas_call(own_kernel, out_shape=[field(slices - 1)] * 3 + [field(sli...  3.5 us
  transfers between devices with their start and end apart: 7, of which 3 were waited for; matrix products, arithmetic and copies ran while one was open for 0% of the time, Pallas kernels for 10%

profile of v9, /device:TPU:1, one launch (start us, length us, event | category | flops | bytes accessed | tf_op | source)
XLA Modules:
  0.0 87.3 jit_solution(17076016609132477692)
XLA Ops:
  0.6 1.4 %pack_sides.1 = (f32[104,512]{1,0:T(8,128)S(1)}, f32[104,512]{1,0:T(8,128)S(1)}, f32[4,8,16,512]{3,2,1,0:T(8,128)S(1)}, f32[8,16,512]{2,1,0:T(8,128)S(1)}, s32[2...) custom-call(f32[4,8,16,512]{3,2,1,0:T(8,128)} %s_hbm.1, f32[8,16,512]{2,1,0:T(8,128)} %ph_hbm.1, s32[2,16,512]{2,1,0:T(8,128)} %bond_hbm.1, ...), custom_call_target="tpu_custom_call" | custom-call | tf_op jit(solution)/shard_map/pack_sides/pallas_call | solution.py:74
  2.0 2.2 %collective-permute-start.3 = (f32[104,512]{1,0:T(8,128)S(1)}, f32[104,512]{1,0:T(8,128)S(1)}, u32[]{:S(2)}, u32[]{:S(2)}) collective-permute-start(f32[104,512]{1,0:T(8,128)S(1)} %get-tuple-element.73), channel_id=1, source_target_pairs={{7,0},{0,1},{1,2},{2,3},{3,4},{4,5},{5,6},{6,7},{15,8},{8,9},{9,10... | collective-permute-start | bytes 638984 | tf_op jit(solution)/shard_map/ppermute | solution.py:600
  4.2 2.3 %collective-permute-start.4 = (f32[104,512]{1,0:T(8,128)S(1)}, f32[104,512]{1,0:T(8,128)S(1)}, u32[]{:S(2)}, u32[]{:S(2)}) collective-permute-start(f32[104,512]{1,0:T(8,128)S(1)} %get-tuple-element.74), channel_id=1, source_target_pairs={{1,0},{2,1},{3,2},{4,3},{5,4},{6,5},{7,6},{0,7},{9,8},{10,9},{11,1... | collective-permute-start | bytes 638984 | tf_op jit(solution)/shard_map/ppermute | solution.py:600
  6.5 2.8 %collective-permute-start = (f32[15,16,512]{2,1,0:T(8,128)S(1)}, f32[15,16,512]{2,1,0:T(8,128)S(1)}, u32[]{:S(2)}, u32[]{:S(2)}) collective-permute-start(f32[15,16,512]{2,1,0:T(8,128)S(1)} %pack_ahead.1.ahead), channel_id=1, source_target_pairs={{248,0},{0,8},{8,16},{16,24},{24,32},{32,40},{40,48},{48,56},{56,6... | collective-permute-start | bytes 1474568 | tf_op jit(solution)/shard_map/ppermute | solution.py:600
  9.4 3.5 %own_parts.1 = (f32[4,7,16,512]{3,2,1,0:T(8,128)S(1)}, f32[4,7,16,512]{3,2,1,0:T(8,128)S(1)}, f32[4,7,16,512]{3,2,1,0:T(8,128)S(1)}, f32[4,5,16,512]{3,2,1,0:T(8...) custom-call(f32[4,8,16,512]{3,2,1,0:T(8,128)S(1)} %get-tuple-element.60.s_ref, ...), custom_call_target="tpu_custom_call" | custom-call | tf_op jit(solution)/shard_map/own_parts/pallas_call | solution.py:187
  12.9 0.1 collective-permute-start.1
  13.0 0.0 copy-start.1
  13.0 5.2 %collective-permute-start.2 = (f32[40,512]{1,0:T(8,128)S(1)}, f32[40,512]{1,0:T(8,128)S(1)}, u32[]{:S(2)}, u32[]{:S(2)}) collective-permute-start(f32[40,512]{1,0:T(8,128)S(1)} %get-tuple-element.72), channel_id=1, source_target_pairs={{249,0},{250,1},{251,2},{252,3},{253,4},{254,5},{255,6},{248,7},{1... | collective-permute-start | bytes 245768 | tf_op jit(solution)/shard_map/ppermute | solution.py:608
  18.2 0.2 circulant.1.table_ref
  18.5 1.3 %early_parts.1 = (f32[4,3,16,512]{3,2,1,0:T(8,128)S(1)}, f32[4,2,16,512]{3,2,1,0:T(8,128)S(1)}, f32[4,2,16,512]{3,2,1,0:T(8,128)S(1)}, f32[4,3,16,512]{3,2,1,0:T...) custom-call(f32[15,16,512]{2,1,0:T(8,128)S(1)} %collective-permute-done.before, ...), custom_call_target="tpu_custom_call" | custom-call | tf_op jit(solution)/shard_map/early_parts/pallas_call | solution.py:363
  19.8 1.5 %collective-permute-done.4.below = f32[104,512]{1,0:T(8,128)S(1)} collective-permute-done((f32[104,512]{1,0:T(8,128)S(1)}, f32[104,512]{1,0:T(8,128)S(1)}, u32[]{:S(2)}, u32[]{:S(2)}) %collective-permute-start.4) | collective-permute-done | bytes 213024 | tf_op jit(solution)/shard_map/ppermute | solution.py:600
  21.3 2.5 %inner_operators.1 = (f32[4,6,16,512]{3,2,1,0:T(8,128)S(1)}, f32[4,6,16,512]{3,2,1,0:T(8,128)S(1)}, f32[4,5,16,512]{3,2,1,0:T(8,128)S(1)}, f32[4,24,512]{2,1,0:T...) custom-call(f32[4,8,16,512]{3,2,1,0:T(8,128)S(1)} %get-tuple-element.60.s_ref, ...), custom_call_target="tpu_custom_call" | custom-call | tf_op jit(solution)/shard_map/inner_operators/pallas_call | solution.py:302
  23.8 1.0 %outer_operators.1 = (f32[4,2,16,512]{3,2,1,0:T(8,128)S(1)}, f32[4,2,16,512]{3,2,1,0:T(8,128)S(1)}, f32[4,3,16,512]{3,2,1,0:T(8,128)S(1)}, f32[256,128]{1,0:T(8,128)S(1)}) custom-call(f32[15,16,512]{2,1,0:T(8,128)S(1)} %collective-permute-done.before, f32[40,512]{1,0:T(8,128)S(1)} %collective-permute-done.1.above, ...), custom_call_target="tpu_custom_call" | custom-call | tf_op jit(solution)/shard_map/outer_operators/pallas_call | solution.py:425
  24.9 0.0 copy-start
  24.9 24.1 %all_to_all.21 = f32[256,1,128]{2,1,0:T(1,128)S(1)} all-to-all(f32[256,1,128]{2,1,0:T(1,128)S(1)} %bitcast.10), channel_id=1, replica_groups=mesh['tm'=32,'slab'=8] {'tm','slab'}, dimensions={0} | all-to-all | bytes 262144 | tf_op jit(solution)/shard_map/all_to_all | solution.py:628
  49.0 1.3 %force.1 = (f32[7,16,512]{2,1,0:T(8,128)S(1)}, f32[16,512]{1,0:T(8,128)S(1)}, f32[32,16,128]{2,1,0:T(8,128)}) custom-call(f32[256,128]{1,0:T(8,128)S(1)} %bitcast.9, f32[4,8,16,512]{3,2,1,0:T(8,128)S(1)} %get-tuple-element.60.s_ref, f32[4,6,16,512]{3,2,1,0:T(8,128)S(1)} %get-tuple-element.107.p_in, f32[4,6,16,512]{3,2,1,0:T(8,128)S(1)} %get-tuple-element.101.q_inner.q_in, ...), custom_call_target="tpu_custom_call" | custom-call | tf_op jit(solution)/shard_map/force/pallas_call | solution.py:495
  50.3 4.6 %all-to-all-start.1 = ((f32[32,16,128]{2,1,0:T(8,128)}), f32[32,16,128]{2,1,0:T(8,128)S(1)}, u32[]{:S(2)}, u32[]{:S(2)}) async-start(f32[32,16,128]{2,1,0:T(8,128)} %get-tuple-element.112), calls=%async_computation.1 | async-start | bytes 524288 | tf_op jit(solution)/shard_map/all_to_all | solution.py:630
  54.8 0.4 collective-permute-start.5
  55.3 8.3 %collective-permute-done.5.late_ref = f32[16,512]{1,0:T(8,128)S(1)} collective-permute-done((f32[16,512]{1,0:T(8,128)S(1)}, f32[16,512]{1,0:T(8,128)S(1)}, u32[]{:S(2)}, u32[]{:S(2)}) %collective-permute-start.5) | collective-permute-done | bytes 32800 | tf_op jit(solution)/shard_map/ppermute | solution.py:600
  63.5 0.7 join_times.1
  64.3 4.1 %all-to-all-done.1 = f32[32,16,128]{2,1,0:T(8,128)S(1)} async-done(((f32[32,16,128]{2,1,0:T(8,128)}), f32[32,16,128]{2,1,0:T(8,128)S(1)}, u32[]{:S(2)}, u32[]{:S(2)}) %all-to-all-start.1) | async-done | bytes 262176 | tf_op jit(solution)/shard_map/all_to_all | solution.py:630
  68.4 0.4 drift.1
  68.8 17.7 %all_to_all.22.back_ref = f32[32,16,128]{2,1,0:T(8,128)S(1)} all-to-all(f32[32,16,128]{2,1,0:T(8,128)S(1)} %bitcast.8), channel_id=1, replica_groups=mesh['tm'=32,'slab'=8] {'tm'}, dimensions={0} | all-to-all | bytes 524288 | tf_op jit(solution)/shard_map/all_to_all | solution.py:634
  86.4 0.9 add_drift.1
  (8 shorter events, 0.1 us)
Async XLA Ops:
  2.0 17.8 %collective-permute-start.3 = (f32[104,512]{1,0:T(8,128)S(1)}, f32[104,512]{1,0:T(8,128)S(1)}, u32[]{:S(2)}, u32[]{:S(2)}) collective-permute-start(f32[104,512]{1,0:T(8,128)S(1)} %get-tuple-element.73), channel_id=1, source_target_pairs={{7,0},{0,1},{1,2},{2,3},{3,4},{4,5},{5,6},{6,7},{15,8},{8,9},{9,10... | collective-permute-start | bytes 638984 | tf_op jit(solution)/shard_map/ppermute | solution.py:600
  4.2 17.1 %collective-permute-start.4 = (f32[104,512]{1,0:T(8,128)S(1)}, f32[104,512]{1,0:T(8,128)S(1)}, u32[]{:S(2)}, u32[]{:S(2)}) collective-permute-start(f32[104,512]{1,0:T(8,128)S(1)} %get-tuple-element.74), channel_id=1, source_target_pairs={{1,0},{2,1},{3,2},{4,3},{5,4},{6,5},{7,6},{0,7},{9,8},{10,9},{11,1... | collective-permute-start | bytes 638984 | tf_op jit(solution)/shard_map/ppermute | solution.py:600
  6.5 11.9 %collective-permute-start = (f32[15,16,512]{2,1,0:T(8,128)S(1)}, f32[15,16,512]{2,1,0:T(8,128)S(1)}, u32[]{:S(2)}, u32[]{:S(2)}) collective-permute-start(f32[15,16,512]{2,1,0:T(8,128)S(1)} %pack_ahead.1.ahead), channel_id=1, source_target_pairs={{248,0},{0,8},{8,16},{16,24},{24,32},{32,40},{40,48},{48,56},{56,6... | collective-permute-start | bytes 1474568 | tf_op jit(solution)/shard_map/ppermute | solution.py:600
  12.9 10.9 %collective-permute-start.1 = (f32[40,512]{1,0:T(8,128)S(1)}, f32[40,512]{1,0:T(8,128)S(1)}, u32[]{:S(2)}, u32[]{:S(2)}) collective-permute-start(f32[40,512]{1,0:T(8,128)S(1)} %get-tuple-element.71), channel_id=1, source_target_pairs={{255,0},{248,1},{249,2},{250,3},{251,4},{252,5},{253,6},{254,7},{7... | collective-permute-start | bytes 245768 | tf_op jit(solution)/shard_map/ppermute | solution.py:608
  13.0 5.2 %copy-start.1 = (f32[256]{0:T(256)S(1)}, f32[256]{0:T(256)}, u32[]{:S(2)}) copy-start(f32[256]{0:T(256)} %param.8) | copy-start | bytes 3076
  13.0 10.8 %collective-permute-start.2 = (f32[40,512]{1,0:T(8,128)S(1)}, f32[40,512]{1,0:T(8,128)S(1)}, u32[]{:S(2)}, u32[]{:S(2)}) collective-permute-start(f32[40,512]{1,0:T(8,128)S(1)} %get-tuple-element.72), channel_id=1, source_target_pairs={{249,0},{250,1},{251,2},{252,3},{253,4},{254,5},{255,6},{248,7},{1... | collective-permute-start | bytes 245768 | tf_op jit(solution)/shard_map/ppermute | solution.py:608
  24.9 24.1 %copy-start = (f32[8,16,512]{2,1,0:T(8,128)S(1)}, f32[8,16,512]{2,1,0:T(8,128)}, u32[]{:S(2)}) copy-start(f32[8,16,512]{2,1,0:T(8,128)} %pi_ref.1) | copy-start | bytes 786436
  50.3 18.1 %all-to-all-start.1 = ((f32[32,16,128]{2,1,0:T(8,128)}), f32[32,16,128]{2,1,0:T(8,128)S(1)}, u32[]{:S(2)}, u32[]{:S(2)}) async-start(f32[32,16,128]{2,1,0:T(8,128)} %get-tuple-element.112), calls=%async_computation.1 | async-start | bytes 524288 | tf_op jit(solution)/shard_map/all_to_all | solution.py:630
  54.8 8.7 %collective-permute-start.5 = (f32[16,512]{1,0:T(8,128)S(1)}, f32[16,512]{1,0:T(8,128)S(1)}, u32[]{:S(2)}, u32[]{:S(2)}) collective-permute-start(f32[16,512]{1,0:T(8,128)S(1)} %get-tuple-element.114), channel_id=1, source_target_pairs={{8,0},{16,8},{24,16},{32,24},{40,32},{48,40},{56,48},{64,56},{72,6... | collective-permute-start | bytes 98312 | tf_op jit(solution)/shard_map/ppermute | solution.py:600
